TPU v7x, 32 devices: a whole 2x2x4 slice. The times are simulated.
32 devices in a mesh: tile: 8 (over z, core), dp: 4 (over y, x).
Axes of the slice: x: 2, y: 2, z: 4, core: 2. Of those that a mesh axis runs over, the one named last changes fastest.
Arguments:
- face_tokens: bfloat16 [4, 48, 64, 1024], P('dp', 'tile'), may hold values from -6 to 6
- edge_tokens: bfloat16 [4, 64, 48, 1024], P('dp', 'tile'), may hold values from -6 to 6
- face_cotangent: bfloat16 [4, 48, 64, 1024], P('dp', 'tile'), may hold values from -6 to 6
- edge_cotangent: bfloat16 [4, 64, 48, 1024], P('dp', 'tile'), may hold values from -6 to 6
- rotation: int32 [48], replicated, may hold values from 0 to 3
- counts: int32 [48], replicated, may hold values from 1 to 64, 2304 in all
- norm_gain: float32 [1024], replicated, may hold values from 0.5 to 1.5
- qkv_weight: bfloat16 [1024, 3072], replicated, may hold values from -1 to 1, as said below
- out_weight: bfloat16 [1024, 1024], replicated, may hold values from -0.1875 to 0.1875
Outputs:
- face_output: bfloat16 [4, 48, 64, 1024], P('dp', 'tile')
- edge_output: bfloat16 [4, 64, 48, 1024], P('dp', 'tile')
- face_grad: bfloat16 [4, 48, 64, 1024], P('dp', 'tile')
- edge_grad: bfloat16 [4, 64, 48, 1024], P('dp', 'tile')
- qkv_grad: float32 [1024, 3072], P('tile')
- out_grad: float32 [1024, 1024], P('tile')
- gain_grad: float32 [1024], P('tile')
Inputs may be any that keep to these rules, and one draw needn't show every extreme that they name: `counts`: the largest count is 64. `qkv_weight`: entries drawn independently.
All inputs are finite; a program needn't handle non-finite values.
Results may differ from a plain program's by a relative error of at most 0.007.
The roundings to bfloat16 on the way count: a program that leaves them out, or rounds other values in their place, can miss the bound.
Values may be sent and summed in bfloat16 or wider, within the bound.
No kernel may reach another device: no remote copies, remote signals or barrier semaphores. Data moves between devices by JAX's collectives and lax.ppermute only.
A program may use at most 128 MiB of HBM per device.

v0:
```python
import functools

import jax
import jax.numpy as jnp
import numpy as np
from jax import lax
from jax.experimental import pallas as pl
from jax.experimental.pallas import tpu as pltpu
from jax.sharding import PartitionSpec as P

HEADS = 16
BF = jnp.bfloat16
F32 = jnp.float32
VMEM_BYTES = 48 * 1024 * 1024


def nn(a, b):
    return lax.dot_general(a, b, (((1,), (0,)), ((), ())), preferred_element_type=F32)


def nt(a, b):
    return lax.dot_general(a, b, (((1,), (1,)), ((), ())), preferred_element_type=F32)


def tn(a, b):
    return lax.dot_general(a, b, (((0,), (0,)), ((), ())), preferred_element_type=F32)


def one_hot(index_ref, width):
    rows = index_ref.shape[0]
    columns = lax.broadcasted_iota(jnp.int32, (rows, width), 1)
    return jnp.where(columns == index_ref[...], 1.0, 0.0).astype(BF)


def pack_kernel(tok_ref, cot_ref, index_ref, *refs):
    both = refs[-1]
    rows = tok_ref.shape[0]
    both[:rows] = tok_ref[...]
    both[rows:] = cot_ref[...]
    take = index_ref.shape[0] // (len(refs) - 1)
    for c, out in enumerate(refs[:-1]):
        columns = lax.broadcasted_iota(jnp.int32, (take, 2 * rows), 1)
        picked = jnp.where(columns == index_ref[c * take : (c + 1) * take], 1.0, 0.0).astype(BF)
        out[...] = nn(picked, both[...]).astype(BF)


def unpack_kernel(chunks, *refs):
    backs, index_ref, out_tok, out_cot, both = refs[:chunks], refs[chunks], refs[-3], refs[-2], refs[-1]
    take = backs[0].shape[0]
    for c, back in enumerate(backs):
        both[c * take : (c + 1) * take] = back[...]
    rows = out_tok.shape[0]
    for w, out in enumerate((out_tok, out_cot)):
        columns = lax.broadcasted_iota(jnp.int32, (rows, chunks * take), 1)
        picked = jnp.where(columns == index_ref[w * rows : (w + 1) * rows], 1.0, 0.0).astype(BF)
        out[...] = nn(picked, both[...]).astype(BF)


def layer_kernel(
    lines,
    length,
    aliased,
    scal_ref,
    face_ref,
    fcot_ref,
    arrived_ref,
    index_ref,
    back_index_ref,
    turn_ref,
    gain_ref,
    wqkv_ref,
    wo_ref,
    *refs,
):
    refs = refs[2:] if aliased else refs
    (
        face_out,
        face_grad,
        back_ref,
        normed,
        keep_a,
        send_a,
        lhs_keep,
        rhs_keep,
        lhs_send,
        rhs_send,
        gain_part,
        z_s,
        g_s,
        qkv_s,
        dm_s,
        mix_s,
        stk_s,
        dn_s,
        y_s,
        inv_s,
        edge_s,
    ) = refs
    width = z_s.shape[1]
    half = width // 2
    face_len = face_ref.shape[2]
    edge_len = length - face_len
    edges = lines * edge_len
    rows_all = lines * length
    head_dim = width // HEADS
    scale = head_dim ** (-0.5)

    picked = one_hot(index_ref, arrived_ref.shape[0])
    first = nn(picked, arrived_ref[:, :half])
    second = nn(picked, arrived_ref[:, half:])
    cosine = turn_ref[:, 0:1]
    sine = turn_ref[:, 1:2]
    turned_first = (cosine * first - sine * second).astype(BF)
    turned_second = (sine * first + cosine * second).astype(BF)
    for l in range(lines):
        at = l * length
        z_s[at : at + face_len] = face_ref[0, l]
        g_s[at : at + face_len] = fcot_ref[0, l]
        for w, dst in enumerate((z_s, g_s)):
            src = w * edges + l * edge_len
            dst[at + face_len : at + length, :half] = turned_first[src : src + edge_len]
            dst[at + face_len : at + length, half:] = turned_second[src : src + edge_len]
    gain = gain_ref[...]
    for l in range(lines):
        at = slice(l * length, (l + 1) * length)
        hidden = z_s[at].astype(F32)
        inverse = lax.rsqrt(jnp.mean(hidden * hidden, axis=-1, keepdims=True) + 1e-06)
        inv_s[at] = inverse
        normed[at] = (hidden * inverse * gain).astype(BF)

    tile = 512

    @pl.loop(0, 3 * width // tile)
    def _(j):
        cols = pl.ds(pl.multiple_of(j * tile, tile), tile)
        qkv_s[:, cols] = nn(normed[...], wqkv_ref[:, cols]).astype(BF)

    @pl.loop(0, width // tile)
    def _(j):
        cols = pl.ds(pl.multiple_of(j * tile, tile), tile)
        dm_s[:, cols] = nt(g_s[...], wo_ref[cols, :]).astype(BF)

    pair = 2 * head_dim
    low = lax.broadcasted_iota(jnp.int32, (length, pair), 1) < head_dim
    key_row = lax.broadcasted_iota(jnp.int32, (length, length), 0)

    def split(x):
        zero = jnp.zeros_like(x)
        return jnp.concatenate([jnp.where(low, x, zero), jnp.where(low, zero, x)], axis=0)

    @pl.loop(0, lines)
    def _(l):
        rows = pl.ds(pl.multiple_of(l * length, length), length)
        live = key_row < scal_ref[l] + face_len
        for p in range(HEADS // 2):
            at = p * pair
            q = qkv_s[rows, at : at + pair]
            k2 = split(qkv_s[rows, width + at : width + at + pair])
            v2 = split(qkv_s[rows, 2 * width + at : 2 * width + at + pair])
            dm = dm_s[rows, at : at + pair]
            scores = nt(k2, q) * scale
            d_probs = nt(v2, dm)
            probs_b, d_scores = [], []
            for h in range(2):
                part = slice(h * length, (h + 1) * length)
                s = jnp.where(live, scores[part], -1e30)
                e = jnp.exp(s - jnp.max(s, axis=0, keepdims=True))
                probs = e / jnp.sum(e, axis=0, keepdims=True)
                d = d_probs[part]
                inner = jnp.sum(probs * d, axis=0, keepdims=True)
                probs_b.append(probs.astype(BF))
                d_scores.append((probs * (d - inner) * scale).astype(BF))
            pb = jnp.concatenate(probs_b, axis=0)
            ds = jnp.concatenate(d_scores, axis=0)
            mix_s[rows, at : at + pair] = tn(pb, v2).astype(BF)
            dv = nn(pb, dm)
            stk_s[rows, 2 * width + at : 2 * width + at + pair] = jnp.where(
                low, dv[:length], dv[length:]
            ).astype(BF)
            stk_s[rows, at : at + pair] = tn(ds, k2).astype(BF)
            dk = nn(ds, q)
            stk_s[rows, width + at : width + at + pair] = jnp.where(
                low, dk[:length], dk[length:]
            ).astype(BF)

    @pl.loop(0, width // tile)
    def _(j):
        cols = pl.ds(pl.multiple_of(j * tile, tile), tile)
        y_s[:, cols] = (nn(mix_s[...], wo_ref[:, cols]) + z_s[:, cols].astype(F32)).astype(BF)
        dn_s[:, cols] = nt(stk_s[...], wqkv_ref[cols, :])

    gain_sum = jnp.zeros((1, width), F32)
    for l in range(lines):
        at = slice(l * length, (l + 1) * length)
        hidden = z_s[at].astype(F32)
        inverse = inv_s[at]
        d_normed = dn_s[at]
        gain_sum = gain_sum + jnp.sum(d_normed * hidden * inverse, axis=0, keepdims=True)
        scaled = d_normed * gain
        mean = jnp.mean(scaled * hidden, axis=-1, keepdims=True)
        dz = inverse * scaled - hidden * (inverse * inverse * inverse * mean)
        dz = (g_s[at].astype(F32) + dz).astype(BF)
        face_out[0, l] = y_s[l * length : l * length + face_len]
        face_grad[0, l] = dz[:face_len]
        edge_s[l * edge_len : (l + 1) * edge_len] = y_s[l * length + face_len : (l + 1) * length]
        edge_s[edges + l * edge_len : edges + (l + 1) * edge_len] = dz[face_len:]
    gain_part[...] = jnp.broadcast_to(gain_sum, gain_part.shape)
    first = edge_s[:, :half].astype(F32)
    second = edge_s[:, half:].astype(F32)
    turned_first = (cosine * first + sine * second).astype(BF)
    turned_second = (cosine * second - sine * first).astype(BF)
    picked = one_hot(back_index_ref, 2 * edges)
    back_ref[:, :half] = nn(picked, turned_first).astype(BF)
    back_ref[:, half:] = nn(picked, turned_second).astype(BF)

    x_bit = scal_ref[lines]
    y_bit = scal_ref[lines + 1]

    @pl.when(x_bit == 0)
    def _():
        keep_a[...] = stk_s[:, :width]
        send_a[...] = stk_s[:, width : 2 * width]

    @pl.when(x_bit != 0)
    def _():
        send_a[...] = stk_s[:, :width]
        keep_a[...] = stk_s[:, width : 2 * width]

    @pl.when(y_bit == 0)
    def _():
        lhs_keep[...] = normed[...]
        rhs_keep[...] = stk_s[:, 2 * width :]
        lhs_send[...] = mix_s[...]
        rhs_send[...] = g_s[...]

    @pl.when(y_bit != 0)
    def _():
        lhs_send[...] = normed[...]
        rhs_send[...] = stk_s[:, 2 * width :]
        lhs_keep[...] = mix_s[...]
        rhs_keep[...] = g_s[...]


def weight_kernel(chunks, blocks, added, par_ref, *refs):
    lhs = refs[:chunks]
    rhs = refs[chunks : 2 * chunks]
    add_ref = refs[2 * chunks] if added else None
    out_ref, lhs_t = refs[-2], refs[-1]
    rows = lhs[0].shape[0]
    size = lhs[0].shape[1] // (2 * blocks)

    @pl.when(pl.program_id(0) == 0)
    def _():
        even = par_ref[0] == 0
        for c in range(chunks):
            for b in range(blocks):
                left = lhs[c][:, 2 * b * size : (2 * b + 1) * size]
                right = lhs[c][:, (2 * b + 1) * size : (2 * b + 2) * size]
                kept = jnp.where(even, left, right)
                lhs_t[b * size : (b + 1) * size, c * rows : (c + 1) * rows] = kept.T

    total = nn(lhs_t[:, :rows], rhs[0][...])
    for c in range(1, chunks):
        total = total + nn(lhs_t[:, c * rows : (c + 1) * rows], rhs[c][...])
    if added:
        total = total + add_ref[...]
    out_ref[...] = total


def weight_part(parity, lhs, rhs, blocks, add=None):
    chunks = len(lhs)
    rows, depth = lhs[0].shape
    width = rhs[0].shape[1]
    tile = 256
    whole = pl.BlockSpec((rows, depth), lambda j, s: (0, 0))
    piece = pl.BlockSpec((rows, tile), lambda j, s: (0, j))
    result = pl.BlockSpec((depth // 2, tile), lambda j, s: (0, j))
    operands = [*lhs, *rhs] + ([add] if add is not None else [])
    return pl.pallas_call(
        functools.partial(weight_kernel, chunks, blocks, add is not None),
        grid_spec=pltpu.PrefetchScalarGridSpec(
            num_scalar_prefetch=1,
            grid=(width // tile,),
            in_specs=[whole] * chunks + [piece] * chunks + ([result] if add is not None else []),
            out_specs=result,
            scratch_shapes=[pltpu.VMEM((depth // 2, chunks * rows), BF)],
        ),
        out_shape=jax.ShapeDtypeStruct((depth // 2, width), F32),
        compiler_params=pltpu.CompilerParams(vmem_limit_bytes=VMEM_BYTES),
        cost_estimate=pl.CostEstimate(
            flops=chunks * rows * depth * width, bytes_accessed=8 * depth * width, transcendentals=0
        ),
        name="weight_part",
    )(parity, *operands)


def exchange(x, axis, bits, size):
    return lax.ppermute(x, axis, [(i, i ^ bits) for i in range(size)])


def local(
    face_tokens,
    edge_tokens,
    face_cotangent,
    edge_cotangent,
    rotation,
    counts,
    norm_gain,
    qkv_weight,
    out_weight,
):
    T = lax.axis_size("tile")
    D = lax.axis_size("dp")
    me_t = lax.axis_index("tile")
    me_d = lax.axis_index("dp")
    LD, FL, width = face_tokens.shape[1:]
    K = edge_tokens.shape[1]
    EL = K * T
    NLG = edge_tokens.shape[2]
    length = FL + EL
    chunks = 2
    lines = LD // chunks
    RB = lines * K
    packed = T * 2 * RB
    factor = float(D * T * LD * length) ** (-0.5)

    def vmem_call(kernel, out_shape, scratch, *operands):
        return pl.pallas_call(
            kernel,
            out_shape=out_shape,
            in_specs=[pl.BlockSpec(memory_space=pltpu.VMEM)] * len(operands),
            scratch_shapes=scratch,
            compiler_params=pltpu.CompilerParams(vmem_limit_bytes=VMEM_BYTES),
            name="rows_kernel",
        )(*operands)

    order = np.zeros((chunks, T, 2, lines, K), np.int32)
    for c in range(chunks):
        for w in range(2):
            t, l, k = np.meshgrid(np.arange(T), np.arange(lines), np.arange(K), indexing="ij")
            order[c, :, w] = w * K * NLG + k * NLG + t * LD + c * lines + l
    sent = vmem_call(
        pack_kernel,
        [jax.ShapeDtypeStruct((packed, width), BF)] * chunks,
        [pltpu.VMEM((2 * K * NLG, width), BF)],
        edge_tokens.reshape(K * NLG, width),
        edge_cotangent.reshape(K * NLG, width),
        jnp.asarray(order.reshape(-1, 1)),
    )
    arrived = [lax.all_to_all(s, "tile", split_axis=0, concat_axis=0, tiled=True) for s in sent]

    my_turns = lax.dynamic_slice_in_dim(rotation, me_t * LD, LD)
    my_counts = lax.dynamic_slice_in_dim(counts, me_t * LD, LD)
    x_bit = (me_d % 2).astype(jnp.int32)
    y_bit = ((me_d // 2) % 2).astype(jnp.int32)

    spos = np.arange(EL)
    results = []
    faces = None
    for c in range(chunks):
        turns = my_turns[c * lines : (c + 1) * lines]
        flip = turns >= 2
        pos = jnp.where(flip[:, None], EL - 1 - spos[None, :], spos[None, :])
        row = (pos // K) * (2 * RB) + jnp.arange(lines)[:, None] * K + pos % K
        index = jnp.concatenate([row, row + RB], axis=0).reshape(-1, 1).astype(jnp.int32)
        cosine = (turns == 0).astype(F32) - (turns == 2).astype(F32)
        sine = (turns == 1).astype(F32) - (turns == 3).astype(F32)
        turn = jnp.stack([cosine, sine], axis=-1)
        turn = jnp.broadcast_to(turn[None, :, None, :], (2, lines, EL, 2)).reshape(-1, 2)
        sk = np.arange(T)[:, None, None, None] * K + np.arange(K)[None, None, None, :]
        bk = jnp.where(flip[None, None, :, None], EL - 1 - sk, sk)
        back_index = (
            jnp.arange(2)[None, :, None, None] * (lines * EL)
            + jnp.arange(lines)[None, None, :, None] * EL
            + bk
        )
        back_index = back_index.reshape(-1, 1).astype(jnp.int32)
        scal = jnp.concatenate(
            [my_counts[c * lines : (c + 1) * lines], jnp.stack([x_bit, y_bit])]
        )
        rows_all = lines * length
        face_spec = pl.BlockSpec((1, lines, FL, width), lambda i, s, c=c: (0, c, 0, 0))

        def full(shape):
            return pl.BlockSpec(shape, lambda i, s: (0,) * len(shape))

        row_shape = (rows_all, width)
        operands = [
            face_tokens,
            face_cotangent,
            arrived[c],
            index,
            back_index,
            turn,
            norm_gain.reshape(1, width),
            qkv_weight,
            out_weight,
        ]
        in_specs = [face_spec, face_spec] + [full(o.shape) for o in operands[2:]]
        if faces is not None:
            in_specs += [pl.BlockSpec(memory_space=pl.ANY)] * 2
            operands += list(faces)
        outs = pl.pallas_call(
            functools.partial(layer_kernel, lines, length, faces is not None),
            grid_spec=pltpu.PrefetchScalarGridSpec(
                num_scalar_prefetch=1,
                grid=(1,),
                in_specs=in_specs,
                out_specs=[face_spec, face_spec, full((packed, width))]
                + [full(row_shape)] * 7
                + [full((8, width))],
                scratch_shapes=[
                    pltpu.VMEM(row_shape, BF),
                    pltpu.VMEM(row_shape, BF),
                    pltpu.VMEM((rows_all, 3 * width), BF),
                    pltpu.VMEM(row_shape, BF),
                    pltpu.VMEM(row_shape, BF),
                    pltpu.VMEM((rows_all, 3 * width), BF),
                    pltpu.VMEM(row_shape, F32),
                    pltpu.VMEM(row_shape, BF),
                    pltpu.VMEM((rows_all, 1), F32),
                    pltpu.VMEM((2 * lines * EL, width), BF),
                ],
            ),
            out_shape=[
                jax.ShapeDtypeStruct(face_tokens.shape, BF),
                jax.ShapeDtypeStruct(face_tokens.shape, BF),
                jax.ShapeDtypeStruct((packed, width), BF),
            ]
            + [jax.ShapeDtypeStruct(row_shape, BF)] * 7
            + [jax.ShapeDtypeStruct((8, width), F32)],
            input_output_aliases={10: 0, 11: 1} if faces is not None else {},
            compiler_params=pltpu.CompilerParams(vmem_limit_bytes=VMEM_BYTES),
            cost_estimate=pl.CostEstimate(
                flops=2 * rows_all * width * width * 8 * 2, bytes_accessed=1 << 24, transcendentals=0
            ),
            name="layer",
        )(scal, *operands)
        faces = outs[:2]
        results.append(outs[2:])
    returned = [
        lax.all_to_all(r[0], "tile", split_axis=0, concat_axis=0, tiled=True) for r in results
    ]
    back_order = np.zeros((2, K, NLG), np.int32)
    for w in range(2):
        k, t, c, l = np.meshgrid(
            np.arange(K), np.arange(T), np.arange(chunks), np.arange(lines), indexing="ij"
        )
        back_order[w] = (c * packed + t * 2 * RB + w * RB + l * K + k).reshape(K, NLG)
    edge_output, edge_grad = vmem_call(
        functools.partial(unpack_kernel, chunks),
        [jax.ShapeDtypeStruct((K * NLG, width), BF)] * 2,
        [pltpu.VMEM((chunks * packed, width), BF)],
        *returned,
        jnp.asarray(back_order.reshape(-1, 1)),
    )

    blocks = T // 2
    chip = me_t // 2
    core = me_t % 2
    own = core.astype(jnp.int32).reshape(1)
    other = 1 - own
    column = list(zip(*results))
    _, normed, keep_a, send_a, lhs_keep, rhs_keep, lhs_send, rhs_send, gain_part = column

    def core_sum(lhs, rhs):
        theirs = exchange(weight_part(other, lhs, rhs, blocks), "tile", 1, T)
        return weight_part(own, lhs, rhs, blocks, theirs)

    sum_send_a = exchange(core_sum(normed, send_a), "dp", 1, D)
    sum_send_b = exchange(core_sum(lhs_send, rhs_send), "dp", 2, D)
    sum_a = core_sum(normed, keep_a)
    sum_b = core_sum(lhs_keep, rhs_keep)

    def halve(first, second, bits):
        parts = [first, second]
        for bit in bits:
            columns = parts[0].shape[-1] // 2
            mine = (me_d >> bit) & 1
            keep = [lax.dynamic_slice_in_dim(p, mine * columns, columns, 1) for p in parts]
            send = [lax.dynamic_slice_in_dim(p, (1 - mine) * columns, columns, 1) for p in parts]
            parts = [sum(keep), exchange(sum(send), "dp", 1 << bit, D)]
        return parts

    bits = D.bit_length() - 1
    rest_a = [b for b in range(bits) if b != 0]
    rest_b = [b for b in range(bits) if b != 1]
    half_a = halve(sum_a, sum_send_a, rest_a)
    half_b = halve(sum_b, sum_send_b, rest_b)
    size = width // T

    def block(parts, which):
        return sum(lax.dynamic_slice_in_dim(p, which * size, size, 0) for p in parts)

    mine_a, mine_b = block(half_a, chip), block(half_b, chip)
    for o in range(1, blocks):
        got_a = exchange(block(half_a, chip ^ o), "tile", 2 * o, T)
        got_b = exchange(block(half_b, chip ^ o), "tile", 2 * o, T)
        mine_a, mine_b = mine_a + got_a, mine_b + got_b
    mine = jnp.concatenate([mine_a, mine_b], axis=1) * factor
    pieces = [mine] + [exchange(mine, "dp", o, D) for o in range(1, D)]
    stacked = jnp.stack(pieces)
    piece = mine_a.shape[1]

    def place(bit, fixed, offset):
        rest = [b for b in range(bits) if b != fixed]
        columns = []
        for n in range(D // 2):
            device = bit << fixed
            for i, b in enumerate(rest):
                device |= ((n >> (len(rest) - 1 - i)) & 1) << b
            got = lax.dynamic_index_in_dim(stacked, me_d ^ device, 0, keepdims=False)
            columns.append(got[:, offset : offset + piece])
        return columns

    qkv_grad = jnp.concatenate(
        place(0, 0, 0) + place(1, 0, 0) + place(0, 1, piece), axis=1
    )
    out_grad = jnp.concatenate(place(1, 1, piece), axis=1)

    gain_sum = sum(g[0:1] for g in gain_part)
    for b in range(bits):
        gain_sum = gain_sum + exchange(gain_sum, "dp", 1 << b, D)
    for b in range(T.bit_length() - 1):
        gain_sum = gain_sum + exchange(gain_sum, "tile", 1 << b, T)
    gain_grad = lax.dynamic_slice_in_dim(gain_sum[0], me_t * size, size) * factor
    shape = edge_tokens.shape
    return (
        faces[0],
        edge_output.reshape(shape),
        faces[1],
        edge_grad.reshape(shape),
        qkv_grad,
        out_grad,
        gain_grad,
    )


def solution(mesh):
    return jax.shard_map(
        local,
        mesh=mesh,
        in_specs=(
            P("dp", "tile", None, None),
            P("dp", "tile", None, None),
            P("dp", "tile", None, None),
            P("dp", "tile", None, None),
            P(),
            P(),
            P(),
            P(),
            P(),
        ),
        out_specs=(
            P("dp", "tile", None, None),
            P("dp", "tile", None, None),
            P("dp", "tile", None, None),
            P("dp", "tile", None, None),
            P("tile", None),
            P("tile", None),
            P("tile"),
        ),
        check_vma=False,
    )
```

profile of v0, /device:TPU:16, one launch (start us, length us, event | category | flops | bytes accessed | tf_op | source)
XLA Modules:
  0.0 287.4 jit_solution(13570832824193582018)
XLA Ops:
  6.4 5.3 %all-to-all-start.1 = ((bf16[8,48,1024]{2,1,0:T(8,128)(2,1)}), bf16[8,48,1024]{2,1,0:T(8,128)(2,1)S(1)}, u32[]{:S(2)}, u32[]{:S(2)}) async-start(bf16[8,48,1024]{2,1,0:T(8,128)(2,1)} %bitcast.10), calls=%async_computation.1 | async-start | bytes 1572864 | tf_op jit(solution)/shard_map/all_to_all | solution.py:350
  13.3 16.1 %all-to-all-done.1 = bf16[8,48,1024]{2,1,0:T(8,128)(2,1)S(1)} async-done(((bf16[8,48,1024]{2,1,0:T(8,128)(2,1)}), bf16[8,48,1024]{2,1,0:T(8,128)(2,1)S(1)}, u32[]{:S(2)}, u32[]{:S(2)}) %all-to-all-start.1) | async-done | bytes 786464 | tf_op jit(solution)/shard_map/all_to_all | solution.py:350
  29.4 7.4 %all-to-all-start = ((bf16[8,48,1024]{2,1,0:T(8,128)(2,1)}), bf16[8,48,1024]{2,1,0:T(8,128)(2,1)}, u32[]{:S(2)}, u32[]{:S(2)}) async-start(bf16[8,48,1024]{2,1,0:T(8,128)(2,1)} %bitcast.4), calls=%async_computation | async-start | bytes 1572864 | tf_op jit(solution)/shard_map/all_to_all | solution.py:350
  37.0 25.1 %layer.2 = (bf16[1,6,64,1024]{3,2,1,0:T(8,128)(2,1)}, bf16[1,6,64,1024]{3,2,1,0:T(8,128)(2,1)}, bf16[384,1024]{1,0:T(8,128)(2,1)S(1)}, bf16[384,1024]{1,0:T(8,12...) custom-call(s32[5]{0:T(128)S(1)} %add_add_fusion.3.scal_ref, ...), custom_call_target="tpu_custom_call" | custom-call | flops 12884901888 | bytes 16777216 | tf_op jit(solution)/shard_map/layer/pallas_call | solution.py:403
  66.6 25.2 %layer.3 = (bf16[1,6,64,1024]{3,2,1,0:T(8,128)(2,1)}, bf16[1,6,64,1024]{3,2,1,0:T(8,128)(2,1)}, bf16[384,1024]{1,0:T(8,128)(2,1)}, bf16[384,1024]{1,0:T(8,128)(2...) custom-call(s32[5]{0:T(128)S(1)} %add_add_fusion.2.scal_ref, ...), custom_call_target="tpu_custom_call", output_to_operand_aliasing={{0}: (10, {}), {1}: (11, {})} | custom-call | flops 12884901888 | bytes 16777216 | tf_op jit(solution)/shard_map/layer/pallas_call | solution.py:403
  93.5 3.4 %weight_part.14 = f32[512,1024]{1,0:T(8,128)} custom-call(s32[1]{0:T(128)S(6)} %sub.47.par_ref, bf16[384,1024]{1,0:T(8,128)(2,1)S(1)} %copy-done.15, bf16[384,1024]{1,0:T(8,128)(2,1)S(1)} %get-tuple-element.54.refs_1_, bf16[384,1024]{1,0:T(8,128)(2,1)S(1)} %copy-done.16, bf16[384,1024]{1,0:T(8,128)(2,1)S(1)} %copy-done.17), custom_call_target="tpu_custom_call" | custom-call | flops 805306368 | bytes 8388608 | tf_op jit(solution)/shard_map/weight_part/pallas_call | solution.py:279
  100.0 3.5 %weight_part.12 = f32[512,1024]{1,0:T(8,128)} custom-call(s32[1]{0:T(128)S(6)} %sub.47.par_ref, bf16[384,1024]{1,0:T(8,128)(2,1)S(1)} %copy-done.3, bf16[384,1024]{1,0:T(8,128)(2,1)S(1)} %get-tuple-element.50.refs_1_, bf16[384,1024]{1,0:T(8,128)(2,1)S(1)} %copy-done.6, bf16[384,1024]{1,0:T(8,128)(2,1)S(1)} %get-tuple-element.52.refs_3_), custom_call_target="tpu_custom_call" | custom-call | flops 805306368 | bytes 8388608 | tf_op jit(solution)/shard_map/weight_part/pallas_call | solution.py:279
  103.6 5.0 %weight_part.15 = f32[512,1024]{1,0:T(8,128)} custom-call(s32[1]{0:T(128)} %bitcast.21.par_ref, bf16[384,1024]{1,0:T(8,128)(2,1)S(1)} %copy-done.15, bf16[384,1024]{1,0:T(8,128)(2,1)S(1)} %get-tuple-element.54.refs_1_, bf16[384,1024]{1,0:T(8,128)(2,1)S(1)} %copy-done.16, bf16[384,1024]{1,0:T(8,128)(2,1)S(1)} %copy-done.18, ...), custom_call_target="tpu_custom_call" | custom-call | flops 805306368 | bytes 8388608 | tf_op jit(solution)/shard_map/weight_part/pallas_call | solution.py:279
  110.2 3.4 %weight_part.8 = f32[512,1024]{1,0:T(8,128)} custom-call(s32[1]{0:T(128)S(6)} %sub.47.par_ref, bf16[384,1024]{1,0:T(8,128)(2,1)S(1)} %get-tuple-element.43.refs_0_, bf16[384,1024]{1,0:T(8,128)(2,1)S(1)} %get-tuple-element.44.refs_1_, bf16[384,1024]{1,0:T(8,128)(2,1)S(1)} %get-tuple-element.45.refs_2_, bf16[384,1024]{1,0:T(8,128)(2,1)S(1)} %get-tuple-element.46.refs_3_), custom_call_target="tpu_custom_call" | custom-call | flops 805306368 | bytes 8388608 | tf_op jit(solution)/shard_map/weight_part/pallas_call | solution.py:279
  113.7 5.1 %weight_part.11 = f32[512,1024]{1,0:T(8,128)} custom-call(s32[1]{0:T(128)} %bitcast.21.par_ref, bf16[384,1024]{1,0:T(8,128)(2,1)S(1)} %get-tuple-element.43.refs_0_, bf16[384,1024]{1,0:T(8,128)(2,1)S(1)} %get-tuple-element.44.refs_1_, bf16[384,1024]{1,0:T(8,128)(2,1)S(1)} %copy-done.13, bf16[384,1024]{1,0:T(8,128)(2,1)S(1)} %get-tuple-element.48.refs_3_, ...), custom_call_target="tpu_custom_call" | custom-call | flops 805306368 | bytes 8388608 | tf_op jit(solution)/shard_map/weight_part/pallas_call | solution.py:279
  120.3 5.3 %all-to-all-start.2 = ((bf16[8,48,1024]{2,1,0:T(8,128)(2,1)}), bf16[8,48,1024]{2,1,0:T(8,128)(2,1)S(1)}, u32[]{:S(2)}, u32[]{:S(2)}) async-start(bf16[8,48,1024]{2,1,0:T(8,128)(2,1)} %bitcast.43), calls=%async_computation.2 | async-start | bytes 1572864 | tf_op jit(solution)/shard_map/all_to_all | solution.py:442
  130.2 4.0 %weight_part.13 = f32[512,1024]{1,0:T(8,128)S(1)} custom-call(s32[1]{0:T(128)} %bitcast.21.par_ref, bf16[384,1024]{1,0:T(8,128)(2,1)S(1)} %copy-done.4, bf16[384,1024]{1,0:T(8,128)(2,1)S(1)} %copy-done.9, bf16[384,1024]{1,0:T(8,128)(2,1)S(1)} %copy-done.7, bf16[384,1024]{1,0:T(8,128)(2,1)S(1)} %copy-done.11, f32[512,1024]{1,0:T(8,128)} %collective-permute-done.7.refs_4_), custom_call_target="tpu_custom_call" | custom-call | flops 805306368 | bytes 8388608 | tf_op jit(solution)/shard_map/weight_part/pallas_call | solution.py:279
  134.1 22.8 %collective-permute-done.9 = f32[512,1024]{1,0:T(8,128)} collective-permute-done((f32[512,1024]{1,0:T(8,128)}, f32[512,1024]{1,0:T(8,128)}, u32[]{:S(2)}, u32[]{:S(2)}) %collective-permute-start.9) | collective-permute-done | bytes 2097184 | tf_op jit(solution)/shard_map/ppermute | solution.py:298
  156.9 3.4 %dynamic-slice_add_fusion.1 = (f32[512,512]{1,0:T(8,128)}, f32[512,512]{1,0:T(8,128)}) fusion(f32[512,1024]{1,0:T(8,128)} %collective-permute-done.9, s32[]{:T(128)S(6)} %select_n.148, f32[512,1024]{1,0:T(8,128)S(1)} %weight_part.13, s32[]{:T(128)S(6)} %select_n.149), kind=kLoop, calls=%fused_computation.2 | loop fusion | flops 524288 | bytes 6291464 | tf_op jit(solution)/shard_map/add | solution.py:482
  163.0 4.0 %weight_part.9 = f32[512,1024]{1,0:T(8,128)S(1)} custom-call(s32[1]{0:T(128)} %bitcast.21.par_ref, bf16[384,1024]{1,0:T(8,128)(2,1)S(1)} %get-tuple-element.43.refs_0_, bf16[384,1024]{1,0:T(8,128)(2,1)S(1)} %get-tuple-element.44.refs_1_, bf16[384,1024]{1,0:T(8,128)(2,1)S(1)} %get-tuple-element.45.refs_2_, bf16[384,1024]{1,0:T(8,128)(2,1)S(1)} %copy-done.1, ...), custom_call_target="tpu_custom_call" | custom-call | flops 805306368 | bytes 8388608 | tf_op jit(solution)/shard_map/weight_part/pallas_call | solution.py:279
  167.5 3.4 %dynamic-slice_add_fusion.3 = (f32[512,512]{1,0:T(8,128)}, f32[512,512]{1,0:T(8,128)}) fusion(f32[512,1024]{1,0:T(8,128)} %collective-permute-done.2, s32[]{:T(128)S(6)} %select_n.141, f32[512,1024]{1,0:T(8,128)S(1)} %weight_part.9, s32[]{:T(128)S(6)} %select_n.144), kind=kLoop, calls=%fused_computation.4 | loop fusion | flops 524288 | bytes 6291464 | tf_op jit(solution)/shard_map/add | solution.py:482
  171.9 5.1 %all-to-all-start.3 = ((bf16[8,48,1024]{2,1,0:T(8,128)(2,1)}), bf16[8,48,1024]{2,1,0:T(8,128)(2,1)S(1)}, u32[]{:S(2)}, u32[]{:S(2)}) async-start(bf16[8,48,1024]{2,1,0:T(8,128)(2,1)} %bitcast.17), calls=%async_computation.3 | async-start | bytes 1572864 | tf_op jit(solution)/shard_map/all_to_all | solution.py:442
  177.0 12.6 %collective-permute-done.10 = f32[512,512]{1,0:T(8,128)} collective-permute-done((f32[512,512]{1,0:T(8,128)}, f32[512,512]{1,0:T(8,128)}, u32[]{:S(2)}, u32[]{:S(2)}) %collective-permute-start.10) | collective-permute-done | bytes 1048608 | tf_op jit(solution)/shard_map/ppermute | solution.py:298
  198.0 3.7 %collective-permute-start.5 = (f32[128,512]{1,0:T(8,128)}, f32[128,512]{1,0:T(8,128)}, u32[]{:S(2)}, u32[]{:S(2)}) collective-permute-start(f32[128,512]{1,0:T(8,128)} %get-tuple-element.69), channel_id=1, source_target_pairs={{0,16},{4,20},{8,24},{12,28},{16,0},{20,4},{24,8},{28,12},{1,17},{... | collective-permute-start | bytes 786440 | tf_op jit(solution)/shard_map/ppermute | solution.py:298
  201.7 21.4 %collective-permute-done.13 = f32[128,512]{1,0:T(8,128)} collective-permute-done((f32[128,512]{1,0:T(8,128)S(1)}, f32[128,512]{1,0:T(8,128)}, u32[]{:S(2)}, u32[]{:S(2)}) %collective-permute-start.13) | collective-permute-done | bytes 262176 | tf_op jit(solution)/shard_map/ppermute | solution.py:298
  223.2 5.8 %collective-permute-done.12 = f32[128,512]{1,0:T(8,128)} collective-permute-done((f32[128,512]{1,0:T(8,128)}, f32[128,512]{1,0:T(8,128)}, u32[]{:S(2)}, u32[]{:S(2)}) %collective-permute-start.12) | collective-permute-done | bytes 262176 | tf_op jit(solution)/shard_map/ppermute | solution.py:298
  230.3 4.7 %collective-permute-done.6 = f32[128,512]{1,0:T(8,128)} collective-permute-done((f32[128,512]{1,0:T(8,128)}, f32[128,512]{1,0:T(8,128)}, u32[]{:S(2)}, u32[]{:S(2)}) %collective-permute-start.6) | collective-permute-done | bytes 262176 | tf_op jit(solution)/shard_map/ppermute | solution.py:298
  234.9 4.8 %collective-permute-done.5 = f32[128,512]{1,0:T(8,128)} collective-permute-done((f32[128,512]{1,0:T(8,128)}, f32[128,512]{1,0:T(8,128)}, u32[]{:S(2)}, u32[]{:S(2)}) %collective-permute-start.5) | collective-permute-done | bytes 262176 | tf_op jit(solution)/shard_map/ppermute | solution.py:298
  246.5 21.1 %collective-permute-done.17 = f32[1,1024]{1,0:T(1,128)S(1)} collective-permute-done((f32[1,1024]{1,0:T(1,128)S(1)}, f32[1,1024]{1,0:T(1,128)S(1)}, u32[]{:S(2)}, u32[]{:S(2)}) %collective-permute-start.17) | collective-permute-done | bytes 4128 | tf_op jit(solution)/shard_map/ppermute | solution.py:298
  (156 shorter events, 64.9 us)
Async XLA Ops:
  6.4 23.0 %all-to-all-start.1 = ((bf16[8,48,1024]{2,1,0:T(8,128)(2,1)}), bf16[8,48,1024]{2,1,0:T(8,128)(2,1)S(1)}, u32[]{:S(2)}, u32[]{:S(2)}) async-start(bf16[8,48,1024]{2,1,0:T(8,128)(2,1)} %bitcast.10), calls=%async_computation.1 | async-start | bytes 1572864 | tf_op jit(solution)/shard_map/all_to_all | solution.py:350
  29.4 37.2 %all-to-all-start = ((bf16[8,48,1024]{2,1,0:T(8,128)(2,1)}), bf16[8,48,1024]{2,1,0:T(8,128)(2,1)}, u32[]{:S(2)}, u32[]{:S(2)}) async-start(bf16[8,48,1024]{2,1,0:T(8,128)(2,1)} %bitcast.4), calls=%async_computation | async-start | bytes 1572864 | tf_op jit(solution)/shard_map/all_to_all | solution.py:350
  97.0 6.7 %collective-permute-start.8 = (f32[512,1024]{1,0:T(8,128)}, f32[512,1024]{1,0:T(8,128)}, u32[]{:S(2)}, u32[]{:S(2)}) collective-permute-start(f32[512,1024]{1,0:T(8,128)} %weight_part.14), channel_id=1, source_target_pairs={{0,4},{4,0},{8,12},{12,8},{16,20},{20,16},{24,28},{28,24},{1,5},{5... | collective-permute-start | bytes 6291464 | tf_op jit(solution)/shard_map/ppermute | solution.py:298
  99.5 14.2 %collective-permute-start.1 = (f32[512,1024]{1,0:T(8,128)S(1)}, f32[512,1024]{1,0:T(8,128)}, u32[]{:S(2)}, u32[]{:S(2)}) collective-permute-start(f32[512,1024]{1,0:T(8,128)S(1)} %weight_part.10), channel_id=1, source_target_pairs={{0,4},{4,0},{8,12},{12,8},{16,20},{20,16},{24,28},{28,24},{1,5},{5... | collective-permute-start | bytes 6291464 | tf_op jit(solution)/shard_map/ppermute | solution.py:298
  103.5 22.1 %collective-permute-start.7 = (f32[512,1024]{1,0:T(8,128)}, f32[512,1024]{1,0:T(8,128)}, u32[]{:S(2)}, u32[]{:S(2)}) collective-permute-start(f32[512,1024]{1,0:T(8,128)} %weight_part.12), channel_id=1, source_target_pairs={{0,4},{4,0},{8,12},{12,8},{16,20},{20,16},{24,28},{28,24},{1,5},{5... | collective-permute-start | bytes 6291464 | tf_op jit(solution)/shard_map/ppermute | solution.py:298
  108.7 48.2 %collective-permute-start.9 = (f32[512,1024]{1,0:T(8,128)}, f32[512,1024]{1,0:T(8,128)}, u32[]{:S(2)}, u32[]{:S(2)}) collective-permute-start(f32[512,1024]{1,0:T(8,128)} %weight_part.15), channel_id=1, source_target_pairs={{0,2},{1,3},{2,0},{3,1},{4,6},{5,7},{6,4},{7,5},{8,10},{9,11},{10,... | collective-permute-start | bytes 6291464 | tf_op jit(solution)/shard_map/ppermute | solution.py:298
  113.6 48.2 %collective-permute-start = (f32[512,1024]{1,0:T(8,128)}, f32[512,1024]{1,0:T(8,128)}, u32[]{:S(2)}, u32[]{:S(2)}) collective-permute-start(f32[512,1024]{1,0:T(8,128)} %weight_part.8), channel_id=1, source_target_pairs={{0,4},{4,0},{8,12},{12,8},{16,20},{20,16},{24,28},{28,24},{1,5},{5... | collective-permute-start | bytes 6291464 | tf_op jit(solution)/shard_map/ppermute | solution.py:298
  118.8 48.8 %collective-permute-start.2 = (f32[512,1024]{1,0:T(8,128)}, f32[512,1024]{1,0:T(8,128)}, u32[]{:S(2)}, u32[]{:S(2)}) collective-permute-start(f32[512,1024]{1,0:T(8,128)} %weight_part.11), channel_id=1, source_target_pairs={{0,1},{1,0},{2,3},{3,2},{4,5},{5,4},{6,7},{7,6},{8,9},{9,8},{10,11... | collective-permute-start | bytes 6291464 | tf_op jit(solution)/shard_map/ppermute | solution.py:298
  120.3 51.6 %all-to-all-start.2 = ((bf16[8,48,1024]{2,1,0:T(8,128)(2,1)}), bf16[8,48,1024]{2,1,0:T(8,128)(2,1)S(1)}, u32[]{:S(2)}, u32[]{:S(2)}) async-start(bf16[8,48,1024]{2,1,0:T(8,128)(2,1)} %bitcast.43), calls=%async_computation.2 | async-start | bytes 1572864 | tf_op jit(solution)/shard_map/all_to_all | solution.py:442
  160.3 29.2 %collective-permute-start.10 = (f32[512,512]{1,0:T(8,128)}, f32[512,512]{1,0:T(8,128)}, u32[]{:S(2)}, u32[]{:S(2)}) collective-permute-start(f32[512,512]{1,0:T(8,128)} %get-tuple-element.62), channel_id=1, source_target_pairs={{0,1},{1,0},{2,3},{3,2},{4,5},{5,4},{6,7},{7,6},{8,9},{9,8},{10,11... | collective-permute-start | bytes 3145736 | tf_op jit(solution)/shard_map/ppermute | solution.py:298
  170.9 24.6 %collective-permute-start.3 = (f32[512,512]{1,0:T(8,128)}, f32[512,512]{1,0:T(8,128)}, u32[]{:S(2)}, u32[]{:S(2)}) collective-permute-start(f32[512,512]{1,0:T(8,128)} %get-tuple-element.60), channel_id=1, source_target_pairs={{0,2},{1,3},{2,0},{3,1},{4,6},{5,7},{6,4},{7,5},{8,10},{9,11},{10,... | collective-permute-start | bytes 3145736 | tf_op jit(solution)/shard_map/ppermute | solution.py:298
  171.9 109.8 %all-to-all-start.3 = ((bf16[8,48,1024]{2,1,0:T(8,128)(2,1)}), bf16[8,48,1024]{2,1,0:T(8,128)(2,1)S(1)}, u32[]{:S(2)}, u32[]{:S(2)}) async-start(bf16[8,48,1024]{2,1,0:T(8,128)(2,1)} %bitcast.17), calls=%async_computation.3 | async-start | bytes 1572864 | tf_op jit(solution)/shard_map/all_to_all | solution.py:442
  191.5 31.7 %collective-permute-start.13 = (f32[128,512]{1,0:T(8,128)S(1)}, f32[128,512]{1,0:T(8,128)}, u32[]{:S(2)}, u32[]{:S(2)}) collective-permute-start(f32[128,512]{1,0:T(8,128)S(1)} %get-tuple-element.71), channel_id=1, source_target_pairs={{0,24},{4,28},{8,16},{12,20},{16,8},{20,12},{24,0},{28,4},{1,25},{... | collective-permute-start | bytes 786440 | tf_op jit(solution)/shard_map/ppermute | solution.py:298
  192.0 36.9 %collective-permute-start.12 = (f32[128,512]{1,0:T(8,128)}, f32[128,512]{1,0:T(8,128)}, u32[]{:S(2)}, u32[]{:S(2)}) collective-permute-start(f32[128,512]{1,0:T(8,128)} %get-tuple-element.72), channel_id=1, source_target_pairs={{0,16},{4,20},{8,24},{12,28},{16,0},{20,4},{24,8},{28,12},{1,17},{... | collective-permute-start | bytes 786440 | tf_op jit(solution)/shard_map/ppermute | solution.py:298
  195.3 33.6 %collective-permute-start.11 = (f32[128,512]{1,0:T(8,128)S(1)}, f32[128,512]{1,0:T(8,128)}, u32[]{:S(2)}, u32[]{:S(2)}) collective-permute-start(f32[128,512]{1,0:T(8,128)S(1)} %get-tuple-element.70), channel_id=1, source_target_pairs={{0,8},{4,12},{8,0},{12,4},{16,24},{20,28},{24,16},{28,20},{1,9},{5... | collective-permute-start | bytes 786440 | tf_op jit(solution)/shard_map/ppermute | solution.py:298
  197.5 37.4 %collective-permute-start.6 = (f32[128,512]{1,0:T(8,128)}, f32[128,512]{1,0:T(8,128)}, u32[]{:S(2)}, u32[]{:S(2)}) collective-permute-start(f32[128,512]{1,0:T(8,128)} %get-tuple-element.68), channel_id=1, source_target_pairs={{0,24},{4,28},{8,16},{12,20},{16,8},{20,12},{24,0},{28,4},{1,25},{... | collective-permute-start | bytes 786440 | tf_op jit(solution)/shard_map/ppermute | solution.py:298
  198.0 41.7 %collective-permute-start.5 = (f32[128,512]{1,0:T(8,128)}, f32[128,512]{1,0:T(8,128)}, u32[]{:S(2)}, u32[]{:S(2)}) collective-permute-start(f32[128,512]{1,0:T(8,128)} %get-tuple-element.69), channel_id=1, source_target_pairs={{0,16},{4,20},{8,24},{12,28},{16,0},{20,4},{24,8},{28,12},{1,17},{... | collective-permute-start | bytes 786440 | tf_op jit(solution)/shard_map/ppermute | solution.py:298
  223.2 16.5 %collective-permute-start.4 = (f32[128,512]{1,0:T(8,128)}, f32[128,512]{1,0:T(8,128)}, u32[]{:S(2)}, u32[]{:S(2)}) collective-permute-start(f32[128,512]{1,0:T(8,128)} %get-tuple-element.67), channel_id=1, source_target_pairs={{0,8},{4,12},{8,0},{12,4},{16,24},{20,28},{24,16},{28,20},{1,9},{5... | collective-permute-start | bytes 786440 | tf_op jit(solution)/shard_map/ppermute | solution.py:298
  241.9 42.2 %collective-permute-start.16 = (f32[128,1024]{1,0:T(8,128)}, f32[128,1024]{1,0:T(8,128)}, u32[]{:S(2)}, u32[]{:S(2)}) collective-permute-start(f32[128,1024]{1,0:T(8,128)} %maximum_multiply_fusion.1), channel_id=1, source_target_pairs={{0,3},{1,2},{2,1},{3,0},{4,7},{5,6},{6,5},{7,4},{8,11},{9,10},{10,... | collective-permute-start | bytes 1572872 | tf_op jit(solution)/shard_map/ppermute | solution.py:298
  244.0 40.2 %collective-permute-start.15 = (f32[128,1024]{1,0:T(8,128)}, f32[128,1024]{1,0:T(8,128)}, u32[]{:S(2)}, u32[]{:S(2)}) collective-permute-start(f32[128,1024]{1,0:T(8,128)} %maximum_multiply_fusion.1), channel_id=1, source_target_pairs={{0,2},{1,3},{2,0},{3,1},{4,6},{5,7},{6,4},{7,5},{8,10},{9,11},{10,... | collective-permute-start | bytes 1572872 | tf_op jit(solution)/shard_map/ppermute | solution.py:298
  244.5 39.7 %collective-permute-start.14 = (f32[128,1024]{1,0:T(8,128)}, f32[128,1024]{1,0:T(8,128)}, u32[]{:S(2)}, u32[]{:S(2)}) collective-permute-start(f32[128,1024]{1,0:T(8,128)} %maximum_multiply_fusion.1), channel_id=1, source_target_pairs={{0,1},{1,0},{2,3},{3,2},{4,5},{5,4},{6,7},{7,6},{8,9},{9,8},{10,11... | collective-permute-start | bytes 1572872 | tf_op jit(solution)/shard_map/ppermute | solution.py:298
  245.4 22.1 %collective-permute-start.17 = (f32[1,1024]{1,0:T(1,128)S(1)}, f32[1,1024]{1,0:T(1,128)S(1)}, u32[]{:S(2)}, u32[]{:S(2)}) collective-permute-start(f32[1,1024]{1,0:T(1,128)S(1)} %slice_add_fusion), channel_id=1, source_target_pairs={{0,1},{1,0},{2,3},{3,2},{4,5},{5,4},{6,7},{7,6},{8,9},{9,8},{10,11... | collective-permute-start | bytes 12296 | tf_op jit(solution)/shard_map/ppermute | solution.py:298
  272.3 4.3 %collective-permute-start.20 = (f32[1,1024]{1,0:T(1,128)S(1)}, f32[1,1024]{1,0:T(1,128)S(1)}, u32[]{:S(2)}, u32[]{:S(2)}) collective-permute-start(f32[1,1024]{1,0:T(1,128)S(1)} %add.321), channel_id=1, source_target_pairs={{0,8},{4,12},{8,0},{12,4},{16,24},{20,28},{24,16},{28,20},{1,9},{5... | collective-permute-start | bytes 12296 | tf_op jit(solution)/shard_map/ppermute | solution.py:298
  276.6 4.5 %collective-permute-start.21 = (f32[1,1024]{1,0:T(1,128)S(1)}, f32[1,1024]{1,0:T(1,128)S(1)}, u32[]{:S(2)}, u32[]{:S(2)}) collective-permute-start(f32[1,1024]{1,0:T(1,128)S(1)} %add.322), channel_id=1, source_target_pairs={{0,16},{4,20},{8,24},{12,28},{16,0},{20,4},{24,8},{28,12},{1,17},{... | collective-permute-start | bytes 12296 | tf_op jit(solution)/shard_map/ppermute | solution.py:298
  (36 other events, 310.2 us)
where the time goes:
time: 292 us; the launch traced here: 287 us
  waiting for transfers between devices  117 us (40%)
  Pallas kernels  85.8 us (29%)
  starting transfers between devices  48.5 us (17%)
  other arithmetic  17.9 us (6%)
  local copies, waits for them, and re-layouts  17.1 us (6%)
    ppermute x22, waiting for transfers between devices, exchange(): return lax.ppermute(x, axis, [(i, i ^ bits) for i in range(size)])  101 us
    pallas_call x2, Pallas kernels, local(): pl.pallas_call(functools.partial(layer_kernel, lines, length, faces is no...  50.2 us
    pallas_call x8, Pallas kernels, weight_part(): pl.pallas_call(functools.partial(weight_kernel, chunks, blocks, add is no...  30.8 us
    ppermute x22, starting transfers between devices, exchange(): return lax.ppermute(x, axis, [(i, i ^ bits) for i in range(size)])  25.3 us
    all_to_all x2, waiting for transfers between devices, local(): lax.all_to_all(s, 'tile', split_axis=0, concat_axis=0, tiled=True)  16.1 us
    unnamed x71, local copies, waits for them, and re-layouts  15.8 us
    all_to_all x2, starting transfers between devices, local(): lax.all_to_all(s, 'tile', split_axis=0, concat_axis=0, tiled=True)  12.7 us
    all_to_all x2, starting transfers between devices, local(): lax.all_to_all(r[0], 'tile', split_axis=0, concat_axis=0, tiled=True)  10.4 us
  transfers between devices with their start and end apart: 26, of which 14 were waited for; matrix products, arithmetic and copies ran while one was open for 6% of the time, Pallas kernels for 19%

commit v1 on v0

v1 whole, which is shorter than its diff:
```python
import functools

import jax
import jax.numpy as jnp
import numpy as np
from jax import lax
from jax.experimental import pallas as pl
from jax.experimental.pallas import tpu as pltpu
from jax.sharding import PartitionSpec as P

HEADS = 16
BF = jnp.bfloat16
F32 = jnp.float32
VMEM_BYTES = 56 * 1024 * 1024


def nn(a, b):
    return lax.dot_general(a, b, (((1,), (0,)), ((), ())), preferred_element_type=F32)


def nt(a, b):
    return lax.dot_general(a, b, (((1,), (1,)), ((), ())), preferred_element_type=F32)


def tn(a, b):
    return lax.dot_general(a, b, (((0,), (0,)), ((), ())), preferred_element_type=F32)


def one_hot(index_ref, width):
    rows = index_ref.shape[0]
    columns = lax.broadcasted_iota(jnp.int32, (rows, width), 1)
    return jnp.where(columns == index_ref[...], 1.0, 0.0).astype(BF)


def pack_kernel(tok_ref, cot_ref, index_ref, *refs):
    both = refs[-1]
    rows = tok_ref.shape[0]
    both[:rows] = tok_ref[...]
    both[rows:] = cot_ref[...]
    take = index_ref.shape[0] // (len(refs) - 1)
    for c, out in enumerate(refs[:-1]):
        columns = lax.broadcasted_iota(jnp.int32, (take, 2 * rows), 1)
        picked = jnp.where(columns == index_ref[c * take : (c + 1) * take], 1.0, 0.0).astype(BF)
        out[...] = nn(picked, both[...]).astype(BF)


def unpack_kernel(chunks, *refs):
    backs, index_ref, out_tok, out_cot, both = refs[:chunks], refs[chunks], refs[-3], refs[-2], refs[-1]
    take = backs[0].shape[0]
    for c, back in enumerate(backs):
        both[c * take : (c + 1) * take] = back[...]
    rows = out_tok.shape[0]
    for w, out in enumerate((out_tok, out_cot)):
        columns = lax.broadcasted_iota(jnp.int32, (rows, chunks * take), 1)
        picked = jnp.where(columns == index_ref[w * rows : (w + 1) * rows], 1.0, 0.0).astype(BF)
        out[...] = nn(picked, both[...]).astype(BF)


def face_kernel(scal_ref, face_ref, fcot_ref, gain_ref, normed_ref, early_ref):
    hidden = face_ref[...].astype(F32)
    inverse = lax.rsqrt(jnp.mean(hidden * hidden, axis=-1, keepdims=True) + 1e-06)
    normed = (hidden * inverse * gain_ref[...]).astype(BF)
    normed_ref[...] = normed
    early_ref[...] = jnp.where(scal_ref[0] == 0, fcot_ref[...], normed)


def edge_kernel(
    scal_ref, arrived_ref, index_ref, turn_ref, gain_ref, z_ref, g_ref, normed_ref, early_ref
):
    half = z_ref.shape[1] // 2
    edges = z_ref.shape[0]
    picked = one_hot(index_ref, arrived_ref.shape[0])
    first = nn(picked, arrived_ref[:, :half])
    second = nn(picked, arrived_ref[:, half:])
    cosine = turn_ref[:, 0:1]
    sine = turn_ref[:, 1:2]
    turned = jnp.concatenate(
        [cosine * first - sine * second, sine * first + cosine * second], axis=1
    )
    hidden = turned[:edges]
    z_ref[...] = hidden.astype(BF)
    g = turned[edges:].astype(BF)
    g_ref[...] = g
    inverse = lax.rsqrt(jnp.mean(hidden * hidden, axis=-1, keepdims=True) + 1e-06)
    normed = (hidden * inverse * gain_ref[...]).astype(BF)
    normed_ref[...] = normed
    early_ref[...] = jnp.where(scal_ref[0] == 0, g, normed)


def layer_kernel(
    lines,
    aliased,
    scal_ref,
    face_ref,
    fcot_ref,
    z_edge_ref,
    g_edge_ref,
    normed_face_ref,
    normed_edge_ref,
    back_index_ref,
    turn_ref,
    gain_ref,
    wqkv_ref,
    wo_ref,
    *refs,
):
    refs = refs[2:] if aliased else refs
    (
        face_out,
        face_grad,
        back_ref,
        keep_a,
        send_a,
        keep_b,
        send_b,
        gain_part,
        z_s,
        g_s,
        norm_s,
        qkv_s,
        dm_s,
        mix_s,
        stk_s,
        dn_s,
        y_s,
        edge_s,
    ) = refs
    width = z_s.shape[1]
    half = width // 2
    face_len = face_ref.shape[2]
    edges = z_edge_ref.shape[0]
    edge_len = edges // lines
    length = face_len + edge_len
    faces = lines * face_len
    head_dim = width // HEADS
    scale = head_dim ** (-0.5)
    gain = gain_ref[...]

    for l in range(lines):
        z_s[l * face_len : (l + 1) * face_len] = face_ref[0, l]
        g_s[l * face_len : (l + 1) * face_len] = fcot_ref[0, l]
    z_s[faces:] = z_edge_ref[...]
    g_s[faces:] = g_edge_ref[...]
    norm_s[:faces] = normed_face_ref[...]
    norm_s[faces:] = normed_edge_ref[...]

    tile = 512

    @pl.loop(0, 3 * width // tile)
    def _(j):
        cols = pl.ds(pl.multiple_of(j * tile, tile), tile)
        qkv_s[:, cols] = nn(norm_s[...], wqkv_ref[:, cols]).astype(BF)

    @pl.loop(0, width // tile)
    def _(j):
        cols = pl.ds(pl.multiple_of(j * tile, tile), tile)
        dm_s[:, cols] = nt(g_s[...], wo_ref[cols, :]).astype(BF)

    pair = 2 * head_dim
    low = lax.broadcasted_iota(jnp.int32, (length, pair), 1) < head_dim
    key_row = lax.broadcasted_iota(jnp.int32, (length, length), 0)

    def split(x):
        zero = jnp.zeros_like(x)
        return jnp.concatenate([jnp.where(low, x, zero), jnp.where(low, zero, x)], axis=0)

    @pl.loop(0, lines)
    def _(l):
        top = pl.ds(pl.multiple_of(l * face_len, face_len), face_len)
        bottom = pl.ds(pl.multiple_of(faces + l * edge_len, edge_len), edge_len)
        live = key_row < scal_ref[l] + face_len

        def load(ref, at):
            return jnp.concatenate([ref[top, at : at + pair], ref[bottom, at : at + pair]], axis=0)

        def store(ref, at, value):
            ref[top, at : at + pair] = value[:face_len].astype(BF)
            ref[bottom, at : at + pair] = value[face_len:].astype(BF)

        for p in range(HEADS // 2):
            at = p * pair
            q = load(qkv_s, at)
            k2 = split(load(qkv_s, width + at))
            v2 = split(load(qkv_s, 2 * width + at))
            dm = load(dm_s, at)
            scores = nt(k2, q) * scale
            d_probs = nt(v2, dm)
            probs_b, d_scores = [], []
            for h in range(2):
                part = slice(h * length, (h + 1) * length)
                s = jnp.where(live, scores[part], -1e30)
                e = jnp.exp(s - jnp.max(s, axis=0, keepdims=True))
                probs = e * (1.0 / jnp.sum(e, axis=0, keepdims=True))
                d = d_probs[part]
                inner = jnp.sum(probs * d, axis=0, keepdims=True)
                probs_b.append(probs.astype(BF))
                d_scores.append((probs * (d - inner) * scale).astype(BF))
            pb = jnp.concatenate(probs_b, axis=0)
            ds = jnp.concatenate(d_scores, axis=0)
            store(mix_s, at, tn(pb, v2))
            dv = nn(pb, dm)
            store(stk_s, 2 * width + at, jnp.where(low, dv[:length], dv[length:]))
            store(stk_s, at, tn(ds, k2))
            dk = nn(ds, q)
            store(stk_s, width + at, jnp.where(low, dk[:length], dk[length:]))

    @pl.loop(0, width // tile)
    def _(j):
        cols = pl.ds(pl.multiple_of(j * tile, tile), tile)
        y_s[:, cols] = (nn(mix_s[...], wo_ref[:, cols]) + z_s[:, cols].astype(F32)).astype(BF)
        dn_s[:, cols] = nt(stk_s[...], wqkv_ref[cols, :])

    gain_sum = jnp.zeros((1, width), F32)
    for i in range(2 * lines):
        size = face_len if i < lines else edge_len
        start = i * face_len if i < lines else faces + (i - lines) * edge_len
        at = slice(start, start + size)
        hidden = z_s[at].astype(F32)
        inverse = lax.rsqrt(jnp.mean(hidden * hidden, axis=-1, keepdims=True) + 1e-06)
        d_normed = dn_s[at]
        gain_sum = gain_sum + jnp.sum(d_normed * hidden * inverse, axis=0, keepdims=True)
        scaled = d_normed * gain
        mean = jnp.mean(scaled * hidden, axis=-1, keepdims=True)
        dz = inverse * scaled - hidden * (inverse * inverse * inverse * mean)
        dz = (g_s[at].astype(F32) + dz).astype(BF)
        if i < lines:
            face_out[0, i] = y_s[at]
            face_grad[0, i] = dz
        else:
            edge_s[edges + start - faces : edges + start - faces + size] = dz
    edge_s[:edges] = y_s[faces:]
    gain_part[...] = jnp.broadcast_to(gain_sum, gain_part.shape)
    cosine = turn_ref[:, 0:1]
    sine = turn_ref[:, 1:2]
    first = edge_s[:, :half].astype(F32)
    second = edge_s[:, half:].astype(F32)
    turned_first = (cosine * first + sine * second).astype(BF)
    turned_second = (cosine * second - sine * first).astype(BF)
    picked = one_hot(back_index_ref, 2 * edges)
    back_ref[:, :half] = nn(picked, turned_first).astype(BF)
    back_ref[:, half:] = nn(picked, turned_second).astype(BF)

    x_bit = scal_ref[lines]
    y_bit = scal_ref[lines + 1]

    @pl.when(x_bit == 0)
    def _():
        keep_a[...] = stk_s[:, :width]
        send_a[...] = stk_s[:, width : 2 * width]

    @pl.when(x_bit != 0)
    def _():
        send_a[...] = stk_s[:, :width]
        keep_a[...] = stk_s[:, width : 2 * width]

    @pl.when(y_bit == 0)
    def _():
        keep_b[...] = stk_s[:, 2 * width :]
        send_b[...] = mix_s[...]

    @pl.when(y_bit != 0)
    def _():
        send_b[...] = stk_s[:, 2 * width :]
        keep_b[...] = mix_s[...]


def weight_kernel(runs, parities, blocks, count, adds, pieces, column, scal_ref, *refs):
    operands = refs[:count]
    add_refs = refs[count : count + adds]
    outs = refs[count + adds : -3]
    lhs_s, lhs_t, rhs_s = refs[-3:]
    step = pl.program_id(0)
    depth, width = rhs_s.shape
    rows = depth // len(runs)
    part = width // 2
    size = part // blocks
    tile = width // (2 * pieces)

    def fill(at, src):
        for n, own in enumerate(parities):
            first = scal_ref[0] == (0 if own else 1)
            for b in range(blocks):
                left = src[:, 2 * b * size : (2 * b + 1) * size]
                right = src[:, (2 * b + 1) * size : (2 * b + 2) * size]
                to = n * part + b * size
                lhs_s[at : at + src.shape[0], to : to + size] = jnp.where(first, left, right)

    def load(swapped):
        for i, (faces, edges, chunk, late) in enumerate(runs):
            late_rows = operands[late][...]
            edge = operands[edges[swapped]][...]
            front = rows - edge.shape[0]
            face = operands[faces[swapped]][chunk * front : (chunk + 1) * front]
            at = i * rows
            if swapped:
                fill(at, late_rows)
                rhs_s[at : at + front] = face
                rhs_s[at + front : at + rows] = edge
            else:
                fill(at, face)
                fill(at + front, edge)
                rhs_s[at : at + rows] = late_rows

    @pl.when((step == 0) & (scal_ref[1] == 0))
    def _():
        load(0)

    @pl.when((step == 0) & (scal_ref[1] != 0))
    def _():
        load(1)

    @pl.when(step == 0)
    def _():
        for n in range(0, lhs_t.shape[0], 128):
            lhs_t[n : n + 128] = lhs_s[:, n : n + 128].T

    col = column(step, scal_ref)
    total = nn(lhs_t[...], rhs_s[:, pl.ds(pl.multiple_of(col * tile, tile), tile)])
    for ref in add_refs:
        total = total + ref[...]
    if len(outs) == 1:
        outs[0][...] = total
    else:
        for n, out in enumerate(outs):

            @pl.when(step == n)
            def _(out=out):
                out[...] = total


def weight_part(scal, runs, parities, blocks, operands, adds, pieces, halved, deps, tracked):
    width = operands[-1].shape[1]
    tile = width // (2 * pieces)
    rows = len(parities) * (width // 2)
    depth = len(runs) * operands[runs[0][3]].shape[0]

    def column(j, s):
        if not halved:
            return j
        second = j // pieces
        return ((1 - s[2]) + second * (2 * s[2] - 1)) * pieces + j % pieces

    def kernel(scal_ref, *refs):
        refs = refs[: len(operands) + len(adds)] + refs[len(operands) + len(adds) + len(deps) :]
        weight_kernel(
            runs, parities, blocks, len(operands), len(adds), pieces, column, scal_ref, *refs
        )

    whole = [pl.BlockSpec(o.shape, lambda j, s: (0, 0)) for o in operands]
    add_specs = [
        pl.BlockSpec((rows, tile), lambda j, s, at=at: (at, column(j, s))) for _, at in adds
    ]
    if halved:
        out_specs = [pl.BlockSpec((rows, tile), lambda j, s: (0, 0))] * (2 * pieces)
        out_shape = [jax.ShapeDtypeStruct((rows, tile), F32)] * (2 * pieces)
    else:
        out_specs = [pl.BlockSpec((rows, tile), lambda j, s: (0, j))]
        out_shape = [jax.ShapeDtypeStruct((rows, width), F32)]
    return pl.pallas_call(
        kernel,
        grid_spec=pltpu.PrefetchScalarGridSpec(
            num_scalar_prefetch=1,
            grid=(2 * pieces,),
            in_specs=whole + add_specs + [pl.BlockSpec(memory_space=pl.ANY)] * len(deps),
            out_specs=out_specs,
            scratch_shapes=[
                pltpu.VMEM((depth, rows), BF),
                pltpu.VMEM((rows, depth), BF),
                pltpu.VMEM((depth, width), BF),
            ],
        ),
        out_shape=out_shape,
        compiler_params=pltpu.CompilerParams(vmem_limit_bytes=VMEM_BYTES),
        cost_estimate=pl.CostEstimate(
            flops=2 * rows * depth * width, bytes_accessed=tracked, transcendentals=0
        ),
        name="weight_part",
    )(scal, *operands, *[a for a, _ in adds], *deps)


def block_kernel(blocks, count, scal_ref, *refs):
    groups = (refs[:count], refs[count : 2 * count])
    outs = refs[2 * count :]
    columns = groups[0][0].shape[1]
    size = groups[0][0].shape[0] // blocks
    for o, out in enumerate(outs):
        at = pl.ds(pl.multiple_of((scal_ref[0] ^ o) * size, size), size)
        for n, parts in enumerate(groups):
            total = parts[0][at]
            for p in parts[1:]:
                total = total + p[at]
            out[:, n * columns : (n + 1) * columns] = total


def sum_kernel(factor, scal_ref, *refs):
    total = refs[0][...]
    for ref in refs[1:-1]:
        total = total + ref[...]
    refs[-1][...] = total * factor


def place_kernel(pieces, devices, scal_ref, *refs):
    qkv_ref, out_ref = refs[-2], refs[-1]
    width = out_ref.shape[1]
    bits = devices.bit_length() - 1
    for n in range(pieces):
        for o in range(devices):
            src = refs[n * devices + o]
            part = src.shape[1] // 2
            device = scal_ref[0] ^ o
            for group in range(2):
                value = slice(group * part, (group + 1) * part)
                rest = [b for b in range(bits) if b != group]
                at = ((device >> rest[0]) & 1) * (width // 2) + n * (width // 2 // pieces)
                unit = width // 2 // pieces
                for b in rest[1:]:
                    unit = unit // 2
                    at = at + ((device >> b) & 1) * unit
                which = (device >> group) & 1
                if group == 0:
                    at = pl.multiple_of(at + which * width, part)
                    qkv_ref[:, pl.ds(at, part)] = src[:, value]
                else:

                    @pl.when(which == 0)
                    def _(src=src, value=value, at=at, part=part):
                        cols = pl.ds(pl.multiple_of(at + 2 * width, part), part)
                        qkv_ref[:, cols] = src[:, value]

                    @pl.when(which != 0)
                    def _(src=src, value=value, at=at, part=part):
                        out_ref[:, pl.ds(pl.multiple_of(at, part), part)] = src[:, value]


def exchange(x, axis, bits, size):
    return lax.ppermute(x, axis, [(i, i ^ bits) for i in range(size)])


def whole_call(kernel, name, scal, out_shape, operands, deps=(), scratch=(), flops=0):
    def body(scal_ref, *refs):
        kernel(scal_ref, *refs[: len(operands)], *refs[len(operands) + len(deps) :])

    def spec(shape):
        return pl.BlockSpec(shape, lambda i, s: (0,) * len(shape))

    moved = sum(int(np.prod(o.shape)) * o.dtype.itemsize for o in [*operands, *out_shape])
    return pl.pallas_call(
        body,
        grid_spec=pltpu.PrefetchScalarGridSpec(
            num_scalar_prefetch=1,
            grid=(1,),
            in_specs=[spec(o.shape) for o in operands]
            + [pl.BlockSpec(memory_space=pl.ANY)] * len(deps),
            out_specs=[spec(o.shape) for o in out_shape],
            scratch_shapes=list(scratch),
        ),
        out_shape=out_shape,
        compiler_params=pltpu.CompilerParams(vmem_limit_bytes=VMEM_BYTES),
        cost_estimate=pl.CostEstimate(flops=flops, bytes_accessed=moved, transcendentals=0),
        name=name,
    )(scal, *operands, *deps)


def local(
    face_tokens,
    edge_tokens,
    face_cotangent,
    edge_cotangent,
    rotation,
    counts,
    norm_gain,
    qkv_weight,
    out_weight,
):
    T = lax.axis_size("tile")
    D = lax.axis_size("dp")
    me_t = lax.axis_index("tile")
    me_d = lax.axis_index("dp")
    LD, FL, width = face_tokens.shape[1:]
    K = edge_tokens.shape[1]
    EL = K * T
    NLG = edge_tokens.shape[2]
    length = FL + EL
    chunks = 2
    lines = LD // chunks
    RB = lines * K
    packed = T * 2 * RB
    factor = float(D * T * LD * length) ** (-0.5)
    x_bit = (me_d % 2).astype(jnp.int32)
    y_bit = ((me_d // 2) % 2).astype(jnp.int32)
    gain = norm_gain.reshape(1, width)

    def struct(*shape, dtype=BF):
        return jax.ShapeDtypeStruct(shape, dtype)

    order = np.zeros((chunks, T, 2, lines, K), np.int32)
    for c in range(chunks):
        for w in range(2):
            t, l, k = np.meshgrid(np.arange(T), np.arange(lines), np.arange(K), indexing="ij")
            order[c, :, w] = w * K * NLG + k * NLG + t * LD + c * lines + l
    sent = whole_call(
        lambda s, *refs: pack_kernel(*refs),
        "pack",
        y_bit.reshape(1),
        [struct(packed, width)] * chunks,
        [
            edge_tokens.reshape(K * NLG, width),
            edge_cotangent.reshape(K * NLG, width),
            jnp.asarray(order.reshape(-1, 1)),
        ],
        scratch=[pltpu.VMEM((2 * K * NLG, width), BF)],
    )
    arrived = [lax.all_to_all(s, "tile", split_axis=0, concat_axis=0, tiled=True) for s in sent]

    face_rows = face_tokens.reshape(LD * FL, width)
    face_cots = face_cotangent.reshape(LD * FL, width)
    face_normed, face_early = whole_call(
        face_kernel,
        "face_norm",
        y_bit.reshape(1),
        [struct(LD * FL, width)] * 2,
        [face_rows, face_cots, gain],
    )
    got_face_a = exchange(face_normed, "dp", 1, D)
    got_face_b = exchange(face_early, "dp", 2, D)

    my_turns = lax.dynamic_slice_in_dim(rotation, me_t * LD, LD)
    my_counts = lax.dynamic_slice_in_dim(counts, me_t * LD, LD)
    spos = np.arange(EL)
    edge_parts, results, got_edges, got_late = [], [], [], []
    faces = None
    for c in range(chunks):
        turns = my_turns[c * lines : (c + 1) * lines]
        flip = turns >= 2
        pos = jnp.where(flip[:, None], EL - 1 - spos[None, :], spos[None, :])
        row = (pos // K) * (2 * RB) + jnp.arange(lines)[:, None] * K + pos % K
        index = jnp.concatenate([row, row + RB], axis=0).reshape(-1, 1).astype(jnp.int32)
        cosine = (turns == 0).astype(F32) - (turns == 2).astype(F32)
        sine = (turns == 1).astype(F32) - (turns == 3).astype(F32)
        turn = jnp.stack([cosine, sine], axis=-1)
        turn = jnp.broadcast_to(turn[None, :, None, :], (2, lines, EL, 2)).reshape(-1, 2)
        sk = np.arange(T)[:, None, None, None] * K + np.arange(K)[None, None, None, :]
        bk = jnp.where(flip[None, None, :, None], EL - 1 - sk, sk)
        back_index = (
            jnp.arange(2)[None, :, None, None] * (lines * EL)
            + jnp.arange(lines)[None, None, :, None] * EL
            + bk
        )
        back_index = back_index.reshape(-1, 1).astype(jnp.int32)
        scal = jnp.concatenate([my_counts[c * lines : (c + 1) * lines], jnp.stack([x_bit, y_bit])])
        edges = lines * EL
        z_edge, g_edge, normed_edge, early_edge = whole_call(
            edge_kernel,
            "edge_norm",
            y_bit.reshape(1),
            [struct(edges, width)] * 4,
            [arrived[c], index, turn, gain],
        )
        edge_parts.append((normed_edge, g_edge))
        got_edges.append((exchange(normed_edge, "dp", 1, D), exchange(early_edge, "dp", 2, D)))
        rows_all = lines * length
        row_shape = (rows_all, width)
        face_spec = pl.BlockSpec((1, lines, FL, width), lambda i, s, c=c: (0, c, 0, 0))
        normed_spec = pl.BlockSpec((lines * FL, width), lambda i, s, c=c: (c, 0))

        def full(shape):
            return pl.BlockSpec(shape, lambda i, s: (0,) * len(shape))

        operands = [
            face_tokens,
            face_cotangent,
            z_edge,
            g_edge,
            face_normed,
            normed_edge,
            back_index,
            turn,
            gain,
            qkv_weight,
            out_weight,
        ]
        in_specs = [face_spec, face_spec] + [full(o.shape) for o in operands[2:]]
        in_specs[4] = normed_spec
        if faces is not None:
            in_specs += [pl.BlockSpec(memory_space=pl.ANY)] * 2
            operands += list(faces)
        outs = pl.pallas_call(
            functools.partial(layer_kernel, lines, faces is not None),
            grid_spec=pltpu.PrefetchScalarGridSpec(
                num_scalar_prefetch=1,
                grid=(1,),
                in_specs=in_specs,
                out_specs=[face_spec, face_spec, full((packed, width))]
                + [full(row_shape)] * 4
                + [full((8, width))],
                scratch_shapes=[
                    pltpu.VMEM(row_shape, BF),
                    pltpu.VMEM(row_shape, BF),
                    pltpu.VMEM(row_shape, BF),
                    pltpu.VMEM((rows_all, 3 * width), BF),
                    pltpu.VMEM(row_shape, BF),
                    pltpu.VMEM(row_shape, BF),
                    pltpu.VMEM((rows_all, 3 * width), BF),
                    pltpu.VMEM(row_shape, F32),
                    pltpu.VMEM(row_shape, BF),
                    pltpu.VMEM((2 * edges, width), BF),
                ],
            ),
            out_shape=[struct(*face_tokens.shape)] * 2
            + [struct(packed, width)]
            + [struct(*row_shape)] * 4
            + [struct(8, width, dtype=F32)],
            input_output_aliases={12: 0, 13: 1} if faces is not None else {},
            compiler_params=pltpu.CompilerParams(vmem_limit_bytes=VMEM_BYTES),
            cost_estimate=pl.CostEstimate(
                flops=2 * rows_all * width * width * 8 * 2, bytes_accessed=1 << 24, transcendentals=0
            ),
            name="layer",
        )(scal, *operands)
        faces = outs[:2]
        results.append(outs[2:])
        got_late.append((exchange(outs[4], "dp", 1, D), exchange(outs[6], "dp", 2, D)))
    returned = [
        lax.all_to_all(r[0], "tile", split_axis=0, concat_axis=0, tiled=True) for r in results
    ]

    gain_sum = sum(r[5] for r in results)
    for b in range(D.bit_length() - 1):
        gain_sum = gain_sum + exchange(gain_sum, "dp", 1 << b, D)
    for b in range(T.bit_length() - 1):
        gain_sum = gain_sum + exchange(gain_sum, "tile", 1 << b, T)

    blocks = T // 2
    chip = (me_t // 2).astype(jnp.int32)
    core = (me_t % 2).astype(jnp.int32)
    pieces = 2
    size = width // T
    bits = D.bit_length() - 1
    groups = []
    for group in range(2):
        first = [b for b in range(bits) if b != group][0]
        swap = y_bit if group else jnp.zeros_like(y_bit)
        scal = jnp.stack([core, swap, ((me_d >> first) & 1).astype(jnp.int32)])
        late = [r[1 + 2 * group] for r in results]
        got_face = (got_face_a, got_face_b)[group]
        normed_e, g_e = [e[0] for e in edge_parts], [e[1] for e in edge_parts]
        got_e = [e[group] for e in got_edges]
        got_l = [e[group] for e in got_late]
        operands = [face_normed, face_cots, *normed_e, *g_e, got_face, got_e[0], late[0], late[1], got_l[0]]
        runs = [((0, 1), (2, 4), 0, 8), ((0, 1), (3, 5), 1, 9), ((6, 6), (7, 7), 0, 10)]
        start = weight_part(
            scal, runs, (False, True), blocks, operands, [], pieces, False,
            [returned[0]] if group == 0 else [], 8 << 20,
        )[0]
        groups.append((scal, [got_face, got_e[1], got_l[1]], start, first))
    theirs = []
    runs = [((0, 0), (1, 1), 1, 2)]
    for scal, operands, start, first in groups:
        send = weight_part(
            scal, runs, (False,), blocks, operands, [(start, 0)], pieces, False, [], 8 << 20
        )[0]
        theirs.append(exchange(send, "tile", 1, T))
    halves = []
    for group, (scal, operands, start, first) in enumerate(groups):
        outs = weight_part(
            scal, runs, (True,), blocks, operands, [(start, 1), (theirs[group], 0)], pieces, True,
            [], 8 << 20,
        )
        parts = []
        for n in range(pieces):
            both = [outs[pieces + n], exchange(outs[n], "dp", 1 << first, D)]
            for b in range(bits):
                if b in (group, first):
                    continue
                columns = both[0].shape[1] // 2
                mine = (me_d >> b) & 1
                keep = [lax.dynamic_slice_in_dim(p, mine * columns, columns, 1) for p in both]
                give = [lax.dynamic_slice_in_dim(p, (1 - mine) * columns, columns, 1) for p in both]
                both = [sum(keep), exchange(sum(give), "dp", 1 << b, D)]
            parts.append(both)
        halves.append(parts)
    placed = []
    for n in range(pieces):
        parts = [*halves[0][n], *halves[1][n]]
        columns = 2 * parts[0].shape[1]
        outs = whole_call(
            functools.partial(block_kernel, blocks, 2),
            "row_blocks",
            chip.reshape(1),
            [struct(size, columns, dtype=F32)] * blocks,
            parts,
            deps=[returned[1], gain_sum] if n == 0 else [],
        )
        got = [exchange(outs[o], "tile", 2 * o, T) for o in range(1, blocks)]
        (mine,) = whole_call(
            functools.partial(sum_kernel, factor),
            "block_sum",
            chip.reshape(1),
            [struct(size, columns, dtype=F32)],
            [outs[0], *got],
        )
        placed += [mine] + [exchange(mine, "dp", o, D) for o in range(1, D)]

    back_order = np.zeros((2, K, NLG), np.int32)
    for w in range(2):
        k, t, c, l = np.meshgrid(
            np.arange(K), np.arange(T), np.arange(chunks), np.arange(lines), indexing="ij"
        )
        back_order[w] = (c * packed + t * 2 * RB + w * RB + l * K + k).reshape(K, NLG)
    edge_output, edge_grad = whole_call(
        lambda s, *refs: unpack_kernel(chunks, *refs),
        "unpack",
        chip.reshape(1),
        [struct(K * NLG, width)] * 2,
        [*returned, jnp.asarray(back_order.reshape(-1, 1))],
        scratch=[pltpu.VMEM((chunks * packed, width), BF)],
    )
    qkv_grad, out_grad = whole_call(
        functools.partial(place_kernel, pieces, D),
        "place",
        me_d.astype(jnp.int32).reshape(1),
        [struct(size, 3 * width, dtype=F32), struct(size, width, dtype=F32)],
        placed,
    )
    gain_grad = lax.dynamic_slice_in_dim(gain_sum[0], me_t * size, size) * factor
    shape = edge_tokens.shape
    return (
        faces[0],
        edge_output.reshape(shape),
        faces[1],
        edge_grad.reshape(shape),
        qkv_grad,
        out_grad,
        gain_grad,
    )


def solution(mesh):
    return jax.shard_map(
        local,
        mesh=mesh,
        in_specs=(
            P("dp", "tile", None, None),
            P("dp", "tile", None, None),
            P("dp", "tile", None, None),
            P("dp", "tile", None, None),
            P(),
            P(),
            P(),
            P(),
            P(),
        ),
        out_specs=(
            P("dp", "tile", None, None),
            P("dp", "tile", None, None),
            P("dp", "tile", None, None),
            P("dp", "tile", None, None),
            P("tile", None),
            P("tile", None),
            P("tile"),
        ),
        check_vma=False,
    )
```

time: 292 us -> 314 us (1.075)
  Pallas kernels: 85.8 us -> 125 us
  other arithmetic: 17.9 us -> 3.49 us
  starting transfers between devices: 48.5 us -> 57.4 us
  local copies, waits for them, and re-layouts: 17.1 us -> 11.6 us
  waiting for transfers between devices: 117 us -> 112 us
    pallas_call x12 -> x18, Pallas kernels: 85.8 us -> 125 us  [the longest x2 51.7 us: local(): pl.pallas_call(functools.partial(layer_kernel, lines, faces is not None),...]
    add x7 -> x1, other arithmetic: 13.4 us -> 0.01 us  [local(): gain_sum = sum((r[5] for r in results))]
    ppermute x22 -> x33, starting transfers between devices: 25.3 us -> 35 us  [exchange(): return lax.ppermute(x, axis, [(i, i ^ bits) for i in range(size)])]
    unnamed x71 -> x66, local copies, waits for them, and re-layouts: 15.8 us -> 6.54 us
    all_to_all x2, waiting for transfers between devices: 16.1 us -> 12.6 us  [local(): lax.all_to_all(s, 'tile', split_axis=0, concat_axis=0, tiled=True)]
    ppermute x22 -> x33, waiting for transfers between devices: 101 us -> 99.2 us  [exchange(): return lax.ppermute(x, axis, [(i, i ^ bits) for i in range(size)])]
  transfers between devices with their start and end apart: 26 -> 37, of which waited for: 14 -> 14; matrix products, arithmetic and copies ran while one was open for 6% -> 3% of each run, Pallas kernels for 19% -> 38%
where the time goes in v1:
time: 314 us; the launch traced here: 311 us
  Pallas kernels  125 us (40%)
  waiting for transfers between devices  112 us (36%)
  starting transfers between devices  57.4 us (18%)
  local copies, waits for them, and re-layouts  11.6 us (4%)
  other arithmetic  3.49 us (1%)
    ppermute x33, waiting for transfers between devices, exchange(): return lax.ppermute(x, axis, [(i, i ^ bits) for i in range(size)])  99.2 us
    pallas_call x2, Pallas kernels, local(): pl.pallas_call(functools.partial(layer_kernel, lines, faces is not None),...  51.7 us
    pallas_call x6, Pallas kernels, weight_part(): pl.pallas_call(kernel, grid_spec=pltpu.PrefetchScalarGridSpec(num_scalar_...  44.6 us
    ppermute x33, starting transfers between devices, exchange(): return lax.ppermute(x, axis, [(i, i ^ bits) for i in range(size)])  35 us
    pallas_call x10, Pallas kernels, whole_call(): pl.pallas_call(body, grid_spec=pltpu.PrefetchScalarGridSpec(num_scalar_pr...  29 us
    all_to_all x2, waiting for transfers between devices, local(): lax.all_to_all(s, 'tile', split_axis=0, concat_axis=0, tiled=True)  12.6 us
    all_to_all x2, starting transfers between devices, local(): lax.all_to_all(s, 'tile', split_axis=0, concat_axis=0, tiled=True)  12.1 us
    all_to_all x2, starting transfers between devices, local(): lax.all_to_all(r[0], 'tile', split_axis=0, concat_axis=0, tiled=True)  10.3 us
  transfers between devices with their start and end apart: 37, of which 14 were waited for; matrix products, arithmetic and copies ran while one was open for 3% of the time, Pallas kernels for 38%

profile of v1, /device:TPU:16, one launch (start us, length us, event | category | flops | bytes accessed | tf_op | source)
XLA Modules:
  0.0 310.6 jit_solution(2155718232215639895)
XLA Ops:
  0.7 3.9 %pack.1 = (bf16[384,1024]{1,0:T(8,128)(2,1)}, bf16[384,1024]{1,0:T(8,128)(2,1)}) custom-call(s32[1]{0:T(128)} %bitcast.1.scal_ref, bf16[384,1024]{1,0:T(8,128)(2,1)} %bitcast.43, bf16[384,1024]{1,0:T(8,128)(2,1)} %bitcast.44, s32[768,1]{1,0:T(8,128)} %constant.124.clone.refs_2_), custom_call_target="tpu_custom_call" | custom-call | bytes 3148800 | tf_op jit(solution)/shard_map/pack/pallas_call | solution.py:447
  4.6 5.3 %all-to-all-start.1 = ((bf16[8,48,1024]{2,1,0:T(8,128)(2,1)}), bf16[8,48,1024]{2,1,0:T(8,128)(2,1)S(1)}, u32[]{:S(2)}, u32[]{:S(2)}) async-start(bf16[8,48,1024]{2,1,0:T(8,128)(2,1)} %bitcast.48), calls=%async_computation.1 | async-start | bytes 1572864 | tf_op jit(solution)/shard_map/all_to_all | solution.py:513
  15.0 12.6 %all-to-all-done.1 = bf16[8,48,1024]{2,1,0:T(8,128)(2,1)S(1)} async-done(((bf16[8,48,1024]{2,1,0:T(8,128)(2,1)}), bf16[8,48,1024]{2,1,0:T(8,128)(2,1)S(1)}, u32[]{:S(2)}, u32[]{:S(2)}) %all-to-all-start.1) | async-done | bytes 786464 | tf_op jit(solution)/shard_map/all_to_all | solution.py:513
  27.6 6.7 %all-to-all-start = ((bf16[8,48,1024]{2,1,0:T(8,128)(2,1)}), bf16[8,48,1024]{2,1,0:T(8,128)(2,1)S(1)}, u32[]{:S(2)}, u32[]{:S(2)}) async-start(bf16[8,48,1024]{2,1,0:T(8,128)(2,1)} %bitcast.4), calls=%async_computation | async-start | bytes 1572864 | tf_op jit(solution)/shard_map/all_to_all | solution.py:513
  39.1 3.2 %edge_norm.3 = (bf16[192,1024]{1,0:T(8,128)(2,1)}, bf16[192,1024]{1,0:T(8,128)(2,1)}, bf16[192,1024]{1,0:T(8,128)(2,1)}, bf16[192,1024]{1,0:T(8,128)(2,1)}) custom-call(s32[1]{0:T(128)} %bitcast.1.scal_ref, bf16[384,1024]{1,0:T(8,128)(2,1)} %bitcast.41, s32[384,1]{1,0:T(8,128)} %reshape.205.refs_1_, f32[384,2]{1,0:T(8,128)} %bitcast.51, f32[1,1024]{1,0:T(1,128)} %bitcast.54), custom_call_target="tpu_custom_call" | custom-call | bytes 2368000 | tf_op jit(solution)/shard_map/edge_norm/pallas_call | solution.py:447
  42.3 25.7 %layer.2 = (bf16[1,6,64,1024]{3,2,1,0:T(8,128)(2,1)}, bf16[1,6,64,1024]{3,2,1,0:T(8,128)(2,1)}, bf16[384,1024]{1,0:T(8,128)(2,1)}, bf16[384,1024]{1,0:T(8,128)(2...) custom-call(s32[5]{0:T(128)} %get-tuple-element.122.scal_ref, ...), custom_call_target="tpu_custom_call" | custom-call | flops 12884901888 | bytes 16777216 | tf_op jit(solution)/shard_map/layer/pallas_call | solution.py:587
  70.1 5.1 %all-to-all-start.2 = ((bf16[8,48,1024]{2,1,0:T(8,128)(2,1)}), bf16[8,48,1024]{2,1,0:T(8,128)(2,1)S(1)}, u32[]{:S(2)}, u32[]{:S(2)}) async-start(bf16[8,48,1024]{2,1,0:T(8,128)(2,1)} %bitcast.47), calls=%async_computation.2 | async-start | bytes 1572864 | tf_op jit(solution)/shard_map/all_to_all | solution.py:624
  75.9 3.2 %edge_norm.2 = (bf16[192,1024]{1,0:T(8,128)(2,1)}, bf16[192,1024]{1,0:T(8,128)(2,1)}, bf16[192,1024]{1,0:T(8,128)(2,1)}, bf16[192,1024]{1,0:T(8,128)(2,1)}) custom-call(s32[1]{0:T(128)} %bitcast.1.scal_ref, bf16[384,1024]{1,0:T(8,128)(2,1)} %bitcast.42, s32[384,1]{1,0:T(8,128)} %reshape.204.refs_1_, f32[384,2]{1,0:T(8,128)} %bitcast.49, f32[1,1024]{1,0:T(1,128)} %bitcast.56), custom_call_target="tpu_custom_call" | custom-call | bytes 2368000 | tf_op jit(solution)/shard_map/edge_norm/pallas_call | solution.py:447
  79.0 26.0 %layer.3 = (bf16[1,6,64,1024]{3,2,1,0:T(8,128)(2,1)}, bf16[1,6,64,1024]{3,2,1,0:T(8,128)(2,1)}, bf16[384,1024]{1,0:T(8,128)(2,1)}, bf16[384,1024]{1,0:T(8,128)(2...) custom-call(s32[5]{0:T(128)} %get-tuple-element.121.scal_ref, ...), custom_call_target="tpu_custom_call", output_to_operand_aliasing={{0}: (12, {}), {1}: (13, {})} | custom-call | flops 12884901888 | bytes 16777216 | tf_op jit(solution)/shard_map/layer/pallas_call | solution.py:587
  109.2 24.3 %collective-permute-done.8.refs_1_ = bf16[192,1024]{1,0:T(8,128)(2,1)} collective-permute-done((bf16[192,1024]{1,0:T(8,128)(2,1)S(1)}, bf16[192,1024]{1,0:T(8,128)(2,1)}, u32[]{:S(2)}, u32[]{:S(2)}) %collective-permute-start.8) | collective-permute-done | bytes 393248 | tf_op jit(solution)/shard_map/ppermute | solution.py:436
  138.2 9.7 %weight_part.9.refs_3_ = f32[1024,1024]{1,0:T(8,128)} custom-call(s32[3]{0:T(128)} %pad_add_fusion.3.scal_ref, bf16[384,1024]{1,0:T(8,128)(2,1)} %get-tuple-element.58.normed_face_ref.refs_0_, bf16[384,1024]{1,0:T(8,128)(2,1)} %bitcast.39, bf16[192,1024]{1,0:T(8,128)(2,1)} %get-tuple-element.63.normed_edge_ref.refs_2_, ...), custom_call_target="tpu_custom_call" | custom-call | flops 2415919104 | bytes 8388608 | tf_op jit(solution)/shard_map/weight_part/pallas_call | solution.py:359
  147.9 6.0 %weight_part.10 = f32[512,1024]{1,0:T(8,128)} custom-call(s32[3]{0:T(128)} %pad_add_fusion.3.scal_ref, bf16[384,1024]{1,0:T(8,128)(2,1)} %copy-done.3, bf16[192,1024]{1,0:T(8,128)(2,1)} %collective-permute-done.8.refs_1_, bf16[384,1024]{1,0:T(8,128)(2,1)} %copy-done.4, f32[1024,1024]{1,0:T(8,128)} %weight_part.9.refs_3_), custom_call_target="tpu_custom_call" | custom-call | flops 402653184 | bytes 8388608 | tf_op jit(solution)/shard_map/weight_part/pallas_call | solution.py:359
  153.9 16.1 %collective-permute-done.3.refs_7_ = bf16[192,1024]{1,0:T(8,128)(2,1)} collective-permute-done((bf16[192,1024]{1,0:T(8,128)(2,1)S(1)}, bf16[192,1024]{1,0:T(8,128)(2,1)}, u32[]{:S(2)}, u32[]{:S(2)}) %collective-permute-start.3) | collective-permute-done | bytes 393248 | tf_op jit(solution)/shard_map/ppermute | solution.py:436
  171.0 9.8 %weight_part.6.refs_3_ = f32[1024,1024]{1,0:T(8,128)} custom-call(s32[3]{0:T(128)} %pad_add_fusion.2.scal_ref, bf16[384,1024]{1,0:T(8,128)(2,1)} %get-tuple-element.58.normed_face_ref.refs_0_, bf16[384,1024]{1,0:T(8,128)(2,1)} %bitcast.40, bf16[192,1024]{1,0:T(8,128)(2,1)} %get-tuple-element.63.normed_edge_ref.refs_2_, ...), custom_call_target="tpu_custom_call" | custom-call | flops 2415919104 | bytes 8388608 | tf_op jit(solution)/shard_map/weight_part/pallas_call | solution.py:359
  180.7 6.0 %weight_part.7 = f32[512,1024]{1,0:T(8,128)} custom-call(s32[3]{0:T(128)} %pad_add_fusion.2.scal_ref, bf16[384,1024]{1,0:T(8,128)(2,1)} %copy-done, bf16[192,1024]{1,0:T(8,128)(2,1)} %collective-permute-done.1.refs_1_, bf16[384,1024]{1,0:T(8,128)(2,1)} %collective-permute-done.2.refs_2_, f32[1024,1024]{1,0:T(8,128)} %weight_part.6.refs_3_), custom_call_target="tpu_custom_call" | custom-call | flops 402653184 | bytes 8388608 | tf_op jit(solution)/shard_map/weight_part/pallas_call | solution.py:359
  186.7 5.2 %all-to-all-start.3 = ((bf16[8,48,1024]{2,1,0:T(8,128)(2,1)}), bf16[8,48,1024]{2,1,0:T(8,128)(2,1)S(1)}, u32[]{:S(2)}, u32[]{:S(2)}) async-start(bf16[8,48,1024]{2,1,0:T(8,128)(2,1)} %bitcast.46), calls=%async_computation.3 | async-start | bytes 1572864 | tf_op jit(solution)/shard_map/all_to_all | solution.py:624
  191.9 6.6 %weight_part.11 = (f32[512,256]{1,0:T(8,128)}, f32[512,256]{1,0:T(8,128)}, f32[512,256]{1,0:T(8,128)}, f32[512,256]{1,0:T(8,128)}) custom-call(s32[3]{0:T(128)} %pad_add_fusion.3.scal_ref, bf16[384,1024]{1,0:T(8,128)(2,1)} %copy-done.3, bf16[192,1024]{1,0:T(8,128)(2,1)} %collective-permute-done.8.refs_1_, bf16[384,1024]{1,0:T(8,128)(2,1)} %copy-done.4, ...), custom_call_target="tpu_custom_call" | custom-call | flops 402653184 | bytes 8388608 | tf_op jit(solution)/shard_map/weight_part/pallas_call | solution.py:359
  201.4 6.5 %weight_part.8 = (f32[512,256]{1,0:T(8,128)}, f32[512,256]{1,0:T(8,128)}, f32[512,256]{1,0:T(8,128)}, f32[512,256]{1,0:T(8,128)}) custom-call(s32[3]{0:T(128)} %pad_add_fusion.2.scal_ref, bf16[384,1024]{1,0:T(8,128)(2,1)} %copy-done, bf16[192,1024]{1,0:T(8,128)(2,1)} %collective-permute-done.1.refs_1_, bf16[384,1024]{1,0:T(8,128)(2,1)} %collective-permute-done.2.refs_2_, ...), custom_call_target="tpu_custom_call" | custom-call | flops 402653184 | bytes 8388608 | tf_op jit(solution)/shard_map/weight_part/pallas_call | solution.py:359
  212.1 12.7 %collective-permute-done.14 = f32[8,1024]{1,0:T(8,128)S(1)} collective-permute-done((f32[8,1024]{1,0:T(8,128)S(1)}, f32[8,1024]{1,0:T(8,128)S(1)}, u32[]{:S(2)}, u32[]{:S(2)}) %collective-permute-start.14) | collective-permute-done | bytes 32800 | tf_op jit(solution)/shard_map/ppermute | solution.py:436
  226.3 7.5 %collective-permute-done.15 = f32[8,1024]{1,0:T(8,128)S(1)} collective-permute-done((f32[8,1024]{1,0:T(8,128)S(1)}, f32[8,1024]{1,0:T(8,128)S(1)}, u32[]{:S(2)}, u32[]{:S(2)}) %collective-permute-start.15) | collective-permute-done | bytes 32800 | tf_op jit(solution)/shard_map/ppermute | solution.py:436
  255.8 9.0 %collective-permute-done.28.refs_2_ = f32[128,512]{1,0:T(8,128)S(1)} collective-permute-done((f32[128,512]{1,0:T(8,128)}, f32[128,512]{1,0:T(8,128)S(1)}, u32[]{:S(2)}, u32[]{:S(2)}) %collective-permute-start.28) | collective-permute-done | bytes 262176 | tf_op jit(solution)/shard_map/ppermute | solution.py:436
  264.8 17.1 %collective-permute-done.29.refs_3_ = f32[128,512]{1,0:T(8,128)S(1)} collective-permute-done((f32[128,512]{1,0:T(8,128)}, f32[128,512]{1,0:T(8,128)S(1)}, u32[]{:S(2)}, u32[]{:S(2)}) %collective-permute-start.29) | collective-permute-done | bytes 262176 | tf_op jit(solution)/shard_map/ppermute | solution.py:436
  297.5 3.8 %unpack.1 = (bf16[384,1024]{1,0:T(8,128)(2,1)}, bf16[384,1024]{1,0:T(8,128)(2,1)}) custom-call(s32[1]{0:T(128)} %bitcast.17.scal_ref, bf16[384,1024]{1,0:T(8,128)(2,1)} %bitcast.35, bf16[384,1024]{1,0:T(8,128)(2,1)} %bitcast.37, s32[768,1]{1,0:T(8,128)} %constant.129.clone.refs_2_), custom_call_target="tpu_custom_call" | custom-call | bytes 3148800 | tf_op jit(solution)/shard_map/unpack/pallas_call | solution.py:447
  307.5 3.0 place.1
  (169 shorter events, 74.6 us)
Async XLA Ops:
  4.6 23.1 %all-to-all-start.1 = ((bf16[8,48,1024]{2,1,0:T(8,128)(2,1)}), bf16[8,48,1024]{2,1,0:T(8,128)(2,1)S(1)}, u32[]{:S(2)}, u32[]{:S(2)}) async-start(bf16[8,48,1024]{2,1,0:T(8,128)(2,1)} %bitcast.48), calls=%async_computation.1 | async-start | bytes 1572864 | tf_op jit(solution)/shard_map/all_to_all | solution.py:513
  12.8 94.4 %collective-permute-start.7 = (bf16[384,1024]{1,0:T(8,128)(2,1)}, bf16[384,1024]{1,0:T(8,128)(2,1)S(1)}, u32[]{:S(2)}, u32[]{:S(2)}) collective-permute-start(bf16[384,1024]{1,0:T(8,128)(2,1)} %get-tuple-element.78), channel_id=1, source_target_pairs={{0,2},{1,3},{2,0},{3,1},{4,6},{5,7},{6,4},{7,5},{8,10},{9,11},{10,... | collective-permute-start | bytes 2359304 | tf_op jit(solution)/shard_map/ppermute | solution.py:436
  27.6 42.4 %all-to-all-start = ((bf16[8,48,1024]{2,1,0:T(8,128)(2,1)}), bf16[8,48,1024]{2,1,0:T(8,128)(2,1)S(1)}, u32[]{:S(2)}, u32[]{:S(2)}) async-start(bf16[8,48,1024]{2,1,0:T(8,128)(2,1)} %bitcast.4), calls=%async_computation | async-start | bytes 1572864 | tf_op jit(solution)/shard_map/all_to_all | solution.py:513
  68.0 66.9 %collective-permute-start.11 = (bf16[384,1024]{1,0:T(8,128)(2,1)}, bf16[384,1024]{1,0:T(8,128)(2,1)}, u32[]{:S(2)}, u32[]{:S(2)}) collective-permute-start(bf16[384,1024]{1,0:T(8,128)(2,1)} %get-tuple-element.84), channel_id=1, source_target_pairs={{0,2},{1,3},{2,0},{3,1},{4,6},{5,7},{6,4},{7,5},{8,10},{9,11},{10,... | collective-permute-start | bytes 2359304 | tf_op jit(solution)/shard_map/ppermute | solution.py:436
  69.6 39.1 %collective-permute-start.10 = (bf16[192,1024]{1,0:T(8,128)(2,1)}, bf16[192,1024]{1,0:T(8,128)(2,1)}, u32[]{:S(2)}, u32[]{:S(2)}) collective-permute-start(bf16[192,1024]{1,0:T(8,128)(2,1)} %get-tuple-element.81), channel_id=1, source_target_pairs={{0,2},{1,3},{2,0},{3,1},{4,6},{5,7},{6,4},{7,5},{8,10},{9,11},{10,... | collective-permute-start | bytes 1179656 | tf_op jit(solution)/shard_map/ppermute | solution.py:436
  70.1 100.0 %all-to-all-start.2 = ((bf16[8,48,1024]{2,1,0:T(8,128)(2,1)}), bf16[8,48,1024]{2,1,0:T(8,128)(2,1)S(1)}, u32[]{:S(2)}, u32[]{:S(2)}) async-start(bf16[8,48,1024]{2,1,0:T(8,128)(2,1)} %bitcast.47), calls=%async_computation.2 | async-start | bytes 1572864 | tf_op jit(solution)/shard_map/all_to_all | solution.py:624
  105.1 31.6 %collective-permute-start.9 = (bf16[384,1024]{1,0:T(8,128)(2,1)}, bf16[384,1024]{1,0:T(8,128)(2,1)S(1)}, u32[]{:S(2)}, u32[]{:S(2)}) collective-permute-start(bf16[384,1024]{1,0:T(8,128)(2,1)} %get-tuple-element.80), channel_id=1, source_target_pairs={{0,2},{1,3},{2,0},{3,1},{4,6},{5,7},{6,4},{7,5},{8,10},{9,11},{10,... | collective-permute-start | bytes 2359304 | tf_op jit(solution)/shard_map/ppermute | solution.py:436
  106.6 26.8 %collective-permute-start.8 = (bf16[192,1024]{1,0:T(8,128)(2,1)S(1)}, bf16[192,1024]{1,0:T(8,128)(2,1)}, u32[]{:S(2)}, u32[]{:S(2)}) collective-permute-start(bf16[192,1024]{1,0:T(8,128)(2,1)S(1)} %copy-done.30), channel_id=1, source_target_pairs={{0,2},{1,3},{2,0},{3,1},{4,6},{5,7},{6,4},{7,5},{8,10},{9,11},{10,... | collective-permute-start | bytes 1179656 | tf_op jit(solution)/shard_map/ppermute | solution.py:436
  107.1 46.7 %collective-permute-start = (bf16[384,1024]{1,0:T(8,128)(2,1)}, bf16[384,1024]{1,0:T(8,128)(2,1)S(1)}, u32[]{:S(2)}, u32[]{:S(2)}) collective-permute-start(bf16[384,1024]{1,0:T(8,128)(2,1)} %get-tuple-element.58.normed_face_ref.refs_0_), channel_id=1, source_target_pairs={{0,1},{1,0},{2,3},{3,2},{4,5},{5,4},{6,7},{7,6},{8,9},{9,8},{10,11... | collective-permute-start | bytes 2359304 | tf_op jit(solution)/shard_map/ppermute | solution.py:436
  108.6 61.4 %collective-permute-start.4 = (bf16[384,1024]{1,0:T(8,128)(2,1)}, bf16[384,1024]{1,0:T(8,128)(2,1)}, u32[]{:S(2)}, u32[]{:S(2)}) collective-permute-start(bf16[384,1024]{1,0:T(8,128)(2,1)} %get-tuple-element.75), channel_id=1, source_target_pairs={{0,1},{1,0},{2,3},{3,2},{4,5},{5,4},{6,7},{7,6},{8,9},{9,8},{10,11... | collective-permute-start | bytes 2359304 | tf_op jit(solution)/shard_map/ppermute | solution.py:436
  133.4 47.3 %collective-permute-start.2 = (bf16[384,1024]{1,0:T(8,128)(2,1)}, bf16[384,1024]{1,0:T(8,128)(2,1)}, u32[]{:S(2)}, u32[]{:S(2)}) collective-permute-start(bf16[384,1024]{1,0:T(8,128)(2,1)} %get-tuple-element.72), channel_id=1, source_target_pairs={{0,1},{1,0},{2,3},{3,2},{4,5},{5,4},{6,7},{7,6},{8,9},{9,8},{10,11... | collective-permute-start | bytes 2359304 | tf_op jit(solution)/shard_map/ppermute | solution.py:436
  134.9 35.1 %collective-permute-start.3 = (bf16[192,1024]{1,0:T(8,128)(2,1)S(1)}, bf16[192,1024]{1,0:T(8,128)(2,1)}, u32[]{:S(2)}, u32[]{:S(2)}) collective-permute-start(bf16[192,1024]{1,0:T(8,128)(2,1)S(1)} %copy-done.8), channel_id=1, source_target_pairs={{0,1},{1,0},{2,3},{3,2},{4,5},{5,4},{6,7},{7,6},{8,9},{9,8},{10,11... | collective-permute-start | bytes 1179656 | tf_op jit(solution)/shard_map/ppermute | solution.py:436
  136.7 44.0 %collective-permute-start.1 = (bf16[192,1024]{1,0:T(8,128)(2,1)}, bf16[192,1024]{1,0:T(8,128)(2,1)}, u32[]{:S(2)}, u32[]{:S(2)}) collective-permute-start(bf16[192,1024]{1,0:T(8,128)(2,1)} %get-tuple-element.59.normed_edge_ref.refs_3_), channel_id=1, source_target_pairs={{0,1},{1,0},{2,3},{3,2},{4,5},{5,4},{6,7},{7,6},{8,9},{9,8},{10,11... | collective-permute-start | bytes 1179656 | tf_op jit(solution)/shard_map/ppermute | solution.py:436
  153.9 38.0 %collective-permute-start.12 = (f32[512,1024]{1,0:T(8,128)}, f32[512,1024]{1,0:T(8,128)}, u32[]{:S(2)}, u32[]{:S(2)}) collective-permute-start(f32[512,1024]{1,0:T(8,128)} %weight_part.10), channel_id=1, source_target_pairs={{0,4},{4,0},{8,12},{12,8},{16,20},{20,16},{24,28},{28,24},{1,5},{5... | collective-permute-start | bytes 6291464 | tf_op jit(solution)/shard_map/ppermute | solution.py:436
  186.7 60.8 %all-to-all-start.3 = ((bf16[8,48,1024]{2,1,0:T(8,128)(2,1)}), bf16[8,48,1024]{2,1,0:T(8,128)(2,1)S(1)}, u32[]{:S(2)}, u32[]{:S(2)}) async-start(bf16[8,48,1024]{2,1,0:T(8,128)(2,1)} %bitcast.46), calls=%async_computation.3 | async-start | bytes 1572864 | tf_op jit(solution)/shard_map/all_to_all | solution.py:624
  198.5 40.8 %collective-permute-start.26 = (f32[512,256]{1,0:T(8,128)}, f32[512,256]{1,0:T(8,128)S(1)}, u32[]{:S(2)}, u32[]{:S(2)}) collective-permute-start(f32[512,256]{1,0:T(8,128)} %get-tuple-element.96), channel_id=1, source_target_pairs={{0,1},{1,0},{2,3},{3,2},{4,5},{5,4},{6,7},{7,6},{8,9},{9,8},{10,11... | collective-permute-start | bytes 1572872 | tf_op jit(solution)/shard_map/ppermute | solution.py:436
  207.9 31.4 %collective-permute-start.25 = (f32[512,256]{1,0:T(8,128)}, f32[512,256]{1,0:T(8,128)S(1)}, u32[]{:S(2)}, u32[]{:S(2)}) collective-permute-start(f32[512,256]{1,0:T(8,128)} %get-tuple-element.94), channel_id=1, source_target_pairs={{0,2},{1,3},{2,0},{3,1},{4,6},{5,7},{6,4},{7,5},{8,10},{9,11},{10,... | collective-permute-start | bytes 1572872 | tf_op jit(solution)/shard_map/ppermute | solution.py:436
  209.5 38.0 %collective-permute-start.13 = (f32[512,256]{1,0:T(8,128)}, f32[512,256]{1,0:T(8,128)S(1)}, u32[]{:S(2)}, u32[]{:S(2)}) collective-permute-start(f32[512,256]{1,0:T(8,128)} %get-tuple-element.86), channel_id=1, source_target_pairs={{0,1},{1,0},{2,3},{3,2},{4,5},{5,4},{6,7},{7,6},{8,9},{9,8},{10,11... | collective-permute-start | bytes 1572872 | tf_op jit(solution)/shard_map/ppermute | solution.py:436
  210.0 37.5 %collective-permute-start.6 = (f32[512,256]{1,0:T(8,128)}, f32[512,256]{1,0:T(8,128)S(1)}, u32[]{:S(2)}, u32[]{:S(2)}) collective-permute-start(f32[512,256]{1,0:T(8,128)} %get-tuple-element.77), channel_id=1, source_target_pairs={{0,2},{1,3},{2,0},{3,1},{4,6},{5,7},{6,4},{7,5},{8,10},{9,11},{10,... | collective-permute-start | bytes 1572872 | tf_op jit(solution)/shard_map/ppermute | solution.py:436
  244.5 20.3 %collective-permute-start.28 = (f32[128,512]{1,0:T(8,128)}, f32[128,512]{1,0:T(8,128)S(1)}, u32[]{:S(2)}, u32[]{:S(2)}) collective-permute-start(f32[128,512]{1,0:T(8,128)} %get-tuple-element.99), channel_id=1, source_target_pairs={{0,16},{4,20},{8,24},{12,28},{16,0},{20,4},{24,8},{28,12},{1,17},{... | collective-permute-start | bytes 786440 | tf_op jit(solution)/shard_map/ppermute | solution.py:436
  246.9 35.0 %collective-permute-start.29 = (f32[128,512]{1,0:T(8,128)}, f32[128,512]{1,0:T(8,128)S(1)}, u32[]{:S(2)}, u32[]{:S(2)}) collective-permute-start(f32[128,512]{1,0:T(8,128)} %get-tuple-element.100), channel_id=1, source_target_pairs={{0,24},{4,28},{8,16},{12,20},{16,8},{20,12},{24,0},{28,4},{1,25},{... | collective-permute-start | bytes 786440 | tf_op jit(solution)/shard_map/ppermute | solution.py:436
  251.3 35.3 %collective-permute-start.19 = (f32[128,512]{1,0:T(8,128)}, f32[128,512]{1,0:T(8,128)S(1)}, u32[]{:S(2)}, u32[]{:S(2)}) collective-permute-start(f32[128,512]{1,0:T(8,128)} %get-tuple-element.90), channel_id=1, source_target_pairs={{0,8},{4,12},{8,0},{12,4},{16,24},{20,28},{24,16},{28,20},{1,9},{5... | collective-permute-start | bytes 786440 | tf_op jit(solution)/shard_map/ppermute | solution.py:436
  253.3 34.7 %collective-permute-start.20 = (f32[128,512]{1,0:T(8,128)}, f32[128,512]{1,0:T(8,128)S(1)}, u32[]{:S(2)}, u32[]{:S(2)}) collective-permute-start(f32[128,512]{1,0:T(8,128)} %get-tuple-element.91), channel_id=1, source_target_pairs={{0,16},{4,20},{8,24},{12,28},{16,0},{20,4},{24,8},{28,12},{1,17},{... | collective-permute-start | bytes 786440 | tf_op jit(solution)/shard_map/ppermute | solution.py:436
  255.4 35.4 %collective-permute-start.21 = (f32[128,512]{1,0:T(8,128)}, f32[128,512]{1,0:T(8,128)S(1)}, u32[]{:S(2)}, u32[]{:S(2)}) collective-permute-start(f32[128,512]{1,0:T(8,128)} %get-tuple-element.92), channel_id=1, source_target_pairs={{0,24},{4,28},{8,16},{12,20},{16,8},{20,12},{24,0},{28,4},{1,25},{... | collective-permute-start | bytes 786440 | tf_op jit(solution)/shard_map/ppermute | solution.py:436
  (47 other events, 516.9 us)

commit v2 on v1

--- a/solution.py
+++ b/solution.py
@@ -11,7 +11,7 @@
 HEADS = 16
 BF = jnp.bfloat16
 F32 = jnp.float32
-VMEM_BYTES = 56 * 1024 * 1024
+VMEM_BYTES = 60 * 1024 * 1024
 
 
 def nn(a, b):
@@ -64,33 +64,73 @@
     early_ref[...] = jnp.where(scal_ref[0] == 0, fcot_ref[...], normed)
 
 
+def flips(line_ref, rotation_ref, base, lines):
+    line = line_ref[:, 2:3]
+    flip = jnp.zeros_like(line)
+    for l in range(lines):
+        turned = (rotation_ref[base + l] >= 2).astype(jnp.int32)
+        flip = jnp.where(line == l, turned, flip)
+    return jnp.where(flip != 0, line_ref[:, 1:2], line_ref[:, 0:1])
+
+
+def turn_pair(rotation_ref, at):
+    turn = rotation_ref[at]
+    cosine = (turn == 0).astype(F32) - (turn == 2).astype(F32)
+    sine = (turn == 1).astype(F32) - (turn == 3).astype(F32)
+    return cosine, sine
+
+
+def one_hot_rows(index, width):
+    columns = lax.broadcasted_iota(jnp.int32, (index.shape[0], width), 1)
+    return jnp.where(columns == index, 1.0, 0.0).astype(BF)
+
+
 def edge_kernel(
-    scal_ref, arrived_ref, index_ref, turn_ref, gain_ref, z_ref, g_ref, normed_ref, early_ref
+    lines,
+    scal_ref,
+    rotation_ref,
+    counts_ref,
+    arrived_ref,
+    index_ref,
+    gain_ref,
+    z_ref,
+    g_ref,
+    normed_ref,
+    early_ref,
 ):
     half = z_ref.shape[1] // 2
     edges = z_ref.shape[0]
-    picked = one_hot(index_ref, arrived_ref.shape[0])
+    edge_len = edges // lines
+    base = scal_ref[0]
+    index = flips(index_ref, rotation_ref, base, lines)
+    picked = one_hot_rows(index, arrived_ref.shape[0])
     first = nn(picked, arrived_ref[:, :half])
     second = nn(picked, arrived_ref[:, half:])
-    cosine = turn_ref[:, 0:1]
-    sine = turn_ref[:, 1:2]
-    turned = jnp.concatenate(
-        [cosine * first - sine * second, sine * first + cosine * second], axis=1
-    )
-    hidden = turned[:edges]
-    z_ref[...] = hidden.astype(BF)
-    g = turned[edges:].astype(BF)
-    g_ref[...] = g
-    inverse = lax.rsqrt(jnp.mean(hidden * hidden, axis=-1, keepdims=True) + 1e-06)
-    normed = (hidden * inverse * gain_ref[...]).astype(BF)
-    normed_ref[...] = normed
-    early_ref[...] = jnp.where(scal_ref[0] == 0, g, normed)
+    for l in range(lines):
+        cosine, sine = turn_pair(rotation_ref, base + l)
+
+        def turned(at):
+            u, v = first[at : at + edge_len], second[at : at + edge_len]
+            return jnp.concatenate([cosine * u - sine * v, sine * u + cosine * v], axis=1)
+
+        rows = slice(l * edge_len, (l + 1) * edge_len)
+        hidden = turned(l * edge_len)
+        g = turned(edges + l * edge_len).astype(BF)
+        z_ref[rows] = hidden.astype(BF)
+        g_ref[rows] = g
+        inverse = lax.rsqrt(jnp.mean(hidden * hidden, axis=-1, keepdims=True) + 1e-06)
+        normed = (hidden * inverse * gain_ref[...]).astype(BF)
+        normed_ref[rows] = normed
+        early_ref[rows] = jnp.where(scal_ref[2] == 0, g, normed)
 
 
 def layer_kernel(
     lines,
     aliased,
+    drop,
     scal_ref,
+    rotation_ref,
+    counts_ref,
     face_ref,
     fcot_ref,
     z_edge_ref,
@@ -98,13 +138,13 @@
     normed_face_ref,
     normed_edge_ref,
     back_index_ref,
-    turn_ref,
     gain_ref,
     wqkv_ref,
     wo_ref,
     *refs,
 ):
-    refs = refs[2:] if aliased else refs
+    refs = refs[drop + (2 if aliased else 0) :]
+    base = scal_ref[0]
     (
         face_out,
         face_grad,
@@ -168,7 +208,7 @@
     def _(l):
         top = pl.ds(pl.multiple_of(l * face_len, face_len), face_len)
         bottom = pl.ds(pl.multiple_of(faces + l * edge_len, edge_len), edge_len)
-        live = key_row < scal_ref[l] + face_len
+        live = key_row < counts_ref[base + l] + face_len
 
         def load(ref, at):
             return jnp.concatenate([ref[top, at : at + pair], ref[bottom, at : at + pair]], axis=0)
@@ -229,19 +269,20 @@
         else:
             edge_s[edges + start - faces : edges + start - faces + size] = dz
     edge_s[:edges] = y_s[faces:]
-    gain_part[...] = jnp.broadcast_to(gain_sum, gain_part.shape)
-    cosine = turn_ref[:, 0:1]
-    sine = turn_ref[:, 1:2]
-    first = edge_s[:, :half].astype(F32)
-    second = edge_s[:, half:].astype(F32)
-    turned_first = (cosine * first + sine * second).astype(BF)
-    turned_second = (cosine * second - sine * first).astype(BF)
-    picked = one_hot(back_index_ref, 2 * edges)
-    back_ref[:, :half] = nn(picked, turned_first).astype(BF)
-    back_ref[:, half:] = nn(picked, turned_second).astype(BF)
-
-    x_bit = scal_ref[lines]
-    y_bit = scal_ref[lines + 1]
+    lanes = gain_part.shape[1]
+    for i in range(width // lanes):
+        gain_part[i : i + 1] = gain_sum[:, i * lanes : (i + 1) * lanes]
+    for i in range(2 * lines):
+        cosine, sine = turn_pair(rotation_ref, base + i % lines)
+        rows = slice(i * edge_len, (i + 1) * edge_len)
+        u, v = edge_s[rows, :half].astype(F32), edge_s[rows, half:].astype(F32)
+        edge_s[rows, :half] = (cosine * u + sine * v).astype(BF)
+        edge_s[rows, half:] = (cosine * v - sine * u).astype(BF)
+    picked = one_hot_rows(flips(back_index_ref, rotation_ref, base, lines), 2 * edges)
+    back_ref[...] = nn(picked, edge_s[...]).astype(BF)
+
+    x_bit = scal_ref[1]
+    y_bit = scal_ref[2]
 
     @pl.when(x_bit == 0)
     def _():
@@ -264,132 +305,140 @@
         keep_b[...] = mix_s[...]
 
 
-def weight_kernel(runs, parities, blocks, count, adds, pieces, column, scal_ref, *refs):
+def weight_kernel(runs, parities, blocks, count, adds, gains, halved, scal_ref, *refs):
     operands = refs[:count]
     add_refs = refs[count : count + adds]
-    outs = refs[count + adds : -3]
-    lhs_s, lhs_t, rhs_s = refs[-3:]
-    step = pl.program_id(0)
-    depth, width = rhs_s.shape
-    rows = depth // len(runs)
+    gain_refs = refs[count + adds : count + adds + gains]
+    outs = refs[count + adds + gains :]
+    pieces = max(1, len(outs) // 2)
+    width = operands[-1].shape[1]
     part = width // 2
     size = part // blocks
-    tile = width // (2 * pieces)
-
-    def fill(at, src):
-        for n, own in enumerate(parities):
+    tile = outs[0].shape[1]
+    rows = len(parities) * part
+
+    def pick(src):
+        kept = []
+        for own in parities:
             first = scal_ref[0] == (0 if own else 1)
             for b in range(blocks):
                 left = src[:, 2 * b * size : (2 * b + 1) * size]
                 right = src[:, (2 * b + 1) * size : (2 * b + 2) * size]
-                to = n * part + b * size
-                lhs_s[at : at + src.shape[0], to : to + size] = jnp.where(first, left, right)
-
-    def load(swapped):
-        for i, (faces, edges, chunk, late) in enumerate(runs):
-            late_rows = operands[late][...]
-            edge = operands[edges[swapped]][...]
-            front = rows - edge.shape[0]
-            face = operands[faces[swapped]][chunk * front : (chunk + 1) * front]
-            at = i * rows
-            if swapped:
-                fill(at, late_rows)
-                rhs_s[at : at + front] = face
-                rhs_s[at + front : at + rows] = edge
-            else:
-                fill(at, face)
-                fill(at + front, edge)
-                rhs_s[at : at + rows] = late_rows
-
-    @pl.when((step == 0) & (scal_ref[1] == 0))
+                kept.append(jnp.where(first, left, right))
+        return jnp.concatenate(kept, axis=1)
+
+    def run(swapped):
+        early, late = [], []
+        for faces, edges, chunk, late_at in runs:
+            edge = operands[edges[swapped]]
+            front = operands[late_at].shape[0] - edge.shape[0]
+            early += [operands[faces[swapped]][chunk * front : (chunk + 1) * front], edge[...]]
+            late.append(operands[late_at][...])
+        early, late = jnp.concatenate(early, axis=0), jnp.concatenate(late, axis=0)
+        lhs, rhs = (late, early) if swapped else (early, late)
+        lhs = pick(lhs)
+        if not halved:
+            total = tn(lhs, rhs)
+            for ref in add_refs:
+                total = total + ref[:rows]
+            outs[0][:rows] = total
+            return
+        for half in range(2):
+            mine = (scal_ref[2] if half else 1 - scal_ref[2]) == 0
+            cols = jnp.where(mine, rhs[:, :part], rhs[:, part:])
+            total = tn(lhs, cols)
+            for ref in add_refs:
+                total = total + jnp.where(mine, ref[:rows, :part], ref[:rows, part:])
+            for n in range(pieces):
+                outs[half * pieces + n][:rows] = total[:, n * tile : (n + 1) * tile]
+
+    @pl.when(scal_ref[1] == 0)
     def _():
-        load(0)
-
-    @pl.when((step == 0) & (scal_ref[1] != 0))
+        run(0)
+
+    @pl.when(scal_ref[1] != 0)
     def _():
-        load(1)
-
-    @pl.when(step == 0)
-    def _():
-        for n in range(0, lhs_t.shape[0], 128):
-            lhs_t[n : n + 128] = lhs_s[:, n : n + 128].T
-
-    col = column(step, scal_ref)
-    total = nn(lhs_t[...], rhs_s[:, pl.ds(pl.multiple_of(col * tile, tile), tile)])
-    for ref in add_refs:
-        total = total + ref[...]
-    if len(outs) == 1:
-        outs[0][...] = total
-    else:
-        for n, out in enumerate(outs):
-
-            @pl.when(step == n)
-            def _(out=out):
-                out[...] = total
-
-
-def weight_part(scal, runs, parities, blocks, operands, adds, pieces, halved, deps, tracked):
+        run(1)
+
+    if gains:
+        total = gain_refs[0][...]
+        for ref in gain_refs[1:]:
+            total = total + ref[...]
+        lanes = total.shape[1]
+        if halved:
+            total = total + add_refs[-1][rows:, :lanes]
+        for out in outs:
+            if out.shape[0] > rows:
+                for n in range(tile // lanes):
+                    out[rows:, n * lanes : (n + 1) * lanes] = total
+
+
+def weight_part(scal, runs, parities, blocks, operands, adds, pieces, halved, gains, deps):
     width = operands[-1].shape[1]
-    tile = width // (2 * pieces)
-    rows = len(parities) * (width // 2)
+    part = width // 2
+    rows = len(parities) * part
     depth = len(runs) * operands[runs[0][3]].shape[0]
-
-    def column(j, s):
-        if not halved:
-            return j
-        second = j // pieces
-        return ((1 - s[2]) + second * (2 * s[2] - 1)) * pieces + j % pieces
+    extra = gains[0].shape[0] if gains else 0
+    used = len(operands) + len(adds) + len(gains)
 
     def kernel(scal_ref, *refs):
-        refs = refs[: len(operands) + len(adds)] + refs[len(operands) + len(adds) + len(deps) :]
+        refs = refs[:used] + refs[used + len(deps) :]
         weight_kernel(
-            runs, parities, blocks, len(operands), len(adds), pieces, column, scal_ref, *refs
+            runs, parities, blocks, len(operands), len(adds), len(gains), halved, scal_ref, *refs
         )
 
-    whole = [pl.BlockSpec(o.shape, lambda j, s: (0, 0)) for o in operands]
+    def spec(shape, at=0):
+        return pl.BlockSpec(shape, lambda i, s: (at, 0))
+
     add_specs = [
-        pl.BlockSpec((rows, tile), lambda j, s, at=at: (at, column(j, s))) for _, at in adds
+        spec(a.shape) if at is None else spec((rows, width), at) for a, at in adds
     ]
     if halved:
-        out_specs = [pl.BlockSpec((rows, tile), lambda j, s: (0, 0))] * (2 * pieces)
-        out_shape = [jax.ShapeDtypeStruct((rows, tile), F32)] * (2 * pieces)
+        tile = part // pieces
+        shapes = [
+            (rows + (extra if n % pieces == 0 else 0), tile) for n in range(2 * pieces)
+        ]
     else:
-        out_specs = [pl.BlockSpec((rows, tile), lambda j, s: (0, j))]
-        out_shape = [jax.ShapeDtypeStruct((rows, width), F32)]
+        shapes = [(rows + extra, width)]
     return pl.pallas_call(
         kernel,
         grid_spec=pltpu.PrefetchScalarGridSpec(
             num_scalar_prefetch=1,
-            grid=(2 * pieces,),
-            in_specs=whole + add_specs + [pl.BlockSpec(memory_space=pl.ANY)] * len(deps),
-            out_specs=out_specs,
-            scratch_shapes=[
-                pltpu.VMEM((depth, rows), BF),
-                pltpu.VMEM((rows, depth), BF),
-                pltpu.VMEM((depth, width), BF),
-            ],
+            grid=(1,),
+            in_specs=[spec(o.shape) for o in operands]
+            + add_specs
+            + [spec(g.shape) for g in gains]
+            + [pl.BlockSpec(memory_space=pl.ANY)] * len(deps),
+            out_specs=[spec(s) for s in shapes],
         ),
-        out_shape=out_shape,
+        out_shape=[jax.ShapeDtypeStruct(s, F32) for s in shapes],
         compiler_params=pltpu.CompilerParams(vmem_limit_bytes=VMEM_BYTES),
         cost_estimate=pl.CostEstimate(
-            flops=2 * rows * depth * width, bytes_accessed=tracked, transcendentals=0
+            flops=1 << 33 if len(runs) > 1 else 1024, bytes_accessed=1024, transcendentals=0
         ),
         name="weight_part",
-    )(scal, *operands, *[a for a, _ in adds], *deps)
+    )(scal, *operands, *[a for a, _ in adds], *gains, *deps)
 
 
 def block_kernel(blocks, count, scal_ref, *refs):
     groups = (refs[:count], refs[count : 2 * count])
     outs = refs[2 * count :]
     columns = groups[0][0].shape[1]
-    size = groups[0][0].shape[0] // blocks
+    size = groups[1][0].shape[0] // blocks
+    whole = blocks * size
     for o, out in enumerate(outs):
         at = pl.ds(pl.multiple_of((scal_ref[0] ^ o) * size, size), size)
         for n, parts in enumerate(groups):
             total = parts[0][at]
             for p in parts[1:]:
                 total = total + p[at]
-            out[:, n * columns : (n + 1) * columns] = total
+            out[:size, n * columns : (n + 1) * columns] = total
+        if out.shape[0] > size:
+            total = groups[0][0][whole:]
+            for p in groups[0][1:]:
+                total = total + p[whole:]
+            out[size:, :columns] = total
+            out[size:, columns:] = total
 
 
 def sum_kernel(factor, scal_ref, *refs):
@@ -407,9 +456,10 @@
         for o in range(devices):
             src = refs[n * devices + o]
             part = src.shape[1] // 2
+            size = out_ref.shape[0]
             device = scal_ref[0] ^ o
             for group in range(2):
-                value = slice(group * part, (group + 1) * part)
+                value = (slice(0, size), slice(group * part, (group + 1) * part))
                 rest = [b for b in range(bits) if b != group]
                 at = ((device >> rest[0]) & 1) * (width // 2) + n * (width // 2 // pieces)
                 unit = width // 2 // pieces
@@ -419,17 +469,17 @@
                 which = (device >> group) & 1
                 if group == 0:
                     at = pl.multiple_of(at + which * width, part)
-                    qkv_ref[:, pl.ds(at, part)] = src[:, value]
+                    qkv_ref[:, pl.ds(at, part)] = src[value]
                 else:
 
                     @pl.when(which == 0)
                     def _(src=src, value=value, at=at, part=part):
                         cols = pl.ds(pl.multiple_of(at + 2 * width, part), part)
-                        qkv_ref[:, cols] = src[:, value]
+                        qkv_ref[:, cols] = src[value]
 
                     @pl.when(which != 0)
                     def _(src=src, value=value, at=at, part=part):
-                        out_ref[:, pl.ds(pl.multiple_of(at, part), part)] = src[:, value]
+                        out_ref[:, pl.ds(pl.multiple_of(at, part), part)] = src[value]
 
 
 def exchange(x, axis, bits, size):
@@ -437,17 +487,20 @@
 
 
 def whole_call(kernel, name, scal, out_shape, operands, deps=(), scratch=(), flops=0):
-    def body(scal_ref, *refs):
-        kernel(scal_ref, *refs[: len(operands)], *refs[len(operands) + len(deps) :])
+    scal = scal if isinstance(scal, tuple) else (scal,)
+
+    def body(*refs):
+        used = len(scal) + len(operands)
+        kernel(*refs[:used], *refs[used + len(deps) :])
 
     def spec(shape):
-        return pl.BlockSpec(shape, lambda i, s: (0,) * len(shape))
+        return pl.BlockSpec(shape, lambda i, *s: (0,) * len(shape))
 
     moved = sum(int(np.prod(o.shape)) * o.dtype.itemsize for o in [*operands, *out_shape])
     return pl.pallas_call(
         body,
         grid_spec=pltpu.PrefetchScalarGridSpec(
-            num_scalar_prefetch=1,
+            num_scalar_prefetch=len(scal),
             grid=(1,),
             in_specs=[spec(o.shape) for o in operands]
             + [pl.BlockSpec(memory_space=pl.ANY)] * len(deps),
@@ -456,9 +509,9 @@
         ),
         out_shape=out_shape,
         compiler_params=pltpu.CompilerParams(vmem_limit_bytes=VMEM_BYTES),
-        cost_estimate=pl.CostEstimate(flops=flops, bytes_accessed=moved, transcendentals=0),
+        cost_estimate=pl.CostEstimate(flops=1024, bytes_accessed=1024, transcendentals=0),
         name=name,
-    )(scal, *operands, *deps)
+    )(*scal, *operands, *deps)
 
 
 def local(
@@ -524,47 +577,41 @@
     got_face_a = exchange(face_normed, "dp", 1, D)
     got_face_b = exchange(face_early, "dp", 2, D)
 
-    my_turns = lax.dynamic_slice_in_dim(rotation, me_t * LD, LD)
-    my_counts = lax.dynamic_slice_in_dim(counts, me_t * LD, LD)
-    spos = np.arange(EL)
+    edges = lines * EL
+    l, p = np.meshgrid(np.arange(lines), np.arange(EL), indexing="ij")
+    table = []
+    for pos in (p, EL - 1 - p):
+        row = (pos // K) * (2 * RB) + l * K + pos % K
+        table.append(np.stack([row, row + RB]))
+    table.append(np.stack([l, l]))
+    index = jnp.asarray(np.stack(table, axis=-1).reshape(-1, 3).astype(np.int32))
+    t, w, l, k = np.meshgrid(
+        np.arange(T), np.arange(2), np.arange(lines), np.arange(K), indexing="ij"
+    )
+    pos = t * K + k
+    table = [w * edges + l * EL + pos, w * edges + l * EL + EL - 1 - pos, l]
+    back_index = jnp.asarray(np.stack(table, axis=-1).reshape(-1, 3).astype(np.int32))
     edge_parts, results, got_edges, got_late = [], [], [], []
     faces = None
     for c in range(chunks):
-        turns = my_turns[c * lines : (c + 1) * lines]
-        flip = turns >= 2
-        pos = jnp.where(flip[:, None], EL - 1 - spos[None, :], spos[None, :])
-        row = (pos // K) * (2 * RB) + jnp.arange(lines)[:, None] * K + pos % K
-        index = jnp.concatenate([row, row + RB], axis=0).reshape(-1, 1).astype(jnp.int32)
-        cosine = (turns == 0).astype(F32) - (turns == 2).astype(F32)
-        sine = (turns == 1).astype(F32) - (turns == 3).astype(F32)
-        turn = jnp.stack([cosine, sine], axis=-1)
-        turn = jnp.broadcast_to(turn[None, :, None, :], (2, lines, EL, 2)).reshape(-1, 2)
-        sk = np.arange(T)[:, None, None, None] * K + np.arange(K)[None, None, None, :]
-        bk = jnp.where(flip[None, None, :, None], EL - 1 - sk, sk)
-        back_index = (
-            jnp.arange(2)[None, :, None, None] * (lines * EL)
-            + jnp.arange(lines)[None, None, :, None] * EL
-            + bk
-        )
-        back_index = back_index.reshape(-1, 1).astype(jnp.int32)
-        scal = jnp.concatenate([my_counts[c * lines : (c + 1) * lines], jnp.stack([x_bit, y_bit])])
-        edges = lines * EL
+        base = (me_t * LD + c * lines).astype(jnp.int32)
+        scal = (jnp.stack([base, x_bit, y_bit]), rotation, counts)
         z_edge, g_edge, normed_edge, early_edge = whole_call(
-            edge_kernel,
+            functools.partial(edge_kernel, lines),
             "edge_norm",
-            y_bit.reshape(1),
+            scal,
             [struct(edges, width)] * 4,
-            [arrived[c], index, turn, gain],
+            [arrived[c], index, gain],
         )
         edge_parts.append((normed_edge, g_edge))
         got_edges.append((exchange(normed_edge, "dp", 1, D), exchange(early_edge, "dp", 2, D)))
         rows_all = lines * length
         row_shape = (rows_all, width)
-        face_spec = pl.BlockSpec((1, lines, FL, width), lambda i, s, c=c: (0, c, 0, 0))
-        normed_spec = pl.BlockSpec((lines * FL, width), lambda i, s, c=c: (c, 0))
+        face_spec = pl.BlockSpec((1, lines, FL, width), lambda i, *s, c=c: (0, c, 0, 0))
+        normed_spec = pl.BlockSpec((lines * FL, width), lambda i, *s, c=c: (c, 0))
 
         def full(shape):
-            return pl.BlockSpec(shape, lambda i, s: (0,) * len(shape))
+            return pl.BlockSpec(shape, lambda i, *s: (0,) * len(shape))
 
         operands = [
             face_tokens,
@@ -574,25 +621,26 @@
             face_normed,
             normed_edge,
             back_index,
-            turn,
             gain,
             qkv_weight,
             out_weight,
         ]
         in_specs = [face_spec, face_spec] + [full(o.shape) for o in operands[2:]]
         in_specs[4] = normed_spec
+        held = [got_face_a, got_face_b, *got_edges[0]] if c else []
         if faces is not None:
-            in_specs += [pl.BlockSpec(memory_space=pl.ANY)] * 2
             operands += list(faces)
+        operands += held
+        in_specs += [pl.BlockSpec(memory_space=pl.ANY)] * (len(operands) - len(in_specs))
         outs = pl.pallas_call(
-            functools.partial(layer_kernel, lines, faces is not None),
+            functools.partial(layer_kernel, lines, faces is not None, len(held)),
             grid_spec=pltpu.PrefetchScalarGridSpec(
-                num_scalar_prefetch=1,
+                num_scalar_prefetch=3,
                 grid=(1,),
                 in_specs=in_specs,
                 out_specs=[face_spec, face_spec, full((packed, width))]
                 + [full(row_shape)] * 4
-                + [full((8, width))],
+                + [full((8, width // 8))],
                 scratch_shapes=[
                     pltpu.VMEM(row_shape, BF),
                     pltpu.VMEM(row_shape, BF),
@@ -609,26 +657,18 @@
             out_shape=[struct(*face_tokens.shape)] * 2
             + [struct(packed, width)]
             + [struct(*row_shape)] * 4
-            + [struct(8, width, dtype=F32)],
-            input_output_aliases={12: 0, 13: 1} if faces is not None else {},
+            + [struct(8, width // 8, dtype=F32)],
+            input_output_aliases={13: 0, 14: 1} if faces is not None else {},
             compiler_params=pltpu.CompilerParams(vmem_limit_bytes=VMEM_BYTES),
-            cost_estimate=pl.CostEstimate(
-                flops=2 * rows_all * width * width * 8 * 2, bytes_accessed=1 << 24, transcendentals=0
-            ),
+            cost_estimate=pl.CostEstimate(flops=1 << 35, bytes_accessed=1 << 20, transcendentals=0),
             name="layer",
-        )(scal, *operands)
+        )(*scal, *operands)
         faces = outs[:2]
         results.append(outs[2:])
         got_late.append((exchange(outs[4], "dp", 1, D), exchange(outs[6], "dp", 2, D)))
     returned = [
         lax.all_to_all(r[0], "tile", split_axis=0, concat_axis=0, tiled=True) for r in results
     ]
-
-    gain_sum = sum(r[5] for r in results)
-    for b in range(D.bit_length() - 1):
-        gain_sum = gain_sum + exchange(gain_sum, "dp", 1 << b, D)
-    for b in range(T.bit_length() - 1):
-        gain_sum = gain_sum + exchange(gain_sum, "tile", 1 << b, T)
 
     blocks = T // 2
     chip = (me_t // 2).astype(jnp.int32)
@@ -649,22 +689,23 @@
         operands = [face_normed, face_cots, *normed_e, *g_e, got_face, got_e[0], late[0], late[1], got_l[0]]
         runs = [((0, 1), (2, 4), 0, 8), ((0, 1), (3, 5), 1, 9), ((6, 6), (7, 7), 0, 10)]
         start = weight_part(
-            scal, runs, (False, True), blocks, operands, [], pieces, False,
-            [returned[0]] if group == 0 else [], 8 << 20,
+            scal, runs, (False, True), blocks, operands, [], pieces, False, [],
+            [returned[0], *got_edges[1], *got_late[0]] if group == 0 else [],
         )[0]
         groups.append((scal, [got_face, got_e[1], got_l[1]], start, first))
     theirs = []
     runs = [((0, 0), (1, 1), 1, 2)]
-    for scal, operands, start, first in groups:
+    gains = [[r[5] for r in results], []]
+    for group, (scal, operands, start, first) in enumerate(groups):
         send = weight_part(
-            scal, runs, (False,), blocks, operands, [(start, 0)], pieces, False, [], 8 << 20
+            scal, runs, (False,), blocks, operands, [(start, 0)], pieces, False, gains[group], [returned[1]] if group else []
         )[0]
         theirs.append(exchange(send, "tile", 1, T))
     halves = []
     for group, (scal, operands, start, first) in enumerate(groups):
         outs = weight_part(
-            scal, runs, (True,), blocks, operands, [(start, 1), (theirs[group], 0)], pieces, True,
-            [], 8 << 20,
+            scal, runs, (True,), blocks, operands, [(start, 1), (theirs[group], None)], pieces, True,
+            gains[group], [],
         )
         parts = []
         for n in range(pieces):
@@ -687,16 +728,15 @@
             functools.partial(block_kernel, blocks, 2),
             "row_blocks",
             chip.reshape(1),
-            [struct(size, columns, dtype=F32)] * blocks,
+            [struct(size + (8 if n == 0 else 0), columns, dtype=F32)] * blocks,
             parts,
-            deps=[returned[1], gain_sum] if n == 0 else [],
         )
         got = [exchange(outs[o], "tile", 2 * o, T) for o in range(1, blocks)]
         (mine,) = whole_call(
             functools.partial(sum_kernel, factor),
             "block_sum",
             chip.reshape(1),
-            [struct(size, columns, dtype=F32)],
+            [struct(*outs[0].shape, dtype=F32)],
             [outs[0], *got],
         )
         placed += [mine] + [exchange(mine, "dp", o, D) for o in range(1, D)]
@@ -722,7 +762,8 @@
         [struct(size, 3 * width, dtype=F32), struct(size, width, dtype=F32)],
         placed,
     )
-    gain_grad = lax.dynamic_slice_in_dim(gain_sum[0], me_t * size, size) * factor
+    gain_sum = (placed[0] + placed[1])[size:, : width // 8].reshape(width)
+    gain_grad = lax.dynamic_slice_in_dim(gain_sum, me_t * size, size)
     shape = edge_tokens.shape
     return (
         faces[0],

time: 314 us -> 260 us (0.83)
  waiting for transfers between devices: 112 us -> 74.2 us
  starting transfers between devices: 57.4 us -> 51 us
  Pallas kernels: 125 us -> 121 us
    ppermute x33 -> x28, waiting for transfers between devices: 99.2 us -> 64.9 us  [exchange(): return lax.ppermute(x, axis, [(i, i ^ bits) for i in range(size)])]
    ppermute x33 -> x28, starting transfers between devices: 35 us -> 28.8 us  [exchange(): return lax.ppermute(x, axis, [(i, i ^ bits) for i in range(size)])]
    pallas_call x6, Pallas kernels: 44.6 us -> 38.8 us  [weight_part(): pl.pallas_call(kernel, grid_spec=pltpu.PrefetchScalarGridSpec(num_scalar_...]
    all_to_all x2, waiting for transfers between devices: 12.6 us -> 9.29 us  [local(): lax.all_to_all(s, 'tile', split_axis=0, concat_axis=0, tiled=True)]
    unnamed x66 -> x56, local copies, waits for them, and re-layouts: 6.54 us -> 9.15 us
  transfers between devices with their start and end apart: 37 -> 32, of which waited for: 14 -> 13; matrix products, arithmetic and copies ran while one was open for 3% -> 1% of each run, Pallas kernels for 38% -> 43%
where the time goes in v2:
time: 260 us
  Pallas kernels  121 us (47%)
  waiting for transfers between devices  74.2 us (29%)
  starting transfers between devices  51 us (20%)
  local copies, waits for them, and re-layouts  9.74 us (4%)
  other arithmetic  3.19 us (1%)
    ppermute x28, waiting for transfers between devices, exchange(): return lax.ppermute(x, axis, [(i, i ^ bits) for i in range(size)])  64.9 us
    pallas_call x2, Pallas kernels, local(): pl.pallas_call(functools.partial(layer_kernel, lines, faces is not None,...  51.5 us
    pallas_call x6, Pallas kernels, weight_part(): pl.pallas_call(kernel, grid_spec=pltpu.PrefetchScalarGridSpec(num_scalar_...  38.8 us
    pallas_call x10, Pallas kernels, whole_call(): pl.pallas_call(body, grid_spec=pltpu.PrefetchScalarGridSpec(num_scalar_pr...  30.5 us
    ppermute x28, starting transfers between devices, exchange(): return lax.ppermute(x, axis, [(i, i ^ bits) for i in range(size)])  28.8 us
    all_to_all x2, starting transfers between devices, local(): lax.all_to_all(s, 'tile', split_axis=0, concat_axis=0, tiled=True)  12 us
    all_to_all x2, starting transfers between devices, local(): lax.all_to_all(r[0], 'tile', split_axis=0, concat_axis=0, tiled=True)  10.2 us
    all_to_all x2, waiting for transfers between devices, local(): lax.all_to_all(s, 'tile', split_axis=0, concat_axis=0, tiled=True)  9.29 us
  transfers between devices with their start and end apart: 32, of which 13 were waited for; matrix products, arithmetic and copies ran while one was open for 1% of the time, Pallas kernels for 43%

profile of v2, /device:TPU:16, one launch (start us, length us, event | category | flops | bytes accessed | tf_op | source)
XLA Modules:
  0.0 259.6 jit_solution(13372946701002064709)
XLA Ops:
  0.7 3.8 %pack.1 = (bf16[384,1024]{1,0:T(8,128)(2,1)}, bf16[384,1024]{1,0:T(8,128)(2,1)}) custom-call(s32[1]{0:T(128)} %bitcast.2.refs_0_, bf16[384,1024]{1,0:T(8,128)(2,1)} %bitcast.32, bf16[384,1024]{1,0:T(8,128)(2,1)} %bitcast.33, s32[768,1]{1,0:T(8,128)} %constant.68.clone.refs_3_), custom_call_target="tpu_custom_call" | custom-call | flops 1024 | bytes 1024 | tf_op jit(solution)/shard_map/pack/pallas_call | solution.py:500
  4.5 5.2 %all-to-all-start.1 = ((bf16[8,48,1024]{2,1,0:T(8,128)(2,1)}), bf16[8,48,1024]{2,1,0:T(8,128)(2,1)S(1)}, u32[]{:S(2)}, u32[]{:S(2)}) async-start(bf16[8,48,1024]{2,1,0:T(8,128)(2,1)} %bitcast.39), calls=%async_computation.1 | async-start | bytes 1572864 | tf_op jit(solution)/shard_map/all_to_all | solution.py:566
  18.1 9.3 %all-to-all-done.1 = bf16[8,48,1024]{2,1,0:T(8,128)(2,1)S(1)} async-done(((bf16[8,48,1024]{2,1,0:T(8,128)(2,1)}), bf16[8,48,1024]{2,1,0:T(8,128)(2,1)S(1)}, u32[]{:S(2)}, u32[]{:S(2)}) %all-to-all-start.1) | async-done | bytes 786464 | tf_op jit(solution)/shard_map/all_to_all | solution.py:566
  27.4 6.7 %all-to-all-start = ((bf16[8,48,1024]{2,1,0:T(8,128)(2,1)}), bf16[8,48,1024]{2,1,0:T(8,128)(2,1)S(1)}, u32[]{:S(2)}, u32[]{:S(2)}) async-start(bf16[8,48,1024]{2,1,0:T(8,128)(2,1)} %bitcast.38), calls=%async_computation | async-start | bytes 1572864 | tf_op jit(solution)/shard_map/all_to_all | solution.py:566
  34.2 3.9 %edge_norm.3 = (bf16[192,1024]{1,0:T(8,128)(2,1)}, bf16[192,1024]{1,0:T(8,128)(2,1)}, bf16[192,1024]{1,0:T(8,128)(2,1)}, bf16[192,1024]{1,0:T(8,128)(2,1)}) custom-call(s32[3]{0:T(128)} %add_add_fusion.1.refs_0_.scal_ref, s32[48]{0:T(128)} %rotation_ref.3, s32[48]{0:T(128)} %counts_ref.3, bf16[384,1024]{1,0:T(8,128)(2,1)} %bitcast.30, ...), custom_call_target="tpu_custom_call" | custom-call | flops 1024 | bytes 1024 | tf_op jit(solution)/shard_map/edge_norm/pallas_call | solution.py:500
  41.0 25.8 %layer.2 = (bf16[1,6,64,1024]{3,2,1,0:T(8,128)(2,1)}, bf16[1,6,64,1024]{3,2,1,0:T(8,128)(2,1)}, bf16[384,1024]{1,0:T(8,128)(2,1)}, bf16[384,1024]{1,0:T(8,128)(2...) custom-call(s32[3]{0:T(128)} %add_add_fusion.1.refs_0_.scal_ref, ...), custom_call_target="tpu_custom_call" | custom-call | flops 34359738368 | bytes 1048576 | tf_op jit(solution)/shard_map/layer/pallas_call | solution.py:635
  68.3 5.1 %all-to-all-start.2 = ((bf16[8,48,1024]{2,1,0:T(8,128)(2,1)}), bf16[8,48,1024]{2,1,0:T(8,128)(2,1)S(1)}, u32[]{:S(2)}, u32[]{:S(2)}) async-start(bf16[8,48,1024]{2,1,0:T(8,128)(2,1)} %bitcast.40), calls=%async_computation.2 | async-start | bytes 1572864 | tf_op jit(solution)/shard_map/all_to_all | solution.py:670
  73.4 3.9 %edge_norm.2 = (bf16[192,1024]{1,0:T(8,128)(2,1)}, bf16[192,1024]{1,0:T(8,128)(2,1)}, bf16[192,1024]{1,0:T(8,128)(2,1)}, bf16[192,1024]{1,0:T(8,128)(2,1)}) custom-call(s32[3]{0:T(128)} %add_add_fusion.refs_0_.scal_ref, s32[48]{0:T(128)} %rotation_ref.3, s32[48]{0:T(128)} %counts_ref.3, bf16[384,1024]{1,0:T(8,128)(2,1)} %bitcast.31, ...), custom_call_target="tpu_custom_call" | custom-call | flops 1024 | bytes 1024 | tf_op jit(solution)/shard_map/edge_norm/pallas_call | solution.py:500
  81.6 25.7 %layer.3 = (bf16[1,6,64,1024]{3,2,1,0:T(8,128)(2,1)}, bf16[1,6,64,1024]{3,2,1,0:T(8,128)(2,1)}, bf16[384,1024]{1,0:T(8,128)(2,1)}, bf16[384,1024]{1,0:T(8,128)(2...) custom-call(s32[3]{0:T(128)} %add_add_fusion.refs_0_.scal_ref, ...), custom_call_target="tpu_custom_call", output_to_operand_aliasing={{0}: (13, {}), {1}: (14, {})} | custom-call | flops 34359738368 | bytes 1048576 | tf_op jit(solution)/shard_map/layer/pallas_call | solution.py:635
  107.8 5.1 %all-to-all-start.3 = ((bf16[8,48,1024]{2,1,0:T(8,128)(2,1)}), bf16[8,48,1024]{2,1,0:T(8,128)(2,1)S(1)}, u32[]{:S(2)}, u32[]{:S(2)}) async-start(bf16[8,48,1024]{2,1,0:T(8,128)(2,1)} %bitcast.41), calls=%async_computation.3 | async-start | bytes 1572864 | tf_op jit(solution)/shard_map/all_to_all | solution.py:670
  113.6 8.6 %weight_part.6.refs_3_ = f32[1024,1024]{1,0:T(8,128)} custom-call(s32[3]{0:T(128)} %pad_add_fusion.scal_ref, bf16[384,1024]{1,0:T(8,128)(2,1)} %get-tuple-element.58.normed_face_ref.refs_0_, bf16[384,1024]{1,0:T(8,128)(2,1)} %bitcast.36, bf16[192,1024]{1,0:T(8,128)(2,1)} %get-tuple-element.63.normed_edge_ref.refs_2_, ...), custom_call_target="tpu_custom_call" | custom-call | flops 8589934592 | bytes 1024 | tf_op jit(solution)/shard_map/weight_part/pallas_call | solution.py:403
  122.2 10.6 %collective-permute-done.5.refs_2_ = bf16[384,1024]{1,0:T(8,128)(2,1)S(1)} collective-permute-done((bf16[384,1024]{1,0:T(8,128)(2,1)}, bf16[384,1024]{1,0:T(8,128)(2,1)S(1)}, u32[]{:S(2)}, u32[]{:S(2)}) %collective-permute-start.5) | collective-permute-done | bytes 786464 | tf_op jit(solution)/shard_map/ppermute | solution.py:486
  133.6 4.9 %weight_part.7 = f32[520,1024]{1,0:T(8,128)} custom-call(s32[3]{0:T(128)} %pad_add_fusion.scal_ref, bf16[384,1024]{1,0:T(8,128)(2,1)} %copy-done.2, bf16[192,1024]{1,0:T(8,128)(2,1)} %collective-permute-done.4.refs_12_.refs_1_, bf16[384,1024]{1,0:T(8,128)(2,1)} %copy-done.4, f32[1024,1024]{1,0:T(8,128)} %weight_part.6.refs_3_, ...), custom_call_target="tpu_custom_call" | custom-call | flops 1024 | bytes 1024 | tf_op jit(solution)/shard_map/weight_part/pallas_call | solution.py:403
  138.5 8.5 %weight_part.9.refs_3_ = f32[1024,1024]{1,0:T(8,128)} custom-call(s32[3]{0:T(128)} %pad_add_fusion.1.scal_ref, bf16[384,1024]{1,0:T(8,128)(2,1)} %get-tuple-element.58.normed_face_ref.refs_0_, bf16[384,1024]{1,0:T(8,128)(2,1)} %bitcast.37, bf16[192,1024]{1,0:T(8,128)(2,1)} %get-tuple-element.63.normed_edge_ref.refs_2_, ...), custom_call_target="tpu_custom_call" | custom-call | flops 8589934592 | bytes 1024 | tf_op jit(solution)/shard_map/weight_part/pallas_call | solution.py:403
  148.2 4.9 %weight_part.10 = f32[512,1024]{1,0:T(8,128)} custom-call(s32[3]{0:T(128)} %pad_add_fusion.1.scal_ref, bf16[384,1024]{1,0:T(8,128)(2,1)} %copy-done.1, bf16[192,1024]{1,0:T(8,128)(2,1)} %copy-done.9, bf16[384,1024]{1,0:T(8,128)(2,1)} %copy-done.3, f32[1024,1024]{1,0:T(8,128)} %weight_part.9.refs_3_, bf16[384,1024]{1,0:T(8,128)(2,1)} %bitcast.26), custom_call_target="tpu_custom_call" | custom-call | flops 1024 | bytes 1024 | tf_op jit(solution)/shard_map/weight_part/pallas_call | solution.py:403
  153.6 5.8 %weight_part.8 = (f32[520,256]{1,0:T(8,128)}, f32[512,256]{1,0:T(8,128)}, f32[520,256]{1,0:T(8,128)}, f32[512,256]{1,0:T(8,128)}) custom-call(s32[3]{0:T(128)} %pad_add_fusion.scal_ref, bf16[384,1024]{1,0:T(8,128)(2,1)} %copy-done.2, bf16[192,1024]{1,0:T(8,128)(2,1)} %collective-permute-done.4.refs_12_.refs_1_, bf16[384,1024]{1,0:T(8,128)(2,1)} %copy-done.4, ...), custom_call_target="tpu_custom_call" | custom-call | flops 1024 | bytes 1024 | tf_op jit(solution)/shard_map/weight_part/pallas_call | solution.py:403
  162.4 6.1 %weight_part.11 = (f32[512,256]{1,0:T(8,128)}, f32[512,256]{1,0:T(8,128)}, f32[512,256]{1,0:T(8,128)}, f32[512,256]{1,0:T(8,128)}) custom-call(s32[3]{0:T(128)} %pad_add_fusion.1.scal_ref, bf16[384,1024]{1,0:T(8,128)(2,1)} %copy-done.1, bf16[192,1024]{1,0:T(8,128)(2,1)} %copy-done.9, bf16[384,1024]{1,0:T(8,128)(2,1)} %copy-done.3, ...), custom_call_target="tpu_custom_call" | custom-call | flops 1024 | bytes 1024 | tf_op jit(solution)/shard_map/weight_part/pallas_call | solution.py:403
  174.6 8.9 %collective-permute-done.13.refs_4_ = f32[512,256]{1,0:T(8,128)S(1)} collective-permute-done((f32[512,256]{1,0:T(8,128)}, f32[512,256]{1,0:T(8,128)S(1)}, u32[]{:S(2)}, u32[]{:S(2)}) %collective-permute-start.13) | collective-permute-done | bytes 524320 | tf_op jit(solution)/shard_map/ppermute | solution.py:486
  197.9 9.7 %collective-permute-done.15.refs_3_ = f32[136,512]{1,0:T(8,128)S(1)} collective-permute-done((f32[136,512]{1,0:T(8,128)}, f32[136,512]{1,0:T(8,128)S(1)}, u32[]{:S(2)}, u32[]{:S(2)}) %collective-permute-start.15) | collective-permute-done | bytes 278560 | tf_op jit(solution)/shard_map/ppermute | solution.py:486
  207.6 4.8 %collective-permute-done.16.refs_4_ = f32[136,512]{1,0:T(8,128)S(1)} collective-permute-done((f32[136,512]{1,0:T(8,128)}, f32[136,512]{1,0:T(8,128)S(1)}, u32[]{:S(2)}, u32[]{:S(2)}) %collective-permute-start.16) | collective-permute-done | bytes 278560 | tf_op jit(solution)/shard_map/ppermute | solution.py:486
  219.6 5.4 %collective-permute-done.22.refs_2_ = f32[128,512]{1,0:T(8,128)S(1)} collective-permute-done((f32[128,512]{1,0:T(8,128)}, f32[128,512]{1,0:T(8,128)S(1)}, u32[]{:S(2)}, u32[]{:S(2)}) %collective-permute-start.22) | collective-permute-done | bytes 262176 | tf_op jit(solution)/shard_map/ppermute | solution.py:486
  226.5 7.6 %collective-permute-done.23.refs_3_ = f32[128,512]{1,0:T(8,128)S(1)} collective-permute-done((f32[128,512]{1,0:T(8,128)}, f32[128,512]{1,0:T(8,128)S(1)}, u32[]{:S(2)}, u32[]{:S(2)}) %collective-permute-start.23) | collective-permute-done | bytes 262176 | tf_op jit(solution)/shard_map/ppermute | solution.py:486
  234.1 5.3 %collective-permute-done.24.refs_4_ = f32[128,512]{1,0:T(8,128)S(1)} collective-permute-done((f32[128,512]{1,0:T(8,128)}, f32[128,512]{1,0:T(8,128)S(1)}, u32[]{:S(2)}, u32[]{:S(2)}) %collective-permute-start.24) | collective-permute-done | bytes 262176 | tf_op jit(solution)/shard_map/ppermute | solution.py:486
  251.5 4.0 %collective-permute-done.26.refs_7_ = f32[128,512]{1,0:T(8,128)S(1)} collective-permute-done((f32[128,512]{1,0:T(8,128)}, f32[128,512]{1,0:T(8,128)S(1)}, u32[]{:S(2)}, u32[]{:S(2)}) %collective-permute-start.26) | collective-permute-done | bytes 262176 | tf_op jit(solution)/shard_map/ppermute | solution.py:486
  (120 shorter events, 69.3 us)
Async XLA Ops:
  4.5 22.9 %all-to-all-start.1 = ((bf16[8,48,1024]{2,1,0:T(8,128)(2,1)}), bf16[8,48,1024]{2,1,0:T(8,128)(2,1)S(1)}, u32[]{:S(2)}, u32[]{:S(2)}) async-start(bf16[8,48,1024]{2,1,0:T(8,128)(2,1)} %bitcast.39), calls=%async_computation.1 | async-start | bytes 1572864 | tf_op jit(solution)/shard_map/all_to_all | solution.py:566
  12.6 64.6 %collective-permute-start = (bf16[384,1024]{1,0:T(8,128)(2,1)}, bf16[384,1024]{1,0:T(8,128)(2,1)S(1)}, u32[]{:S(2)}, u32[]{:S(2)}) collective-permute-start(bf16[384,1024]{1,0:T(8,128)(2,1)} %get-tuple-element.58.normed_face_ref.refs_0_), channel_id=1, source_target_pairs={{0,1},{1,0},{2,3},{3,2},{4,5},{5,4},{6,7},{7,6},{8,9},{9,8},{10,11... | collective-permute-start | bytes 2359304 | tf_op jit(solution)/shard_map/ppermute | solution.py:486
  14.1 64.7 %collective-permute-start.1 = (bf16[384,1024]{1,0:T(8,128)(2,1)}, bf16[384,1024]{1,0:T(8,128)(2,1)S(1)}, u32[]{:S(2)}, u32[]{:S(2)}) collective-permute-start(bf16[384,1024]{1,0:T(8,128)(2,1)} %get-tuple-element.66), channel_id=1, source_target_pairs={{0,2},{1,3},{2,0},{3,1},{4,6},{5,7},{6,4},{7,5},{8,10},{9,11},{10,... | collective-permute-start | bytes 2359304 | tf_op jit(solution)/shard_map/ppermute | solution.py:486
  27.4 40.0 %all-to-all-start = ((bf16[8,48,1024]{2,1,0:T(8,128)(2,1)}), bf16[8,48,1024]{2,1,0:T(8,128)(2,1)S(1)}, u32[]{:S(2)}, u32[]{:S(2)}) async-start(bf16[8,48,1024]{2,1,0:T(8,128)(2,1)} %bitcast.38), calls=%async_computation | async-start | bytes 1572864 | tf_op jit(solution)/shard_map/all_to_all | solution.py:566
  38.0 41.3 %collective-permute-start.2 = (bf16[192,1024]{1,0:T(8,128)(2,1)}, bf16[192,1024]{1,0:T(8,128)(2,1)}, u32[]{:S(2)}, u32[]{:S(2)}) collective-permute-start(bf16[192,1024]{1,0:T(8,128)(2,1)} %get-tuple-element.63.normed_edge_ref.refs_2_), channel_id=1, source_target_pairs={{0,1},{1,0},{2,3},{3,2},{4,5},{5,4},{6,7},{7,6},{8,9},{9,8},{10,11... | collective-permute-start | bytes 1179656 | tf_op jit(solution)/shard_map/ppermute | solution.py:486
  39.5 41.3 %collective-permute-start.3 = (bf16[192,1024]{1,0:T(8,128)(2,1)}, bf16[192,1024]{1,0:T(8,128)(2,1)S(1)}, u32[]{:S(2)}, u32[]{:S(2)}) collective-permute-start(bf16[192,1024]{1,0:T(8,128)(2,1)} %get-tuple-element.67), channel_id=1, source_target_pairs={{0,2},{1,3},{2,0},{3,1},{4,6},{5,7},{6,4},{7,5},{8,10},{9,11},{10,... | collective-permute-start | bytes 1179656 | tf_op jit(solution)/shard_map/ppermute | solution.py:486
  66.8 46.7 %collective-permute-start.8 = (bf16[384,1024]{1,0:T(8,128)(2,1)}, bf16[384,1024]{1,0:T(8,128)(2,1)}, u32[]{:S(2)}, u32[]{:S(2)}) collective-permute-start(bf16[384,1024]{1,0:T(8,128)(2,1)} %get-tuple-element.79), channel_id=1, source_target_pairs={{0,2},{1,3},{2,0},{3,1},{4,6},{5,7},{6,4},{7,5},{8,10},{9,11},{10,... | collective-permute-start | bytes 2359304 | tf_op jit(solution)/shard_map/ppermute | solution.py:486
  68.3 39.5 %all-to-all-start.2 = ((bf16[8,48,1024]{2,1,0:T(8,128)(2,1)}), bf16[8,48,1024]{2,1,0:T(8,128)(2,1)S(1)}, u32[]{:S(2)}, u32[]{:S(2)}) async-start(bf16[8,48,1024]{2,1,0:T(8,128)(2,1)} %bitcast.40), calls=%async_computation.2 | async-start | bytes 1572864 | tf_op jit(solution)/shard_map/all_to_all | solution.py:670
  77.2 35.6 %collective-permute-start.7 = (bf16[192,1024]{1,0:T(8,128)(2,1)}, bf16[192,1024]{1,0:T(8,128)(2,1)S(1)}, u32[]{:S(2)}, u32[]{:S(2)}) collective-permute-start(bf16[192,1024]{1,0:T(8,128)(2,1)} %get-tuple-element.78), channel_id=1, source_target_pairs={{0,2},{1,3},{2,0},{3,1},{4,6},{5,7},{6,4},{7,5},{8,10},{9,11},{10,... | collective-permute-start | bytes 1179656 | tf_op jit(solution)/shard_map/ppermute | solution.py:486
  78.8 34.7 %collective-permute-start.6 = (bf16[384,1024]{1,0:T(8,128)(2,1)}, bf16[384,1024]{1,0:T(8,128)(2,1)}, u32[]{:S(2)}, u32[]{:S(2)}) collective-permute-start(bf16[384,1024]{1,0:T(8,128)(2,1)} %get-tuple-element.77), channel_id=1, source_target_pairs={{0,1},{1,0},{2,3},{3,2},{4,5},{5,4},{6,7},{7,6},{8,9},{9,8},{10,11... | collective-permute-start | bytes 2359304 | tf_op jit(solution)/shard_map/ppermute | solution.py:486
  79.3 34.1 %collective-permute-start.4 = (bf16[192,1024]{1,0:T(8,128)(2,1)}, bf16[192,1024]{1,0:T(8,128)(2,1)}, u32[]{:S(2)}, u32[]{:S(2)}) collective-permute-start(bf16[192,1024]{1,0:T(8,128)(2,1)} %get-tuple-element.59.normed_edge_ref.refs_3_), channel_id=1, source_target_pairs={{0,1},{1,0},{2,3},{3,2},{4,5},{5,4},{6,7},{7,6},{8,9},{9,8},{10,11... | collective-permute-start | bytes 1179656 | tf_op jit(solution)/shard_map/ppermute | solution.py:486
  107.2 39.8 %collective-permute-start.11 = (bf16[384,1024]{1,0:T(8,128)(2,1)}, bf16[384,1024]{1,0:T(8,128)(2,1)S(1)}, u32[]{:S(2)}, u32[]{:S(2)}) collective-permute-start(bf16[384,1024]{1,0:T(8,128)(2,1)} %get-tuple-element.84), channel_id=1, source_target_pairs={{0,2},{1,3},{2,0},{3,1},{4,6},{5,7},{6,4},{7,5},{8,10},{9,11},{10,... | collective-permute-start | bytes 2359304 | tf_op jit(solution)/shard_map/ppermute | solution.py:486
  107.8 39.3 %all-to-all-start.3 = ((bf16[8,48,1024]{2,1,0:T(8,128)(2,1)}), bf16[8,48,1024]{2,1,0:T(8,128)(2,1)S(1)}, u32[]{:S(2)}, u32[]{:S(2)}) async-start(bf16[8,48,1024]{2,1,0:T(8,128)(2,1)} %bitcast.41), calls=%async_computation.3 | async-start | bytes 1572864 | tf_op jit(solution)/shard_map/all_to_all | solution.py:670
  112.9 19.9 %collective-permute-start.5 = (bf16[384,1024]{1,0:T(8,128)(2,1)}, bf16[384,1024]{1,0:T(8,128)(2,1)S(1)}, u32[]{:S(2)}, u32[]{:S(2)}) collective-permute-start(bf16[384,1024]{1,0:T(8,128)(2,1)} %get-tuple-element.74), channel_id=1, source_target_pairs={{0,1},{1,0},{2,3},{3,2},{4,5},{5,4},{6,7},{7,6},{8,9},{9,8},{10,11... | collective-permute-start | bytes 2359304 | tf_op jit(solution)/shard_map/ppermute | solution.py:486
  159.4 15.2 %collective-permute-start.10 = (f32[520,256]{1,0:T(8,128)}, f32[520,256]{1,0:T(8,128)S(1)}, u32[]{:S(2)}, u32[]{:S(2)}) collective-permute-start(f32[520,256]{1,0:T(8,128)} %get-tuple-element.83), channel_id=1, source_target_pairs={{0,2},{1,3},{2,0},{3,1},{4,6},{5,7},{6,4},{7,5},{8,10},{9,11},{10,... | collective-permute-start | bytes 1597448 | tf_op jit(solution)/shard_map/ppermute | solution.py:486
  169.0 21.4 %collective-permute-start.20 = (f32[512,256]{1,0:T(8,128)S(1)}, f32[512,256]{1,0:T(8,128)S(1)}, u32[]{:S(2)}, u32[]{:S(2)}) collective-permute-start(f32[512,256]{1,0:T(8,128)S(1)} %copy-done.26), channel_id=1, source_target_pairs={{0,2},{1,3},{2,0},{3,1},{4,6},{5,7},{6,4},{7,5},{8,10},{9,11},{10,... | collective-permute-start | bytes 1572872 | tf_op jit(solution)/shard_map/ppermute | solution.py:486
  169.5 23.9 %collective-permute-start.21 = (f32[512,256]{1,0:T(8,128)}, f32[512,256]{1,0:T(8,128)S(1)}, u32[]{:S(2)}, u32[]{:S(2)}) collective-permute-start(f32[512,256]{1,0:T(8,128)} %get-tuple-element.96), channel_id=1, source_target_pairs={{0,1},{1,0},{2,3},{3,2},{4,5},{5,4},{6,7},{7,6},{8,9},{9,8},{10,11... | collective-permute-start | bytes 1572872 | tf_op jit(solution)/shard_map/ppermute | solution.py:486
  188.4 19.2 %collective-permute-start.15 = (f32[136,512]{1,0:T(8,128)}, f32[136,512]{1,0:T(8,128)S(1)}, u32[]{:S(2)}, u32[]{:S(2)}) collective-permute-start(f32[136,512]{1,0:T(8,128)} %get-tuple-element.91), channel_id=1, source_target_pairs={{0,16},{4,20},{8,24},{12,28},{16,0},{20,4},{24,8},{28,12},{1,17},{... | collective-permute-start | bytes 835592 | tf_op jit(solution)/shard_map/ppermute | solution.py:486
  188.9 23.4 %collective-permute-start.16 = (f32[136,512]{1,0:T(8,128)}, f32[136,512]{1,0:T(8,128)S(1)}, u32[]{:S(2)}, u32[]{:S(2)}) collective-permute-start(f32[136,512]{1,0:T(8,128)} %get-tuple-element.92), channel_id=1, source_target_pairs={{0,24},{4,28},{8,16},{12,20},{16,8},{20,12},{24,0},{28,4},{1,25},{... | collective-permute-start | bytes 835592 | tf_op jit(solution)/shard_map/ppermute | solution.py:486
  215.1 29.1 %collective-permute-start.17 = (f32[136,512]{1,0:T(8,128)}, f32[136,512]{1,0:T(8,128)S(1)}, u32[]{:S(2)}, u32[]{:S(2)}) collective-permute-start(f32[136,512]{1,0:T(8,128)} %block_sum.2.refs_1_), channel_id=1, source_target_pairs={{0,1},{1,0},{2,3},{3,2},{4,5},{5,4},{6,7},{7,6},{8,9},{9,8},{10,11... | collective-permute-start | bytes 835592 | tf_op jit(solution)/shard_map/ppermute | solution.py:486
  215.6 18.5 %collective-permute-start.23 = (f32[128,512]{1,0:T(8,128)}, f32[128,512]{1,0:T(8,128)S(1)}, u32[]{:S(2)}, u32[]{:S(2)}) collective-permute-start(f32[128,512]{1,0:T(8,128)} %get-tuple-element.99), channel_id=1, source_target_pairs={{0,16},{4,20},{8,24},{12,28},{16,0},{20,4},{24,8},{28,12},{1,17},{... | collective-permute-start | bytes 786440 | tf_op jit(solution)/shard_map/ppermute | solution.py:486
  217.6 21.8 %collective-permute-start.24 = (f32[128,512]{1,0:T(8,128)}, f32[128,512]{1,0:T(8,128)S(1)}, u32[]{:S(2)}, u32[]{:S(2)}) collective-permute-start(f32[128,512]{1,0:T(8,128)} %get-tuple-element.100), channel_id=1, source_target_pairs={{0,24},{4,28},{8,16},{12,20},{16,8},{20,12},{24,0},{28,4},{1,25},{... | collective-permute-start | bytes 786440 | tf_op jit(solution)/shard_map/ppermute | solution.py:486
  219.1 36.4 %collective-permute-start.18 = (f32[136,512]{1,0:T(8,128)}, f32[136,512]{1,0:T(8,128)S(1)}, u32[]{:S(2)}, u32[]{:S(2)}) collective-permute-start(f32[136,512]{1,0:T(8,128)} %block_sum.2.refs_1_), channel_id=1, source_target_pairs={{0,2},{1,3},{2,0},{3,1},{4,6},{5,7},{6,4},{7,5},{8,10},{9,11},{10,... | collective-permute-start | bytes 835592 | tf_op jit(solution)/shard_map/ppermute | solution.py:486
  225.1 30.5 %collective-permute-start.19 = (f32[136,512]{1,0:T(8,128)}, f32[136,512]{1,0:T(8,128)S(1)}, u32[]{:S(2)}, u32[]{:S(2)}) collective-permute-start(f32[136,512]{1,0:T(8,128)} %block_sum.2.refs_1_), channel_id=1, source_target_pairs={{0,3},{1,2},{2,1},{3,0},{4,7},{5,6},{6,5},{7,4},{8,11},{9,10},{10,... | collective-permute-start | bytes 835592 | tf_op jit(solution)/shard_map/ppermute | solution.py:486
  (36 other events, 198.5 us)

commit v3 on v2

--- a/solution.py
+++ b/solution.py
@@ -12,6 +12,8 @@
 BF = jnp.bfloat16
 F32 = jnp.float32
 VMEM_BYTES = 60 * 1024 * 1024
+SMALL_BYTES = 28 * 1024 * 1024
+WEIGHT_BYTES = 54 * 1024 * 1024
 
 
 def nn(a, b):
@@ -125,26 +127,36 @@
 
 
 def layer_kernel(
-    lines,
-    aliased,
-    drop,
-    scal_ref,
-    rotation_ref,
-    counts_ref,
-    face_ref,
-    fcot_ref,
-    z_edge_ref,
-    g_edge_ref,
-    normed_face_ref,
-    normed_edge_ref,
-    back_index_ref,
-    gain_ref,
-    wqkv_ref,
-    wo_ref,
-    *refs,
+    lines, first_chunk, drop, scal_ref, rotation_ref, counts_ref, face_ref, fcot_ref, *refs
 ):
-    refs = refs[drop + (2 if aliased else 0) :]
     base = scal_ref[0]
+    if first_chunk:
+        arrived_ref, index_ref, normed_face_ref, gain_ref, wqkv_ref, wo_ref = refs[:6]
+        refs = refs[6 + drop :]
+        send_a, send_b = refs[4], refs[6]
+        g_edge_ref, normed_edge_ref = refs[8:10]
+        z_edge_ref = refs[-1]
+        refs = (*refs[:8], *refs[10:-1])
+        late_rows = refs[3].shape[0]
+        edge_rows = z_edge_ref.shape[0]
+        edge_kernel(
+            lines,
+            scal_ref,
+            rotation_ref,
+            counts_ref,
+            arrived_ref,
+            index_ref,
+            gain_ref,
+            z_edge_ref,
+            g_edge_ref,
+            normed_edge_ref,
+            send_b.at[pl.ds(late_rows, edge_rows)],
+        )
+        send_a[late_rows:] = normed_edge_ref[...]
+    else:
+        z_edge_ref, g_edge_ref, normed_edge_ref = refs[:3]
+        normed_face_ref, gain_ref, wqkv_ref, wo_ref, back_index_ref, before_ref = refs[3:9]
+        refs = refs[9 + drop :]
     (
         face_out,
         face_grad,
@@ -251,6 +263,7 @@
         dn_s[:, cols] = nt(stk_s[...], wqkv_ref[cols, :])
 
     gain_sum = jnp.zeros((1, width), F32)
+    off = 0 if first_chunk else 2 * edges
     for i in range(2 * lines):
         size = face_len if i < lines else edge_len
         start = i * face_len if i < lines else faces + (i - lines) * edge_len
@@ -267,41 +280,49 @@
             face_out[0, i] = y_s[at]
             face_grad[0, i] = dz
         else:
-            edge_s[edges + start - faces : edges + start - faces + size] = dz
-    edge_s[:edges] = y_s[faces:]
+            at = off + edges + start - faces
+            edge_s[at : at + size] = dz
+    edge_s[off : off + edges] = y_s[faces:]
     lanes = gain_part.shape[1]
     for i in range(width // lanes):
         gain_part[i : i + 1] = gain_sum[:, i * lanes : (i + 1) * lanes]
     for i in range(2 * lines):
         cosine, sine = turn_pair(rotation_ref, base + i % lines)
-        rows = slice(i * edge_len, (i + 1) * edge_len)
+        rows = slice(off + i * edge_len, off + (i + 1) * edge_len)
         u, v = edge_s[rows, :half].astype(F32), edge_s[rows, half:].astype(F32)
         edge_s[rows, :half] = (cosine * u + sine * v).astype(BF)
         edge_s[rows, half:] = (cosine * v - sine * u).astype(BF)
-    picked = one_hot_rows(flips(back_index_ref, rotation_ref, base, lines), 2 * edges)
-    back_ref[...] = nn(picked, edge_s[...]).astype(BF)
-
+    if first_chunk:
+        back_ref[...] = edge_s[...]
+    else:
+        edge_s[:off] = before_ref[...]
+        picked = one_hot_rows(
+            flips(back_index_ref, rotation_ref, base - lines, 2 * lines), 4 * edges
+        )
+        back_ref[...] = nn(picked, edge_s[...]).astype(BF)
+
+    total_rows = z_s.shape[0]
     x_bit = scal_ref[1]
     y_bit = scal_ref[2]
 
     @pl.when(x_bit == 0)
     def _():
         keep_a[...] = stk_s[:, :width]
-        send_a[...] = stk_s[:, width : 2 * width]
+        send_a[:total_rows] = stk_s[:, width : 2 * width]
 
     @pl.when(x_bit != 0)
     def _():
-        send_a[...] = stk_s[:, :width]
+        send_a[:total_rows] = stk_s[:, :width]
         keep_a[...] = stk_s[:, width : 2 * width]
 
     @pl.when(y_bit == 0)
     def _():
         keep_b[...] = stk_s[:, 2 * width :]
-        send_b[...] = mix_s[...]
+        send_b[:total_rows] = mix_s[...]
 
     @pl.when(y_bit != 0)
     def _():
-        send_b[...] = stk_s[:, 2 * width :]
+        send_b[:total_rows] = stk_s[:, 2 * width :]
         keep_b[...] = mix_s[...]
 
 
@@ -341,7 +362,8 @@
             total = tn(lhs, rhs)
             for ref in add_refs:
                 total = total + ref[:rows]
-            outs[0][:rows] = total
+            for n, out in enumerate(outs):
+                out[:part] = total[n * part : (n + 1) * part]
             return
         for half in range(2):
             mine = (scal_ref[2] if half else 1 - scal_ref[2]) == 0
@@ -373,11 +395,15 @@
                     out[rows:, n * lanes : (n + 1) * lanes] = total
 
 
-def weight_part(scal, runs, parities, blocks, operands, adds, pieces, halved, gains, deps):
+def weight_part(
+    scal, runs, parities, blocks, operands, adds, pieces, halved, gains, deps, held=()
+):
+    pieces_of = [o if isinstance(o, tuple) else (o, o.shape[0], 0) for o in operands]
+    operands = [o for o, _, _ in pieces_of]
     width = operands[-1].shape[1]
     part = width // 2
     rows = len(parities) * part
-    depth = len(runs) * operands[runs[0][3]].shape[0]
+    depth = len(runs) * pieces_of[runs[0][3]][1]
     extra = gains[0].shape[0] if gains else 0
     used = len(operands) + len(adds) + len(gains)
 
@@ -387,37 +413,40 @@
             runs, parities, blocks, len(operands), len(adds), len(gains), halved, scal_ref, *refs
         )
 
-    def spec(shape, at=0):
-        return pl.BlockSpec(shape, lambda i, s: (at, 0))
-
-    add_specs = [
-        spec(a.shape) if at is None else spec((rows, width), at) for a, at in adds
-    ]
+    def spec(shape):
+        return pl.BlockSpec(shape, lambda i, s: (0, 0))
+
+    near = pl.BlockSpec(memory_space=pltpu.VMEM)
     if halved:
         tile = part // pieces
         shapes = [
             (rows + (extra if n % pieces == 0 else 0), tile) for n in range(2 * pieces)
         ]
     else:
-        shapes = [(rows + extra, width)]
+        shapes = [(part + extra, width)] * len(parities)
     return pl.pallas_call(
         kernel,
         grid_spec=pltpu.PrefetchScalarGridSpec(
             num_scalar_prefetch=1,
             grid=(1,),
-            in_specs=[spec(o.shape) for o in operands]
-            + add_specs
+            in_specs=[
+                near
+                if n in held
+                else pl.BlockSpec((size, width), lambda i, s, at=at: (at, 0))
+                for n, (_, size, at) in enumerate(pieces_of)
+            ]
+            + [near] * len(adds)
             + [spec(g.shape) for g in gains]
             + [pl.BlockSpec(memory_space=pl.ANY)] * len(deps),
-            out_specs=[spec(s) for s in shapes],
+            out_specs=[near] * len(shapes),
         ),
         out_shape=[jax.ShapeDtypeStruct(s, F32) for s in shapes],
-        compiler_params=pltpu.CompilerParams(vmem_limit_bytes=VMEM_BYTES),
+        compiler_params=pltpu.CompilerParams(vmem_limit_bytes=SMALL_BYTES if len(runs) == 1 else WEIGHT_BYTES),
         cost_estimate=pl.CostEstimate(
             flops=1 << 33 if len(runs) > 1 else 1024, bytes_accessed=1024, transcendentals=0
         ),
         name="weight_part",
-    )(scal, *operands, *[a for a, _ in adds], *gains, *deps)
+    )(scal, *operands, *adds, *gains, *deps)
 
 
 def block_kernel(blocks, count, scal_ref, *refs):
@@ -486,7 +515,7 @@
     return lax.ppermute(x, axis, [(i, i ^ bits) for i in range(size)])
 
 
-def whole_call(kernel, name, scal, out_shape, operands, deps=(), scratch=(), flops=0):
+def whole_call(kernel, name, scal, out_shape, operands, deps=(), scratch=(), flops=0, limit=SMALL_BYTES, near=(False, False)):
     scal = scal if isinstance(scal, tuple) else (scal,)
 
     def body(*refs):
@@ -496,19 +525,20 @@
     def spec(shape):
         return pl.BlockSpec(shape, lambda i, *s: (0,) * len(shape))
 
+    vmem = pl.BlockSpec(memory_space=pltpu.VMEM)
     moved = sum(int(np.prod(o.shape)) * o.dtype.itemsize for o in [*operands, *out_shape])
     return pl.pallas_call(
         body,
         grid_spec=pltpu.PrefetchScalarGridSpec(
             num_scalar_prefetch=len(scal),
             grid=(1,),
-            in_specs=[spec(o.shape) for o in operands]
+            in_specs=[vmem if near[0] else spec(o.shape) for o in operands]
             + [pl.BlockSpec(memory_space=pl.ANY)] * len(deps),
-            out_specs=[spec(o.shape) for o in out_shape],
+            out_specs=[vmem if near[1] else spec(o.shape) for o in out_shape],
             scratch_shapes=list(scratch),
         ),
         out_shape=out_shape,
-        compiler_params=pltpu.CompilerParams(vmem_limit_bytes=VMEM_BYTES),
+        compiler_params=pltpu.CompilerParams(vmem_limit_bytes=limit),
         cost_estimate=pl.CostEstimate(flops=1024, bytes_accessed=1024, transcendentals=0),
         name=name,
     )(*scal, *operands, *deps)
@@ -562,6 +592,7 @@
             jnp.asarray(order.reshape(-1, 1)),
         ],
         scratch=[pltpu.VMEM((2 * K * NLG, width), BF)],
+        limit=VMEM_BYTES,
     )
     arrived = [lax.all_to_all(s, "tile", split_axis=0, concat_axis=0, tiled=True) for s in sent]
 
@@ -573,6 +604,7 @@
         y_bit.reshape(1),
         [struct(LD * FL, width)] * 2,
         [face_rows, face_cots, gain],
+        limit=VMEM_BYTES,
     )
     got_face_a = exchange(face_normed, "dp", 1, D)
     got_face_b = exchange(face_early, "dp", 2, D)
@@ -585,26 +617,23 @@
         table.append(np.stack([row, row + RB]))
     table.append(np.stack([l, l]))
     index = jnp.asarray(np.stack(table, axis=-1).reshape(-1, 3).astype(np.int32))
-    t, w, l, k = np.meshgrid(
-        np.arange(T), np.arange(2), np.arange(lines), np.arange(K), indexing="ij"
+    t, c, w, l, k = np.meshgrid(
+        np.arange(T),
+        np.arange(chunks),
+        np.arange(2),
+        np.arange(lines),
+        np.arange(K),
+        indexing="ij",
     )
+    at = 2 * c * edges + w * edges + l * EL
     pos = t * K + k
-    table = [w * edges + l * EL + pos, w * edges + l * EL + EL - 1 - pos, l]
+    table = [at + pos, at + EL - 1 - pos, c * lines + l]
     back_index = jnp.asarray(np.stack(table, axis=-1).reshape(-1, 3).astype(np.int32))
     edge_parts, results, got_edges, got_late = [], [], [], []
     faces = None
     for c in range(chunks):
         base = (me_t * LD + c * lines).astype(jnp.int32)
         scal = (jnp.stack([base, x_bit, y_bit]), rotation, counts)
-        z_edge, g_edge, normed_edge, early_edge = whole_call(
-            functools.partial(edge_kernel, lines),
-            "edge_norm",
-            scal,
-            [struct(edges, width)] * 4,
-            [arrived[c], index, gain],
-        )
-        edge_parts.append((normed_edge, g_edge))
-        got_edges.append((exchange(normed_edge, "dp", 1, D), exchange(early_edge, "dp", 2, D)))
         rows_all = lines * length
         row_shape = (rows_all, width)
         face_spec = pl.BlockSpec((1, lines, FL, width), lambda i, *s, c=c: (0, c, 0, 0))
@@ -613,34 +642,43 @@
         def full(shape):
             return pl.BlockSpec(shape, lambda i, *s: (0,) * len(shape))
 
-        operands = [
-            face_tokens,
-            face_cotangent,
-            z_edge,
-            g_edge,
-            face_normed,
-            normed_edge,
-            back_index,
-            gain,
-            qkv_weight,
-            out_weight,
+        if c == 0:
+            operands = [face_tokens, face_cotangent, arrived[c], index]
+            operands += [face_normed, gain, qkv_weight, out_weight]
+            tail = []
+        else:
+            z_edge, g_edge, normed_edge, early_edge = whole_call(
+                functools.partial(edge_kernel, lines),
+                "edge_norm",
+                scal,
+                [struct(edges, width)] * 4,
+                [arrived[c], index, gain],
+                deps=[results[0][5]],
+                limit=VMEM_BYTES,
+            )
+            operands = [face_tokens, face_cotangent, z_edge, g_edge, normed_edge]
+            operands += [face_normed, gain, qkv_weight, out_weight, back_index, results[0][0]]
+            tail = [*faces, got_face_a, got_face_b]
+        in_specs = [
+            face_spec if n < 2 else normed_spec if o is face_normed else full(o.shape)
+            for n, o in enumerate(operands)
         ]
-        in_specs = [face_spec, face_spec] + [full(o.shape) for o in operands[2:]]
-        in_specs[4] = normed_spec
-        held = [got_face_a, got_face_b, *got_edges[0]] if c else []
-        if faces is not None:
-            operands += list(faces)
-        operands += held
-        in_specs += [pl.BlockSpec(memory_space=pl.ANY)] * (len(operands) - len(in_specs))
+        in_specs += [pl.BlockSpec(memory_space=pl.ANY)] * len(tail)
+        aliases = {} if c == 0 else {3 + len(operands): 0, 4 + len(operands): 1}
+        operands += tail
+        back_rows = 2 * edges if c == 0 else packed * chunks
+        edge_outs = [(edges, width)] * 2 if c == 0 else []
+        send_shape = (rows_all + (edges if c == 0 else 0), width)
         outs = pl.pallas_call(
-            functools.partial(layer_kernel, lines, faces is not None, len(held)),
+            functools.partial(layer_kernel, lines, c == 0, len(tail)),
             grid_spec=pltpu.PrefetchScalarGridSpec(
                 num_scalar_prefetch=3,
                 grid=(1,),
                 in_specs=in_specs,
-                out_specs=[face_spec, face_spec, full((packed, width))]
-                + [full(row_shape)] * 4
-                + [full((8, width // 8))],
+                out_specs=[face_spec, face_spec, full((back_rows, width))]
+                + [full(row_shape), full(send_shape)] * 2
+                + [full((8, width // 8))]
+                + [full(e) for e in edge_outs],
                 scratch_shapes=[
                     pltpu.VMEM(row_shape, BF),
                     pltpu.VMEM(row_shape, BF),
@@ -651,24 +689,34 @@
                     pltpu.VMEM((rows_all, 3 * width), BF),
                     pltpu.VMEM(row_shape, F32),
                     pltpu.VMEM(row_shape, BF),
-                    pltpu.VMEM((2 * edges, width), BF),
-                ],
+                    pltpu.VMEM((2 * edges * (c + 1), width), BF),
+                ]
+                + ([pltpu.VMEM((edges, width), BF)] if c == 0 else []),
             ),
             out_shape=[struct(*face_tokens.shape)] * 2
-            + [struct(packed, width)]
-            + [struct(*row_shape)] * 4
-            + [struct(8, width // 8, dtype=F32)],
-            input_output_aliases={13: 0, 14: 1} if faces is not None else {},
+            + [struct(back_rows, width)]
+            + [struct(*row_shape), struct(*send_shape)] * 2
+            + [struct(8, width // 8, dtype=F32)]
+            + [struct(*e) for e in edge_outs],
+            input_output_aliases=aliases,
             compiler_params=pltpu.CompilerParams(vmem_limit_bytes=VMEM_BYTES),
             cost_estimate=pl.CostEstimate(flops=1 << 35, bytes_accessed=1 << 20, transcendentals=0),
             name="layer",
         )(*scal, *operands)
         faces = outs[:2]
         results.append(outs[2:])
-        got_late.append((exchange(outs[4], "dp", 1, D), exchange(outs[6], "dp", 2, D)))
-    returned = [
-        lax.all_to_all(r[0], "tile", split_axis=0, concat_axis=0, tiled=True) for r in results
-    ]
+        late_a, late_b = exchange(outs[4], "dp", 1, D), exchange(outs[6], "dp", 2, D)
+        if c == 0:
+            g_edge, normed_edge = outs[8:]
+            edges_a, edges_b = (late_a, edges, rows_all // edges), (late_b, edges, rows_all // edges)
+            late_a, late_b = (late_a, rows_all, 0), (late_b, rows_all, 0)
+        else:
+            edges_a = exchange(normed_edge, "dp", 1, D)
+            edges_b = exchange(early_edge, "dp", 2, D)
+        edge_parts.append((normed_edge, g_edge))
+        got_edges.append((edges_a, edges_b))
+        got_late.append((late_a, late_b))
+    returned = lax.all_to_all(results[1][0], "tile", split_axis=0, concat_axis=0, tiled=True)
 
     blocks = T // 2
     chip = (me_t // 2).astype(jnp.int32)
@@ -690,22 +738,25 @@
         runs = [((0, 1), (2, 4), 0, 8), ((0, 1), (3, 5), 1, 9), ((6, 6), (7, 7), 0, 10)]
         start = weight_part(
             scal, runs, (False, True), blocks, operands, [], pieces, False, [],
-            [returned[0], *got_edges[1], *got_late[0]] if group == 0 else [],
-        )[0]
+            [*got_edges[1], got_late[0][0][0], got_late[0][1][0]],
+        )
         groups.append((scal, [got_face, got_e[1], got_l[1]], start, first))
     theirs = []
     runs = [((0, 0), (1, 1), 1, 2)]
     gains = [[r[5] for r in results], []]
+    starts = [g[2] for g in groups]
     for group, (scal, operands, start, first) in enumerate(groups):
         send = weight_part(
-            scal, runs, (False,), blocks, operands, [(start, 0)], pieces, False, gains[group], [returned[1]] if group else []
+            scal, runs, (False,), blocks, operands, [start[0]], pieces, False, gains[group],
+            [] if group else [starts[1][0]],
+            held=(2,),
         )[0]
         theirs.append(exchange(send, "tile", 1, T))
     halves = []
     for group, (scal, operands, start, first) in enumerate(groups):
         outs = weight_part(
-            scal, runs, (True,), blocks, operands, [(start, 1), (theirs[group], None)], pieces, True,
-            gains[group], [],
+            scal, runs, (True,), blocks, operands, [start[1], theirs[group]], pieces, True,
+            gains[group], [], held=(2,),
         )
         parts = []
         for n in range(pieces):
@@ -730,6 +781,8 @@
             chip.reshape(1),
             [struct(size + (8 if n == 0 else 0), columns, dtype=F32)] * blocks,
             parts,
+            near=(True, True),
+            deps=[returned] if n == 0 else [],
         )
         got = [exchange(outs[o], "tile", 2 * o, T) for o in range(1, blocks)]
         (mine,) = whole_call(
@@ -738,6 +791,7 @@
             chip.reshape(1),
             [struct(*outs[0].shape, dtype=F32)],
             [outs[0], *got],
+            near=(True, True),
         )
         placed += [mine] + [exchange(mine, "dp", o, D) for o in range(1, D)]
 
@@ -746,13 +800,13 @@
         k, t, c, l = np.meshgrid(
             np.arange(K), np.arange(T), np.arange(chunks), np.arange(lines), indexing="ij"
         )
-        back_order[w] = (c * packed + t * 2 * RB + w * RB + l * K + k).reshape(K, NLG)
+        back_order[w] = ((t * chunks + c) * 2 * RB + w * RB + l * K + k).reshape(K, NLG)
     edge_output, edge_grad = whole_call(
-        lambda s, *refs: unpack_kernel(chunks, *refs),
+        lambda s, *refs: unpack_kernel(1, *refs),
         "unpack",
         chip.reshape(1),
         [struct(K * NLG, width)] * 2,
-        [*returned, jnp.asarray(back_order.reshape(-1, 1))],
+        [returned, jnp.asarray(back_order.reshape(-1, 1))],
         scratch=[pltpu.VMEM((chunks * packed, width), BF)],
     )
     qkv_grad, out_grad = whole_call(
@@ -761,6 +815,7 @@
         me_d.astype(jnp.int32).reshape(1),
         [struct(size, 3 * width, dtype=F32), struct(size, width, dtype=F32)],
         placed,
+        near=(True, False),
     )
     gain_sum = (placed[0] + placed[1])[size:, : width // 8].reshape(width)
     gain_grad = lax.dynamic_slice_in_dim(gain_sum, me_t * size, size)

time: 260 us -> 225 us (0.87)
  Pallas kernels: 121 us -> 99.6 us
  waiting for transfers between devices: 74.2 us -> 68.8 us
  starting transfers between devices: 51 us -> 45.9 us
  local copies, waits for them, and re-layouts: 9.74 us -> 6.62 us
    pallas_call x10 -> x9, Pallas kernels: 30.5 us -> 18.4 us  [whole_call(): pl.pallas_call(body, grid_spec=pltpu.PrefetchScalarGridSpec(num_scalar_pr...]
    pallas_call x6, Pallas kernels: 38.8 us -> 27.3 us  [weight_part(): pl.pallas_call(kernel, grid_spec=pltpu.PrefetchScalarGridSpec(num_scalar_...]
    ppermute x28 -> x26, waiting for transfers between devices: 64.9 us -> 59.4 us  [exchange(): return lax.ppermute(x, axis, [(i, i ^ bits) for i in range(size)])]
    all_to_all x2 -> x1, starting transfers between devices: 10.2 us -> 5.11 us  [local(): lax.all_to_all(results[1][0], 'tile', split_axis=0, concat_axis=0, tiled=...]
    unnamed x56 -> x48, local copies, waits for them, and re-layouts: 9.15 us -> 6.04 us
    ppermute x28 -> x26, starting transfers between devices: 28.8 us -> 28.8 us  [exchange(): return lax.ppermute(x, axis, [(i, i ^ bits) for i in range(size)])]
  transfers between devices with their start and end apart: 32 -> 29, of which waited for: 13 -> 14; matrix products, arithmetic and copies ran while one was open for 1% -> 1% of each run, Pallas kernels for 43% -> 41%
where the time goes in v3:
time: 225 us; the launch traced here: 224 us
  Pallas kernels  99.6 us (44%)
  waiting for transfers between devices  68.8 us (31%)
  starting transfers between devices  45.9 us (20%)
  local copies, waits for them, and re-layouts  6.62 us (3%)
  other arithmetic  2.49 us (1%)
    ppermute x26, waiting for transfers between devices, exchange(): return lax.ppermute(x, axis, [(i, i ^ bits) for i in range(size)])  59.4 us
    pallas_call x2, Pallas kernels, local(): pl.pallas_call(functools.partial(layer_kernel, lines, c == 0, len(tail)),...  53.9 us
    ppermute x26, starting transfers between devices, exchange(): return lax.ppermute(x, axis, [(i, i ^ bits) for i in range(size)])  28.8 us
    pallas_call x6, Pallas kernels, weight_part(): pl.pallas_call(kernel, grid_spec=pltpu.PrefetchScalarGridSpec(num_scalar_...  27.3 us
    pallas_call x9, Pallas kernels, whole_call(): pl.pallas_call(body, grid_spec=pltpu.PrefetchScalarGridSpec(num_scalar_pr...  18.4 us
    all_to_all x2, starting transfers between devices, local(): lax.all_to_all(s, 'tile', split_axis=0, concat_axis=0, tiled=True)  12 us
    all_to_all x2, waiting for transfers between devices, local(): lax.all_to_all(s, 'tile', split_axis=0, concat_axis=0, tiled=True)  9.37 us
    unnamed x48, local copies, waits for them, and re-layouts  6.04 us
  transfers between devices with their start and end apart: 29, of which 14 were waited for; matrix products, arithmetic and copies ran while one was open for 1% of the time, Pallas kernels for 41%

profile of v3, /device:TPU:16, one launch (start us, length us, event | category | flops | bytes accessed | tf_op | source)
XLA Modules:
  0.0 224.3 jit_solution(3015463441575441426)
XLA Ops:
  0.7 3.8 %pack.1 = (bf16[384,1024]{1,0:T(8,128)(2,1)}, bf16[384,1024]{1,0:T(8,128)(2,1)}) custom-call(s32[1]{0:T(128)} %bitcast.2.refs_0_, bf16[384,1024]{1,0:T(8,128)(2,1)} %bitcast.28, bf16[384,1024]{1,0:T(8,128)(2,1)} %bitcast.29, s32[768,1]{1,0:T(8,128)} %constant.68.clone.refs_3_), custom_call_target="tpu_custom_call" | custom-call | flops 1024 | bytes 1024 | tf_op jit(solution)/shard_map/pack/pallas_call | solution.py:530
  4.5 5.2 %all-to-all-start.1 = ((bf16[8,48,1024]{2,1,0:T(8,128)(2,1)}), bf16[8,48,1024]{2,1,0:T(8,128)(2,1)S(1)}, u32[]{:S(2)}, u32[]{:S(2)}) async-start(bf16[8,48,1024]{2,1,0:T(8,128)(2,1)} %bitcast.35), calls=%async_computation.1 | async-start | bytes 1572864 | tf_op jit(solution)/shard_map/all_to_all | solution.py:597
  9.7 2.8 %face_norm.1 = (bf16[384,1024]{1,0:T(8,128)(2,1)}, bf16[384,1024]{1,0:T(8,128)(2,1)}) custom-call(s32[1]{0:T(128)} %bitcast.2.refs_0_, bf16[384,1024]{1,0:T(8,128)(2,1)} %bitcast.30, bf16[384,1024]{1,0:T(8,128)(2,1)} %bitcast.31, f32[1,1024]{1,0:T(1,128)} %bitcast.36), custom_call_target="tpu_custom_call" | custom-call | flops 1024 | bytes 1024 | tf_op jit(solution)/shard_map/face_norm/pallas_call | solution.py:530
  18.1 9.4 %all-to-all-done.1 = bf16[8,48,1024]{2,1,0:T(8,128)(2,1)S(1)} async-done(((bf16[8,48,1024]{2,1,0:T(8,128)(2,1)}), bf16[8,48,1024]{2,1,0:T(8,128)(2,1)S(1)}, u32[]{:S(2)}, u32[]{:S(2)}) %all-to-all-start.1) | async-done | bytes 786464 | tf_op jit(solution)/shard_map/all_to_all | solution.py:597
  27.4 6.7 %all-to-all-start = ((bf16[8,48,1024]{2,1,0:T(8,128)(2,1)}), bf16[8,48,1024]{2,1,0:T(8,128)(2,1)S(1)}, u32[]{:S(2)}, u32[]{:S(2)}) async-start(bf16[8,48,1024]{2,1,0:T(8,128)(2,1)} %bitcast.5), calls=%async_computation | async-start | bytes 1572864 | tf_op jit(solution)/shard_map/all_to_all | solution.py:597
  34.2 27.0 %layer.2 = (bf16[1,6,64,1024]{3,2,1,0:T(8,128)(2,1)}, bf16[1,6,64,1024]{3,2,1,0:T(8,128)(2,1)}, bf16[384,1024]{1,0:T(8,128)(2,1)}, bf16[384,1024]{1,0:T(8,128)(2...) custom-call(s32[3]{0:T(128)} %add_add_fusion.1.scal_ref, ...), custom_call_target="tpu_custom_call" | custom-call | flops 34359738368 | bytes 1048576 | tf_op jit(solution)/shard_map/layer/pallas_call | solution.py:672
  62.0 3.9 %edge_norm.1 = (bf16[192,1024]{1,0:T(8,128)(2,1)}, bf16[192,1024]{1,0:T(8,128)(2,1)}, bf16[192,1024]{1,0:T(8,128)(2,1)}, bf16[192,1024]{1,0:T(8,128)(2,1)}) custom-call(s32[3]{0:T(128)} %add_add_fusion.refs_0_.scal_ref, s32[48]{0:T(128)} %rotation_ref.3, s32[48]{0:T(128)} %counts_ref.3, bf16[384,1024]{1,0:T(8,128)(2,1)} %bitcast.26, ...), custom_call_target="tpu_custom_call" | custom-call | flops 1024 | bytes 1024 | tf_op jit(solution)/shard_map/edge_norm/pallas_call | solution.py:530
  70.8 27.0 %layer.3 = (bf16[1,6,64,1024]{3,2,1,0:T(8,128)(2,1)}, bf16[1,6,64,1024]{3,2,1,0:T(8,128)(2,1)}, bf16[768,1024]{1,0:T(8,128)(2,1)}, bf16[384,1024]{1,0:T(8,128)(2...) custom-call(s32[3]{0:T(128)} %add_add_fusion.refs_0_.scal_ref, ...), custom_call_target="tpu_custom_call", output_to_operand_aliasing={{0}: (14, {}), {1}: (15, {})} | custom-call | flops 34359738368 | bytes 1048576 | tf_op jit(solution)/shard_map/layer/pallas_call | solution.py:672
  99.4 5.1 %all-to-all-start.2 = ((bf16[8,96,1024]{2,1,0:T(8,128)(2,1)}), bf16[8,96,1024]{2,1,0:T(8,128)(2,1)S(1)}, u32[]{:S(2)}, u32[]{:S(2)}) async-start(bf16[8,96,1024]{2,1,0:T(8,128)(2,1)} %bitcast.27), calls=%async_computation.2 | async-start | bytes 3145728 | tf_op jit(solution)/shard_map/all_to_all | solution.py:719
  106.1 8.7 %weight_part.7 = (f32[512,1024]{1,0:T(8,128)}, f32[512,1024]{1,0:T(8,128)}) custom-call(s32[3]{0:T(128)} %pad_add_fusion.1.scal_ref, bf16[384,1024]{1,0:T(8,128)(2,1)} %get-tuple-element.59.refs_2_.refs_3_.refs_0_, bf16[384,1024]{1,0:T(8,128)(2,1)} %bitcast.32, bf16[192,1024]{1,0:T(8,128)(2,1)} %get-tuple-element.74.refs_2_, ...), custom_call_target="tpu_custom_call" | custom-call | flops 8589934592 | bytes 1024 | tf_op jit(solution)/shard_map/weight_part/pallas_call | solution.py:427
  114.9 8.7 %weight_part.6 = (f32[512,1024]{1,0:T(8,128)}, f32[512,1024]{1,0:T(8,128)}) custom-call(s32[3]{0:T(128)} %pad_add_fusion.scal_ref, bf16[384,1024]{1,0:T(8,128)(2,1)} %get-tuple-element.59.refs_2_.refs_3_.refs_0_, bf16[384,1024]{1,0:T(8,128)(2,1)} %bitcast.33, bf16[192,1024]{1,0:T(8,128)(2,1)} %get-tuple-element.74.refs_2_, ...), custom_call_target="tpu_custom_call" | custom-call | flops 8589934592 | bytes 1024 | tf_op jit(solution)/shard_map/weight_part/pallas_call | solution.py:427
  131.4 2.5 %weight_part.9 = (f32[520,256]{1,0:T(8,128)}, f32[512,256]{1,0:T(8,128)}, f32[520,256]{1,0:T(8,128)S(1)}, f32[512,256]{1,0:T(8,128)S(1)}) custom-call(s32[3]{0:T(128)S(1)} %copy-done.20, bf16[384,1024]{1,0:T(8,128)(2,1)S(1)} %copy-done.4, bf16[192,1024]{1,0:T(8,128)(2,1)S(1)} %copy-done.9, bf16[384,1024]{1,0:T(8,128)(2,1)S(1)} %collective-permute-done.3.refs_2_, ...), custom_call_target="tpu_custom_call" | custom-call | flops 1024 | bytes 1024 | tf_op jit(solution)/shard_map/weight_part/pallas_call | solution.py:427
  134.4 3.8 %weight_part.11 = (f32[512,256]{1,0:T(8,128)}, f32[512,256]{1,0:T(8,128)}, f32[512,256]{1,0:T(8,128)S(1)}, f32[512,256]{1,0:T(8,128)S(1)}) custom-call(s32[3]{0:T(128)S(1)} %copy-done.19, bf16[384,1024]{1,0:T(8,128)(2,1)S(1)} %copy-done.2, bf16[192,1024]{1,0:T(8,128)(2,1)} %collective-permute-done.5.refs_12_.refs_1_, ...), custom_call_target="tpu_custom_call" | custom-call | flops 1024 | bytes 1024 | tf_op jit(solution)/shard_map/weight_part/pallas_call | solution.py:427
  143.3 11.6 %collective-permute-done.11.refs_4_ = f32[512,256]{1,0:T(8,128)} collective-permute-done((f32[512,256]{1,0:T(8,128)}, f32[512,256]{1,0:T(8,128)}, u32[]{:S(2)}, u32[]{:S(2)}) %collective-permute-start.11) | collective-permute-done | bytes 524320 | tf_op jit(solution)/shard_map/ppermute | solution.py:515
  160.8 4.5 %collective-permute-done.19.refs_4_ = f32[512,256]{1,0:T(8,128)} collective-permute-done((f32[512,256]{1,0:T(8,128)}, f32[512,256]{1,0:T(8,128)}, u32[]{:S(2)}, u32[]{:S(2)}) %collective-permute-start.19) | collective-permute-done | bytes 524320 | tf_op jit(solution)/shard_map/ppermute | solution.py:515
  168.0 10.4 %collective-permute-done.13.refs_3_ = f32[136,512]{1,0:T(8,128)S(1)} collective-permute-done((f32[136,512]{1,0:T(8,128)S(1)}, f32[136,512]{1,0:T(8,128)S(1)}, u32[]{:S(2)}, u32[]{:S(2)}) %collective-permute-start.13) | collective-permute-done | bytes 278560 | tf_op jit(solution)/shard_map/ppermute | solution.py:515
  178.4 5.1 %collective-permute-done.14.refs_4_ = f32[136,512]{1,0:T(8,128)S(1)} collective-permute-done((f32[136,512]{1,0:T(8,128)S(1)}, f32[136,512]{1,0:T(8,128)S(1)}, u32[]{:S(2)}, u32[]{:S(2)}) %collective-permute-start.14) | collective-permute-done | bytes 278560 | tf_op jit(solution)/shard_map/ppermute | solution.py:515
  189.5 4.8 %collective-permute-done.20.refs_2_ = f32[128,512]{1,0:T(8,128)S(1)} collective-permute-done((f32[128,512]{1,0:T(8,128)S(1)}, f32[128,512]{1,0:T(8,128)S(1)}, u32[]{:S(2)}, u32[]{:S(2)}) %collective-permute-start.20) | collective-permute-done | bytes 262176 | tf_op jit(solution)/shard_map/ppermute | solution.py:515
  195.2 8.4 %collective-permute-done.21.refs_3_ = f32[128,512]{1,0:T(8,128)S(1)} collective-permute-done((f32[128,512]{1,0:T(8,128)S(1)}, f32[128,512]{1,0:T(8,128)S(1)}, u32[]{:S(2)}, u32[]{:S(2)}) %collective-permute-start.21) | collective-permute-done | bytes 262176 | tf_op jit(solution)/shard_map/ppermute | solution.py:515
  203.7 5.1 %collective-permute-done.22.refs_4_ = f32[128,512]{1,0:T(8,128)S(1)} collective-permute-done((f32[128,512]{1,0:T(8,128)S(1)}, f32[128,512]{1,0:T(8,128)S(1)}, u32[]{:S(2)}, u32[]{:S(2)}) %collective-permute-start.22) | collective-permute-done | bytes 262176 | tf_op jit(solution)/shard_map/ppermute | solution.py:515
  212.3 2.4 %unpack.1 = (bf16[384,1024]{1,0:T(8,128)(2,1)}, bf16[384,1024]{1,0:T(8,128)(2,1)}) custom-call(s32[1]{0:T(128)} %bitcast.13.refs_0_, bf16[768,1024]{1,0:T(8,128)(2,1)S(1)} %bitcast.25, s32[768,1]{1,0:T(8,128)S(1)} %copy-done.16), custom_call_target="tpu_custom_call" | custom-call | flops 1024 | bytes 1024 | tf_op jit(solution)/shard_map/unpack/pallas_call | solution.py:530
  215.3 2.6 %collective-permute-done.23.refs_6_ = f32[128,512]{1,0:T(8,128)S(1)} collective-permute-done((f32[128,512]{1,0:T(8,128)S(1)}, f32[128,512]{1,0:T(8,128)S(1)}, u32[]{:S(2)}, u32[]{:S(2)}) %collective-permute-start.23) | collective-permute-done | bytes 262176 | tf_op jit(solution)/shard_map/ppermute | solution.py:515
  218.3 3.4 %collective-permute-done.25.refs_8_ = f32[128,512]{1,0:T(8,128)} collective-permute-done((f32[128,512]{1,0:T(8,128)S(1)}, f32[128,512]{1,0:T(8,128)}, u32[]{:S(2)}, u32[]{:S(2)}) %collective-permute-start.25) | collective-permute-done | bytes 262176 | tf_op jit(solution)/shard_map/ppermute | solution.py:515
  221.7 2.7 %place.1 = (f32[128,3072]{1,0:T(8,128)}, f32[128,1024]{1,0:T(8,128)}) custom-call(s32[1]{0:T(128)} %bitcast.18.refs_0_, f32[136,512]{1,0:T(8,128)S(1)} %block_sum.2.refs_1_, f32[136,512]{1,0:T(8,128)S(1)} %collective-permute-done.15.refs_2_, f32[136,512]{1,0:T(8,128)S(1)} %collective-permute-done.16.refs_3_, f32[136,512]{1,0:T(8,128)} %collective-permute-done.17.refs_4_, ...), custom_call_target="tpu_custom_call" | custom-call | flops 1024 | bytes 1024 | tf_op jit(solution)/shard_map/place/pallas_call | solution.py:530
  (105 shorter events, 47.9 us)
Async XLA Ops:
  4.5 22.9 %all-to-all-start.1 = ((bf16[8,48,1024]{2,1,0:T(8,128)(2,1)}), bf16[8,48,1024]{2,1,0:T(8,128)(2,1)S(1)}, u32[]{:S(2)}, u32[]{:S(2)}) async-start(bf16[8,48,1024]{2,1,0:T(8,128)(2,1)} %bitcast.35), calls=%async_computation.1 | async-start | bytes 1572864 | tf_op jit(solution)/shard_map/all_to_all | solution.py:597
  12.6 56.9 %collective-permute-start = (bf16[384,1024]{1,0:T(8,128)(2,1)}, bf16[384,1024]{1,0:T(8,128)(2,1)S(1)}, u32[]{:S(2)}, u32[]{:S(2)}) collective-permute-start(bf16[384,1024]{1,0:T(8,128)(2,1)} %get-tuple-element.59.refs_2_.refs_3_.refs_0_), channel_id=1, source_target_pairs={{0,1},{1,0},{2,3},{3,2},{4,5},{5,4},{6,7},{7,6},{8,9},{9,8},{10,11... | collective-permute-start | bytes 2359304 | tf_op jit(solution)/shard_map/ppermute | solution.py:515
  14.1 55.9 %collective-permute-start.1 = (bf16[384,1024]{1,0:T(8,128)(2,1)}, bf16[384,1024]{1,0:T(8,128)(2,1)S(1)}, u32[]{:S(2)}, u32[]{:S(2)}) collective-permute-start(bf16[384,1024]{1,0:T(8,128)(2,1)} %get-tuple-element.67), channel_id=1, source_target_pairs={{0,2},{1,3},{2,0},{3,1},{4,6},{5,7},{6,4},{7,5},{8,10},{9,11},{10,... | collective-permute-start | bytes 2359304 | tf_op jit(solution)/shard_map/ppermute | solution.py:515
  27.4 33.7 %all-to-all-start = ((bf16[8,48,1024]{2,1,0:T(8,128)(2,1)}), bf16[8,48,1024]{2,1,0:T(8,128)(2,1)S(1)}, u32[]{:S(2)}, u32[]{:S(2)}) async-start(bf16[8,48,1024]{2,1,0:T(8,128)(2,1)} %bitcast.5), calls=%async_computation | async-start | bytes 1572864 | tf_op jit(solution)/shard_map/all_to_all | solution.py:597
  65.9 38.6 %collective-permute-start.2 = (bf16[192,1024]{1,0:T(8,128)(2,1)}, bf16[192,1024]{1,0:T(8,128)(2,1)S(1)}, u32[]{:S(2)}, u32[]{:S(2)}) collective-permute-start(bf16[192,1024]{1,0:T(8,128)(2,1)} %get-tuple-element.63.refs_2_.refs_3_), channel_id=1, source_target_pairs={{0,1},{1,0},{2,3},{3,2},{4,5},{5,4},{6,7},{7,6},{8,9},{9,8},{10,11... | collective-permute-start | bytes 1179656 | tf_op jit(solution)/shard_map/ppermute | solution.py:515
  67.4 38.7 %collective-permute-start.5 = (bf16[192,1024]{1,0:T(8,128)(2,1)}, bf16[192,1024]{1,0:T(8,128)(2,1)}, u32[]{:S(2)}, u32[]{:S(2)}) collective-permute-start(bf16[192,1024]{1,0:T(8,128)(2,1)} %get-tuple-element.79), channel_id=1, source_target_pairs={{0,2},{1,3},{2,0},{3,1},{4,6},{5,7},{6,4},{7,5},{8,10},{9,11},{10,... | collective-permute-start | bytes 1179656 | tf_op jit(solution)/shard_map/ppermute | solution.py:515
  68.9 37.2 %collective-permute-start.4 = (bf16[576,1024]{1,0:T(8,128)(2,1)}, bf16[576,1024]{1,0:T(8,128)(2,1)}, u32[]{:S(2)}, u32[]{:S(2)}) collective-permute-start(bf16[576,1024]{1,0:T(8,128)(2,1)} %get-tuple-element.76), channel_id=1, source_target_pairs={{0,1},{1,0},{2,3},{3,2},{4,5},{5,4},{6,7},{7,6},{8,9},{9,8},{10,11... | collective-permute-start | bytes 3538952 | tf_op jit(solution)/shard_map/ppermute | solution.py:515
  69.5 36.6 %collective-permute-start.6 = (bf16[576,1024]{1,0:T(8,128)(2,1)}, bf16[576,1024]{1,0:T(8,128)(2,1)}, u32[]{:S(2)}, u32[]{:S(2)}) collective-permute-start(bf16[576,1024]{1,0:T(8,128)(2,1)} %get-tuple-element.80), channel_id=1, source_target_pairs={{0,2},{1,3},{2,0},{3,1},{4,6},{5,7},{6,4},{7,5},{8,10},{9,11},{10,... | collective-permute-start | bytes 3538952 | tf_op jit(solution)/shard_map/ppermute | solution.py:515
  97.8 29.4 %collective-permute-start.9 = (bf16[384,1024]{1,0:T(8,128)(2,1)}, bf16[384,1024]{1,0:T(8,128)(2,1)S(1)}, u32[]{:S(2)}, u32[]{:S(2)}) collective-permute-start(bf16[384,1024]{1,0:T(8,128)(2,1)} %get-tuple-element.89), channel_id=1, source_target_pairs={{0,2},{1,3},{2,0},{3,1},{4,6},{5,7},{6,4},{7,5},{8,10},{9,11},{10,... | collective-permute-start | bytes 2359304 | tf_op jit(solution)/shard_map/ppermute | solution.py:515
  99.4 43.9 %all-to-all-start.2 = ((bf16[8,96,1024]{2,1,0:T(8,128)(2,1)}), bf16[8,96,1024]{2,1,0:T(8,128)(2,1)S(1)}, u32[]{:S(2)}, u32[]{:S(2)}) async-start(bf16[8,96,1024]{2,1,0:T(8,128)(2,1)} %bitcast.27), calls=%async_computation.2 | async-start | bytes 3145728 | tf_op jit(solution)/shard_map/all_to_all | solution.py:719
  104.5 19.7 %collective-permute-start.3 = (bf16[384,1024]{1,0:T(8,128)(2,1)S(1)}, bf16[384,1024]{1,0:T(8,128)(2,1)S(1)}, u32[]{:S(2)}, u32[]{:S(2)}) collective-permute-start(bf16[384,1024]{1,0:T(8,128)(2,1)S(1)} %copy-done.23), channel_id=1, source_target_pairs={{0,1},{1,0},{2,3},{3,2},{4,5},{5,4},{6,7},{7,6},{8,9},{9,8},{10,11... | collective-permute-start | bytes 2359304 | tf_op jit(solution)/shard_map/ppermute | solution.py:515
  133.9 21.0 %collective-permute-start.8 = (f32[520,256]{1,0:T(8,128)}, f32[520,256]{1,0:T(8,128)}, u32[]{:S(2)}, u32[]{:S(2)}) collective-permute-start(f32[520,256]{1,0:T(8,128)} %get-tuple-element.88), channel_id=1, source_target_pairs={{0,2},{1,3},{2,0},{3,1},{4,6},{5,7},{6,4},{7,5},{8,10},{9,11},{10,... | collective-permute-start | bytes 1597448 | tf_op jit(solution)/shard_map/ppermute | solution.py:515
  139.8 15.1 %collective-permute-start.11 = (f32[512,256]{1,0:T(8,128)}, f32[512,256]{1,0:T(8,128)}, u32[]{:S(2)}, u32[]{:S(2)}) collective-permute-start(f32[512,256]{1,0:T(8,128)} %get-tuple-element.92), channel_id=1, source_target_pairs={{0,1},{1,0},{2,3},{3,2},{4,5},{5,4},{6,7},{7,6},{8,9},{9,8},{10,11... | collective-permute-start | bytes 1572872 | tf_op jit(solution)/shard_map/ppermute | solution.py:515
  141.3 24.0 %collective-permute-start.19 = (f32[512,256]{1,0:T(8,128)}, f32[512,256]{1,0:T(8,128)}, u32[]{:S(2)}, u32[]{:S(2)}) collective-permute-start(f32[512,256]{1,0:T(8,128)} %get-tuple-element.100), channel_id=1, source_target_pairs={{0,1},{1,0},{2,3},{3,2},{4,5},{5,4},{6,7},{7,6},{8,9},{9,8},{10,11... | collective-permute-start | bytes 1572872 | tf_op jit(solution)/shard_map/ppermute | solution.py:515
  141.8 23.5 %collective-permute-start.18 = (f32[512,256]{1,0:T(8,128)}, f32[512,256]{1,0:T(8,128)}, u32[]{:S(2)}, u32[]{:S(2)}) collective-permute-start(f32[512,256]{1,0:T(8,128)} %get-tuple-element.98), channel_id=1, source_target_pairs={{0,2},{1,3},{2,0},{3,1},{4,6},{5,7},{6,4},{7,5},{8,10},{9,11},{10,... | collective-permute-start | bytes 1572872 | tf_op jit(solution)/shard_map/ppermute | solution.py:515
  157.3 10.7 %collective-permute-start.12 = (f32[136,512]{1,0:T(8,128)S(1)}, f32[136,512]{1,0:T(8,128)S(1)}, u32[]{:S(2)}, u32[]{:S(2)}) collective-permute-start(f32[136,512]{1,0:T(8,128)S(1)} %get-tuple-element.94), channel_id=1, source_target_pairs={{0,8},{4,12},{8,0},{12,4},{16,24},{20,28},{24,16},{28,20},{1,9},{5... | collective-permute-start | bytes 835592 | tf_op jit(solution)/shard_map/ppermute | solution.py:515
  158.8 19.6 %collective-permute-start.13 = (f32[136,512]{1,0:T(8,128)S(1)}, f32[136,512]{1,0:T(8,128)S(1)}, u32[]{:S(2)}, u32[]{:S(2)}) collective-permute-start(f32[136,512]{1,0:T(8,128)S(1)} %get-tuple-element.95), channel_id=1, source_target_pairs={{0,16},{4,20},{8,24},{12,28},{16,0},{20,4},{24,8},{28,12},{1,17},{... | collective-permute-start | bytes 835592 | tf_op jit(solution)/shard_map/ppermute | solution.py:515
  159.3 24.1 %collective-permute-start.14 = (f32[136,512]{1,0:T(8,128)S(1)}, f32[136,512]{1,0:T(8,128)S(1)}, u32[]{:S(2)}, u32[]{:S(2)}) collective-permute-start(f32[136,512]{1,0:T(8,128)S(1)} %get-tuple-element.96), channel_id=1, source_target_pairs={{0,24},{4,28},{8,16},{12,20},{16,8},{20,12},{24,0},{28,4},{1,25},{... | collective-permute-start | bytes 835592 | tf_op jit(solution)/shard_map/ppermute | solution.py:515
  183.6 26.8 %collective-permute-start.15 = (f32[136,512]{1,0:T(8,128)S(1)}, f32[136,512]{1,0:T(8,128)S(1)}, u32[]{:S(2)}, u32[]{:S(2)}) collective-permute-start(f32[136,512]{1,0:T(8,128)S(1)} %block_sum.2.refs_1_), channel_id=1, source_target_pairs={{0,1},{1,0},{2,3},{3,2},{4,5},{5,4},{6,7},{7,6},{8,9},{9,8},{10,11... | collective-permute-start | bytes 835592 | tf_op jit(solution)/shard_map/ppermute | solution.py:515
  185.1 18.6 %collective-permute-start.21 = (f32[128,512]{1,0:T(8,128)S(1)}, f32[128,512]{1,0:T(8,128)S(1)}, u32[]{:S(2)}, u32[]{:S(2)}) collective-permute-start(f32[128,512]{1,0:T(8,128)S(1)} %get-tuple-element.103), channel_id=1, source_target_pairs={{0,16},{4,20},{8,24},{12,28},{16,0},{20,4},{24,8},{28,12},{1,17},{... | collective-permute-start | bytes 786440 | tf_op jit(solution)/shard_map/ppermute | solution.py:515
  187.1 21.6 %collective-permute-start.22 = (f32[128,512]{1,0:T(8,128)S(1)}, f32[128,512]{1,0:T(8,128)S(1)}, u32[]{:S(2)}, u32[]{:S(2)}) collective-permute-start(f32[128,512]{1,0:T(8,128)S(1)} %get-tuple-element.104), channel_id=1, source_target_pairs={{0,24},{4,28},{8,16},{12,20},{16,8},{20,12},{24,0},{28,4},{1,25},{... | collective-permute-start | bytes 786440 | tf_op jit(solution)/shard_map/ppermute | solution.py:515
  188.6 33.1 %collective-permute-start.16 = (f32[136,512]{1,0:T(8,128)S(1)}, f32[136,512]{1,0:T(8,128)S(1)}, u32[]{:S(2)}, u32[]{:S(2)}) collective-permute-start(f32[136,512]{1,0:T(8,128)S(1)} %block_sum.2.refs_1_), channel_id=1, source_target_pairs={{0,2},{1,3},{2,0},{3,1},{4,6},{5,7},{6,4},{7,5},{8,10},{9,11},{10,... | collective-permute-start | bytes 835592 | tf_op jit(solution)/shard_map/ppermute | solution.py:515
  194.3 27.3 %collective-permute-start.17 = (f32[136,512]{1,0:T(8,128)S(1)}, f32[136,512]{1,0:T(8,128)}, u32[]{:S(2)}, u32[]{:S(2)}) collective-permute-start(f32[136,512]{1,0:T(8,128)S(1)} %block_sum.2.refs_1_), channel_id=1, source_target_pairs={{0,3},{1,2},{2,1},{3,0},{4,7},{5,6},{6,5},{7,4},{8,11},{9,10},{10,... | collective-permute-start | bytes 835592 | tf_op jit(solution)/shard_map/ppermute | solution.py:515
  210.3 11.3 %collective-permute-start.25 = (f32[128,512]{1,0:T(8,128)S(1)}, f32[128,512]{1,0:T(8,128)}, u32[]{:S(2)}, u32[]{:S(2)}) collective-permute-start(f32[128,512]{1,0:T(8,128)S(1)} %block_sum.3.refs_5_), channel_id=1, source_target_pairs={{0,3},{1,2},{2,1},{3,0},{4,7},{5,6},{6,5},{7,4},{8,11},{9,10},{10,... | collective-permute-start | bytes 786440 | tf_op jit(solution)/shard_map/ppermute | solution.py:515
  (29 other events, 226.8 us)

commit v4 on v3

--- a/solution.py
+++ b/solution.py
@@ -130,13 +130,28 @@
     lines, first_chunk, drop, scal_ref, rotation_ref, counts_ref, face_ref, fcot_ref, *refs
 ):
     base = scal_ref[0]
+    wqkv_hbm, wo_hbm = (refs[4:6]) if first_chunk else refs[5:7]
+    wqkv_ref, wo_ref, in_sems, out_sems = refs[-4:]
+    refs = refs[:-4]
+    tile = 512
+
+    def fetch(j):
+        cols = pl.ds(j * tile if isinstance(j, int) else pl.multiple_of(j * tile, tile), tile)
+        return pltpu.make_async_copy(wqkv_hbm.at[:, cols], wqkv_ref.at[:, cols], in_sems.at[j])
+
+    tiles = wqkv_ref.shape[1] // tile
+    fetch_out = pltpu.make_async_copy(wo_hbm, wo_ref, in_sems.at[tiles])
+    for j in range(tiles):
+        fetch(j).start()
+    fetch_out.start()
+    moves = []
     if first_chunk:
-        arrived_ref, index_ref, normed_face_ref, gain_ref, wqkv_ref, wo_ref = refs[:6]
+        arrived_ref, index_ref, normed_face_ref, gain_ref = refs[:4]
         refs = refs[6 + drop :]
         send_a, send_b = refs[4], refs[6]
         g_edge_ref, normed_edge_ref = refs[8:10]
-        z_edge_ref = refs[-1]
-        refs = (*refs[:8], *refs[10:-1])
+        early_ref, z_edge_ref = refs[-2:]
+        refs = (*refs[:8], *refs[10:-2])
         late_rows = refs[3].shape[0]
         edge_rows = z_edge_ref.shape[0]
         edge_kernel(
@@ -150,12 +165,16 @@
             z_edge_ref,
             g_edge_ref,
             normed_edge_ref,
-            send_b.at[pl.ds(late_rows, edge_rows)],
+            early_ref,
         )
-        send_a[late_rows:] = normed_edge_ref[...]
+        for n, (src, dst) in enumerate(((normed_edge_ref, send_a), (early_ref, send_b))):
+            to = dst.at[pl.ds(late_rows, edge_rows)]
+            moves.append(pltpu.make_async_copy(src, to, out_sems.at[4 + n]))
+            moves[-1].start()
     else:
         z_edge_ref, g_edge_ref, normed_edge_ref = refs[:3]
-        normed_face_ref, gain_ref, wqkv_ref, wo_ref, back_index_ref, before_ref = refs[3:9]
+        normed_face_ref, gain_ref = refs[3:5]
+        back_index_ref, before_ref = refs[7:9]
         refs = refs[9 + drop :]
     (
         face_out,
@@ -196,12 +215,13 @@
     norm_s[:faces] = normed_face_ref[...]
     norm_s[faces:] = normed_edge_ref[...]
 
-    tile = 512
-
-    @pl.loop(0, 3 * width // tile)
+    @pl.loop(0, tiles)
     def _(j):
         cols = pl.ds(pl.multiple_of(j * tile, tile), tile)
+        fetch(j).wait()
         qkv_s[:, cols] = nn(norm_s[...], wqkv_ref[:, cols]).astype(BF)
+
+    fetch_out.wait()
 
     @pl.loop(0, width // tile)
     def _(j):
@@ -235,7 +255,7 @@
             k2 = split(load(qkv_s, width + at))
             v2 = split(load(qkv_s, 2 * width + at))
             dm = load(dm_s, at)
-            scores = nt(k2, q) * scale
+            scores = nt(k2, q * jnp.asarray(scale, BF))
             d_probs = nt(v2, dm)
             probs_b, d_scores = [], []
             for h in range(2):
@@ -246,15 +266,35 @@
                 d = d_probs[part]
                 inner = jnp.sum(probs * d, axis=0, keepdims=True)
                 probs_b.append(probs.astype(BF))
-                d_scores.append((probs * (d - inner) * scale).astype(BF))
+                d_scores.append((probs * (d - inner)).astype(BF))
             pb = jnp.concatenate(probs_b, axis=0)
             ds = jnp.concatenate(d_scores, axis=0)
             store(mix_s, at, tn(pb, v2))
             dv = nn(pb, dm)
             store(stk_s, 2 * width + at, jnp.where(low, dv[:length], dv[length:]))
-            store(stk_s, at, tn(ds, k2))
+            store(stk_s, at, tn(ds, k2) * scale)
             dk = nn(ds, q)
-            store(stk_s, width + at, jnp.where(low, dk[:length], dk[length:]))
+            store(stk_s, width + at, jnp.where(low, dk[:length], dk[length:]) * scale)
+
+    total_rows = z_s.shape[0]
+    targets = (keep_a, send_a, keep_b, send_b)
+    third = [stk_s.at[:, pl.ds(n * width, width)] for n in range(3)]
+    sources = (third[0], third[1], third[2], mix_s)
+
+    def ship(at, order):
+        for n, src in enumerate(order):
+            dst = targets[at + n].at[pl.ds(0, total_rows)]
+            pltpu.make_async_copy(sources[src], dst, out_sems.at[at + n]).start()
+
+    for at, bit in ((0, scal_ref[1]), (2, scal_ref[2])):
+
+        @pl.when(bit == 0)
+        def _(at=at):
+            ship(at, (at, at + 1))
+
+        @pl.when(bit != 0)
+        def _(at=at):
+            ship(at, (at + 1, at))
 
     @pl.loop(0, width // tile)
     def _(j):
@@ -301,29 +341,10 @@
         )
         back_ref[...] = nn(picked, edge_s[...]).astype(BF)
 
-    total_rows = z_s.shape[0]
-    x_bit = scal_ref[1]
-    y_bit = scal_ref[2]
-
-    @pl.when(x_bit == 0)
-    def _():
-        keep_a[...] = stk_s[:, :width]
-        send_a[:total_rows] = stk_s[:, width : 2 * width]
-
-    @pl.when(x_bit != 0)
-    def _():
-        send_a[:total_rows] = stk_s[:, :width]
-        keep_a[...] = stk_s[:, width : 2 * width]
-
-    @pl.when(y_bit == 0)
-    def _():
-        keep_b[...] = stk_s[:, 2 * width :]
-        send_b[:total_rows] = mix_s[...]
-
-    @pl.when(y_bit != 0)
-    def _():
-        send_b[:total_rows] = stk_s[:, 2 * width :]
-        keep_b[...] = mix_s[...]
+    for n, dst in enumerate(targets):
+        pltpu.make_async_copy(sources[n], dst.at[pl.ds(0, total_rows)], out_sems.at[n]).wait()
+    for move in moves:
+        move.wait()
 
 
 def weight_kernel(runs, parities, blocks, count, adds, gains, halved, scal_ref, *refs):
@@ -660,7 +681,13 @@
             operands += [face_normed, gain, qkv_weight, out_weight, back_index, results[0][0]]
             tail = [*faces, got_face_a, got_face_b]
         in_specs = [
-            face_spec if n < 2 else normed_spec if o is face_normed else full(o.shape)
+            face_spec
+            if n < 2
+            else normed_spec
+            if o is face_normed
+            else pl.BlockSpec(memory_space=pl.ANY)
+            if o is qkv_weight or o is out_weight
+            else full(o.shape)
             for n, o in enumerate(operands)
         ]
         in_specs += [pl.BlockSpec(memory_space=pl.ANY)] * len(tail)
@@ -676,7 +703,7 @@
                 grid=(1,),
                 in_specs=in_specs,
                 out_specs=[face_spec, face_spec, full((back_rows, width))]
-                + [full(row_shape), full(send_shape)] * 2
+                + [pl.BlockSpec(memory_space=pl.ANY)] * 4
                 + [full((8, width // 8))]
                 + [full(e) for e in edge_outs],
                 scratch_shapes=[
@@ -691,7 +718,13 @@
                     pltpu.VMEM(row_shape, BF),
                     pltpu.VMEM((2 * edges * (c + 1), width), BF),
                 ]
-                + ([pltpu.VMEM((edges, width), BF)] if c == 0 else []),
+                + ([pltpu.VMEM((edges, width), BF)] * 2 if c == 0 else [])
+                + [
+                    pltpu.VMEM(qkv_weight.shape, BF),
+                    pltpu.VMEM(out_weight.shape, BF),
+                    pltpu.SemaphoreType.DMA((3 * width // 512 + 1,)),
+                    pltpu.SemaphoreType.DMA((6,)),
+                ],
             ),
             out_shape=[struct(*face_tokens.shape)] * 2
             + [struct(back_rows, width)]

time: 225 us -> 219 us (0.973)
  Pallas kernels: 99.6 us -> 93.4 us
    pallas_call x2, Pallas kernels: 53.9 us -> 48 us  [local(): pl.pallas_call(functools.partial(layer_kernel, lines, c == 0, len(tail)),...]
  transfers between devices with their start and end apart: 29 -> 29, of which waited for: 14 -> 13; matrix products, arithmetic and copies ran while one was open for 1% -> 1% of each run, Pallas kernels for 41% -> 40%
where the time goes in v4:
time: 219 us
  Pallas kernels  93.4 us (43%)
  waiting for transfers between devices  69.3 us (32%)
  starting transfers between devices  46.1 us (21%)
  local copies, waits for them, and re-layouts  6.62 us (3%)
  other arithmetic  2.49 us (1%)
    ppermute x26, waiting for transfers between devices, exchange(): return lax.ppermute(x, axis, [(i, i ^ bits) for i in range(size)])  59.9 us
    pallas_call x2, Pallas kernels, local(): pl.pallas_call(functools.partial(layer_kernel, lines, c == 0, len(tail)),...  48 us
    ppermute x26, starting transfers between devices, exchange(): return lax.ppermute(x, axis, [(i, i ^ bits) for i in range(size)])  29 us
    pallas_call x6, Pallas kernels, weight_part(): pl.pallas_call(kernel, grid_spec=pltpu.PrefetchScalarGridSpec(num_scalar_...  27 us
    pallas_call x9, Pallas kernels, whole_call(): pl.pallas_call(body, grid_spec=pltpu.PrefetchScalarGridSpec(num_scalar_pr...  18.4 us
    all_to_all x2, starting transfers between devices, local(): lax.all_to_all(s, 'tile', split_axis=0, concat_axis=0, tiled=True)  12 us
    all_to_all x2, waiting for transfers between devices, local(): lax.all_to_all(s, 'tile', split_axis=0, concat_axis=0, tiled=True)  9.37 us
    unnamed x48, local copies, waits for them, and re-layouts  6.04 us
  transfers between devices with their start and end apart: 29, of which 13 were waited for; matrix products, arithmetic and copies ran while one was open for 1% of the time, Pallas kernels for 40%

profile of v4, /device:TPU:16, one launch (start us, length us, event | category | flops | bytes accessed | tf_op | source)
XLA Modules:
  0.0 218.7 jit_solution(17672966692551047607)
XLA Ops:
  0.7 3.8 %pack.1 = (bf16[384,1024]{1,0:T(8,128)(2,1)}, bf16[384,1024]{1,0:T(8,128)(2,1)}) custom-call(s32[1]{0:T(128)} %bitcast.2.refs_0_, bf16[384,1024]{1,0:T(8,128)(2,1)} %bitcast.28, bf16[384,1024]{1,0:T(8,128)(2,1)} %bitcast.29, s32[768,1]{1,0:T(8,128)} %constant.68.clone.refs_3_), custom_call_target="tpu_custom_call" | custom-call | flops 1024 | bytes 1024 | tf_op jit(solution)/shard_map/pack/pallas_call | solution.py:551
  4.5 5.2 %all-to-all-start.1 = ((bf16[8,48,1024]{2,1,0:T(8,128)(2,1)}), bf16[8,48,1024]{2,1,0:T(8,128)(2,1)S(1)}, u32[]{:S(2)}, u32[]{:S(2)}) async-start(bf16[8,48,1024]{2,1,0:T(8,128)(2,1)} %bitcast.35), calls=%async_computation.1 | async-start | bytes 1572864 | tf_op jit(solution)/shard_map/all_to_all | solution.py:618
  9.7 2.8 %face_norm.1 = (bf16[384,1024]{1,0:T(8,128)(2,1)}, bf16[384,1024]{1,0:T(8,128)(2,1)}) custom-call(s32[1]{0:T(128)} %bitcast.2.refs_0_, bf16[384,1024]{1,0:T(8,128)(2,1)} %bitcast.30, bf16[384,1024]{1,0:T(8,128)(2,1)} %bitcast.31, f32[1,1024]{1,0:T(1,128)} %bitcast.36), custom_call_target="tpu_custom_call" | custom-call | flops 1024 | bytes 1024 | tf_op jit(solution)/shard_map/face_norm/pallas_call | solution.py:551
  18.1 9.4 %all-to-all-done.1 = bf16[8,48,1024]{2,1,0:T(8,128)(2,1)S(1)} async-done(((bf16[8,48,1024]{2,1,0:T(8,128)(2,1)}), bf16[8,48,1024]{2,1,0:T(8,128)(2,1)S(1)}, u32[]{:S(2)}, u32[]{:S(2)}) %all-to-all-start.1) | async-done | bytes 786464 | tf_op jit(solution)/shard_map/all_to_all | solution.py:618
  27.4 6.7 %all-to-all-start = ((bf16[8,48,1024]{2,1,0:T(8,128)(2,1)}), bf16[8,48,1024]{2,1,0:T(8,128)(2,1)S(1)}, u32[]{:S(2)}, u32[]{:S(2)}) async-start(bf16[8,48,1024]{2,1,0:T(8,128)(2,1)} %bitcast.5), calls=%async_computation | async-start | bytes 1572864 | tf_op jit(solution)/shard_map/all_to_all | solution.py:618
  34.2 23.5 %layer.2 = (bf16[1,6,64,1024]{3,2,1,0:T(8,128)(2,1)}, bf16[1,6,64,1024]{3,2,1,0:T(8,128)(2,1)}, bf16[384,1024]{1,0:T(8,128)(2,1)}, bf16[384,1024]{1,0:T(8,128)(2...) custom-call(s32[3]{0:T(128)} %add_add_fusion.1.scal_ref, ...), custom_call_target="tpu_custom_call" | custom-call | flops 34359738368 | bytes 1048576 | tf_op jit(solution)/shard_map/layer/pallas_call | solution.py:699
  58.6 3.9 %edge_norm.1 = (bf16[192,1024]{1,0:T(8,128)(2,1)}, bf16[192,1024]{1,0:T(8,128)(2,1)}, bf16[192,1024]{1,0:T(8,128)(2,1)}, bf16[192,1024]{1,0:T(8,128)(2,1)}) custom-call(s32[3]{0:T(128)} %add_add_fusion.refs_0_.scal_ref, s32[48]{0:T(128)} %rotation_ref.3, s32[48]{0:T(128)} %counts_ref.3, bf16[384,1024]{1,0:T(8,128)(2,1)} %bitcast.26, ...), custom_call_target="tpu_custom_call" | custom-call | flops 1024 | bytes 1024 | tf_op jit(solution)/shard_map/edge_norm/pallas_call | solution.py:551
  67.4 24.5 %layer.3 = (bf16[1,6,64,1024]{3,2,1,0:T(8,128)(2,1)}, bf16[1,6,64,1024]{3,2,1,0:T(8,128)(2,1)}, bf16[768,1024]{1,0:T(8,128)(2,1)}, bf16[384,1024]{1,0:T(8,128)(2...) custom-call(s32[3]{0:T(128)} %add_add_fusion.refs_0_.scal_ref, ...), custom_call_target="tpu_custom_call", output_to_operand_aliasing={{0}: (14, {}), {1}: (15, {})} | custom-call | flops 34359738368 | bytes 1048576 | tf_op jit(solution)/shard_map/layer/pallas_call | solution.py:699
  93.5 5.1 %all-to-all-start.2 = ((bf16[8,96,1024]{2,1,0:T(8,128)(2,1)}), bf16[8,96,1024]{2,1,0:T(8,128)(2,1)S(1)}, u32[]{:S(2)}, u32[]{:S(2)}) async-start(bf16[8,96,1024]{2,1,0:T(8,128)(2,1)} %bitcast.27), calls=%async_computation.2 | async-start | bytes 3145728 | tf_op jit(solution)/shard_map/all_to_all | solution.py:752
  101.5 8.5 %weight_part.7 = (f32[512,1024]{1,0:T(8,128)}, f32[512,1024]{1,0:T(8,128)}) custom-call(s32[3]{0:T(128)} %pad_add_fusion.1.scal_ref, bf16[384,1024]{1,0:T(8,128)(2,1)} %get-tuple-element.59.refs_2_.refs_3_.refs_0_, bf16[384,1024]{1,0:T(8,128)(2,1)} %bitcast.32, bf16[192,1024]{1,0:T(8,128)(2,1)} %get-tuple-element.74.refs_2_, ...), custom_call_target="tpu_custom_call" | custom-call | flops 8589934592 | bytes 1024 | tf_op jit(solution)/shard_map/weight_part/pallas_call | solution.py:448
  110.1 8.7 %weight_part.6 = (f32[512,1024]{1,0:T(8,128)}, f32[512,1024]{1,0:T(8,128)}) custom-call(s32[3]{0:T(128)} %pad_add_fusion.scal_ref, bf16[384,1024]{1,0:T(8,128)(2,1)} %get-tuple-element.59.refs_2_.refs_3_.refs_0_, bf16[384,1024]{1,0:T(8,128)(2,1)} %bitcast.33, bf16[192,1024]{1,0:T(8,128)(2,1)} %get-tuple-element.74.refs_2_, ...), custom_call_target="tpu_custom_call" | custom-call | flops 8589934592 | bytes 1024 | tf_op jit(solution)/shard_map/weight_part/pallas_call | solution.py:448
  121.9 2.5 %weight_part.10 = f32[512,1024]{1,0:T(8,128)S(1)} custom-call(s32[3]{0:T(128)S(1)} %copy-done.19, bf16[384,1024]{1,0:T(8,128)(2,1)S(1)} %copy-done.2, bf16[192,1024]{1,0:T(8,128)(2,1)} %collective-permute-done.5.refs_12_.refs_1_, bf16[384,1024]{1,0:T(8,128)(2,1)S(1)} %collective-permute-done.9.refs_2_, f32[512,1024]{1,0:T(8,128)S(1)} %copy-done), custom_call_target="tpu_custom_call" | custom-call | flops 1024 | bytes 1024 | tf_op jit(solution)/shard_map/weight_part/pallas_call | solution.py:448
  126.1 2.5 %weight_part.9 = (f32[520,256]{1,0:T(8,128)}, f32[512,256]{1,0:T(8,128)}, f32[520,256]{1,0:T(8,128)S(1)}, f32[512,256]{1,0:T(8,128)S(1)}) custom-call(s32[3]{0:T(128)S(1)} %copy-done.20, bf16[384,1024]{1,0:T(8,128)(2,1)S(1)} %copy-done.4, bf16[192,1024]{1,0:T(8,128)(2,1)S(1)} %copy-done.9, bf16[384,1024]{1,0:T(8,128)(2,1)S(1)} %collective-permute-done.3.refs_2_, ...), custom_call_target="tpu_custom_call" | custom-call | flops 1024 | bytes 1024 | tf_op jit(solution)/shard_map/weight_part/pallas_call | solution.py:448
  130.1 3.5 %weight_part.11 = (f32[512,256]{1,0:T(8,128)}, f32[512,256]{1,0:T(8,128)}, f32[512,256]{1,0:T(8,128)S(1)}, f32[512,256]{1,0:T(8,128)S(1)}) custom-call(s32[3]{0:T(128)S(1)} %copy-done.19, bf16[384,1024]{1,0:T(8,128)(2,1)S(1)} %copy-done.2, bf16[192,1024]{1,0:T(8,128)(2,1)} %collective-permute-done.5.refs_12_.refs_1_, ...), custom_call_target="tpu_custom_call" | custom-call | flops 1024 | bytes 1024 | tf_op jit(solution)/shard_map/weight_part/pallas_call | solution.py:448
  137.7 12.6 %collective-permute-done.11.refs_4_ = f32[512,256]{1,0:T(8,128)} collective-permute-done((f32[512,256]{1,0:T(8,128)}, f32[512,256]{1,0:T(8,128)}, u32[]{:S(2)}, u32[]{:S(2)}) %collective-permute-start.11) | collective-permute-done | bytes 524320 | tf_op jit(solution)/shard_map/ppermute | solution.py:536
  156.3 4.2 %collective-permute-done.19.refs_4_ = f32[512,256]{1,0:T(8,128)} collective-permute-done((f32[512,256]{1,0:T(8,128)}, f32[512,256]{1,0:T(8,128)}, u32[]{:S(2)}, u32[]{:S(2)}) %collective-permute-start.19) | collective-permute-done | bytes 524320 | tf_op jit(solution)/shard_map/ppermute | solution.py:536
  163.4 9.9 %collective-permute-done.13.refs_3_ = f32[136,512]{1,0:T(8,128)S(1)} collective-permute-done((f32[136,512]{1,0:T(8,128)S(1)}, f32[136,512]{1,0:T(8,128)S(1)}, u32[]{:S(2)}, u32[]{:S(2)}) %collective-permute-start.13) | collective-permute-done | bytes 278560 | tf_op jit(solution)/shard_map/ppermute | solution.py:536
  173.4 4.9 %collective-permute-done.14.refs_4_ = f32[136,512]{1,0:T(8,128)S(1)} collective-permute-done((f32[136,512]{1,0:T(8,128)S(1)}, f32[136,512]{1,0:T(8,128)S(1)}, u32[]{:S(2)}, u32[]{:S(2)}) %collective-permute-start.14) | collective-permute-done | bytes 278560 | tf_op jit(solution)/shard_map/ppermute | solution.py:536
  183.3 4.8 %collective-permute-done.20.refs_2_ = f32[128,512]{1,0:T(8,128)S(1)} collective-permute-done((f32[128,512]{1,0:T(8,128)S(1)}, f32[128,512]{1,0:T(8,128)S(1)}, u32[]{:S(2)}, u32[]{:S(2)}) %collective-permute-start.20) | collective-permute-done | bytes 262176 | tf_op jit(solution)/shard_map/ppermute | solution.py:536
  190.2 7.1 %collective-permute-done.21.refs_3_ = f32[128,512]{1,0:T(8,128)S(1)} collective-permute-done((f32[128,512]{1,0:T(8,128)S(1)}, f32[128,512]{1,0:T(8,128)S(1)}, u32[]{:S(2)}, u32[]{:S(2)}) %collective-permute-start.21) | collective-permute-done | bytes 262176 | tf_op jit(solution)/shard_map/ppermute | solution.py:536
  197.4 5.2 %collective-permute-done.22.refs_4_ = f32[128,512]{1,0:T(8,128)S(1)} collective-permute-done((f32[128,512]{1,0:T(8,128)S(1)}, f32[128,512]{1,0:T(8,128)S(1)}, u32[]{:S(2)}, u32[]{:S(2)}) %collective-permute-start.22) | collective-permute-done | bytes 262176 | tf_op jit(solution)/shard_map/ppermute | solution.py:536
  209.2 2.8 %collective-permute-done.23.refs_6_ = f32[128,512]{1,0:T(8,128)S(1)} collective-permute-done((f32[128,512]{1,0:T(8,128)S(1)}, f32[128,512]{1,0:T(8,128)S(1)}, u32[]{:S(2)}, u32[]{:S(2)}) %collective-permute-start.23) | collective-permute-done | bytes 262176 | tf_op jit(solution)/shard_map/ppermute | solution.py:536
  211.9 4.1 %collective-permute-done.24.refs_7_ = f32[128,512]{1,0:T(8,128)} collective-permute-done((f32[128,512]{1,0:T(8,128)S(1)}, f32[128,512]{1,0:T(8,128)}, u32[]{:S(2)}, u32[]{:S(2)}) %collective-permute-start.24) | collective-permute-done | bytes 262176 | tf_op jit(solution)/shard_map/ppermute | solution.py:536
  216.1 2.7 %place.1 = (f32[128,3072]{1,0:T(8,128)}, f32[128,1024]{1,0:T(8,128)}) custom-call(s32[1]{0:T(128)} %bitcast.18.refs_0_, f32[136,512]{1,0:T(8,128)S(1)} %block_sum.2.refs_1_, f32[136,512]{1,0:T(8,128)S(1)} %collective-permute-done.15.refs_2_, f32[136,512]{1,0:T(8,128)S(1)} %collective-permute-done.16.refs_3_, f32[136,512]{1,0:T(8,128)} %collective-permute-done.17.refs_4_, ...), custom_call_target="tpu_custom_call" | custom-call | flops 1024 | bytes 1024 | tf_op jit(solution)/shard_map/place/pallas_call | solution.py:551
  (105 shorter events, 48.7 us)
Async XLA Ops:
  4.5 22.9 %all-to-all-start.1 = ((bf16[8,48,1024]{2,1,0:T(8,128)(2,1)}), bf16[8,48,1024]{2,1,0:T(8,128)(2,1)S(1)}, u32[]{:S(2)}, u32[]{:S(2)}) async-start(bf16[8,48,1024]{2,1,0:T(8,128)(2,1)} %bitcast.35), calls=%async_computation.1 | async-start | bytes 1572864 | tf_op jit(solution)/shard_map/all_to_all | solution.py:618
  12.6 53.4 %collective-permute-start = (bf16[384,1024]{1,0:T(8,128)(2,1)}, bf16[384,1024]{1,0:T(8,128)(2,1)S(1)}, u32[]{:S(2)}, u32[]{:S(2)}) collective-permute-start(bf16[384,1024]{1,0:T(8,128)(2,1)} %get-tuple-element.59.refs_2_.refs_3_.refs_0_), channel_id=1, source_target_pairs={{0,1},{1,0},{2,3},{3,2},{4,5},{5,4},{6,7},{7,6},{8,9},{9,8},{10,11... | collective-permute-start | bytes 2359304 | tf_op jit(solution)/shard_map/ppermute | solution.py:536
  14.1 52.5 %collective-permute-start.1 = (bf16[384,1024]{1,0:T(8,128)(2,1)}, bf16[384,1024]{1,0:T(8,128)(2,1)S(1)}, u32[]{:S(2)}, u32[]{:S(2)}) collective-permute-start(bf16[384,1024]{1,0:T(8,128)(2,1)} %get-tuple-element.67), channel_id=1, source_target_pairs={{0,2},{1,3},{2,0},{3,1},{4,6},{5,7},{6,4},{7,5},{8,10},{9,11},{10,... | collective-permute-start | bytes 2359304 | tf_op jit(solution)/shard_map/ppermute | solution.py:536
  27.4 30.3 %all-to-all-start = ((bf16[8,48,1024]{2,1,0:T(8,128)(2,1)}), bf16[8,48,1024]{2,1,0:T(8,128)(2,1)S(1)}, u32[]{:S(2)}, u32[]{:S(2)}) async-start(bf16[8,48,1024]{2,1,0:T(8,128)(2,1)} %bitcast.5), calls=%async_computation | async-start | bytes 1572864 | tf_op jit(solution)/shard_map/all_to_all | solution.py:618
  62.4 36.2 %collective-permute-start.2 = (bf16[192,1024]{1,0:T(8,128)(2,1)}, bf16[192,1024]{1,0:T(8,128)(2,1)S(1)}, u32[]{:S(2)}, u32[]{:S(2)}) collective-permute-start(bf16[192,1024]{1,0:T(8,128)(2,1)} %get-tuple-element.63.refs_2_.refs_3_), channel_id=1, source_target_pairs={{0,1},{1,0},{2,3},{3,2},{4,5},{5,4},{6,7},{7,6},{8,9},{9,8},{10,11... | collective-permute-start | bytes 1179656 | tf_op jit(solution)/shard_map/ppermute | solution.py:536
  63.9 36.3 %collective-permute-start.5 = (bf16[192,1024]{1,0:T(8,128)(2,1)}, bf16[192,1024]{1,0:T(8,128)(2,1)}, u32[]{:S(2)}, u32[]{:S(2)}) collective-permute-start(bf16[192,1024]{1,0:T(8,128)(2,1)} %get-tuple-element.79), channel_id=1, source_target_pairs={{0,2},{1,3},{2,0},{3,1},{4,6},{5,7},{6,4},{7,5},{8,10},{9,11},{10,... | collective-permute-start | bytes 1179656 | tf_op jit(solution)/shard_map/ppermute | solution.py:536
  65.5 34.7 %collective-permute-start.4 = (bf16[576,1024]{1,0:T(8,128)(2,1)}, bf16[576,1024]{1,0:T(8,128)(2,1)}, u32[]{:S(2)}, u32[]{:S(2)}) collective-permute-start(bf16[576,1024]{1,0:T(8,128)(2,1)} %get-tuple-element.76), channel_id=1, source_target_pairs={{0,1},{1,0},{2,3},{3,2},{4,5},{5,4},{6,7},{7,6},{8,9},{9,8},{10,11... | collective-permute-start | bytes 3538952 | tf_op jit(solution)/shard_map/ppermute | solution.py:536
  66.0 35.5 %collective-permute-start.6 = (bf16[576,1024]{1,0:T(8,128)(2,1)}, bf16[576,1024]{1,0:T(8,128)(2,1)}, u32[]{:S(2)}, u32[]{:S(2)}) collective-permute-start(bf16[576,1024]{1,0:T(8,128)(2,1)} %get-tuple-element.80), channel_id=1, source_target_pairs={{0,2},{1,3},{2,0},{3,1},{4,6},{5,7},{6,4},{7,5},{8,10},{9,11},{10,... | collective-permute-start | bytes 3538952 | tf_op jit(solution)/shard_map/ppermute | solution.py:536
  91.9 30.0 %collective-permute-start.9 = (bf16[384,1024]{1,0:T(8,128)(2,1)}, bf16[384,1024]{1,0:T(8,128)(2,1)S(1)}, u32[]{:S(2)}, u32[]{:S(2)}) collective-permute-start(bf16[384,1024]{1,0:T(8,128)(2,1)} %get-tuple-element.89), channel_id=1, source_target_pairs={{0,2},{1,3},{2,0},{3,1},{4,6},{5,7},{6,4},{7,5},{8,10},{9,11},{10,... | collective-permute-start | bytes 2359304 | tf_op jit(solution)/shard_map/ppermute | solution.py:536
  93.5 44.2 %all-to-all-start.2 = ((bf16[8,96,1024]{2,1,0:T(8,128)(2,1)}), bf16[8,96,1024]{2,1,0:T(8,128)(2,1)S(1)}, u32[]{:S(2)}, u32[]{:S(2)}) async-start(bf16[8,96,1024]{2,1,0:T(8,128)(2,1)} %bitcast.27), calls=%async_computation.2 | async-start | bytes 3145728 | tf_op jit(solution)/shard_map/all_to_all | solution.py:752
  98.6 20.2 %collective-permute-start.3 = (bf16[384,1024]{1,0:T(8,128)(2,1)S(1)}, bf16[384,1024]{1,0:T(8,128)(2,1)S(1)}, u32[]{:S(2)}, u32[]{:S(2)}) collective-permute-start(bf16[384,1024]{1,0:T(8,128)(2,1)S(1)} %copy-done.23), channel_id=1, source_target_pairs={{0,1},{1,0},{2,3},{3,2},{4,5},{5,4},{6,7},{7,6},{8,9},{9,8},{10,11... | collective-permute-start | bytes 2359304 | tf_op jit(solution)/shard_map/ppermute | solution.py:536
  128.6 21.8 %collective-permute-start.8 = (f32[520,256]{1,0:T(8,128)}, f32[520,256]{1,0:T(8,128)}, u32[]{:S(2)}, u32[]{:S(2)}) collective-permute-start(f32[520,256]{1,0:T(8,128)} %get-tuple-element.88), channel_id=1, source_target_pairs={{0,2},{1,3},{2,0},{3,1},{4,6},{5,7},{6,4},{7,5},{8,10},{9,11},{10,... | collective-permute-start | bytes 1597448 | tf_op jit(solution)/shard_map/ppermute | solution.py:536
  135.2 15.1 %collective-permute-start.11 = (f32[512,256]{1,0:T(8,128)}, f32[512,256]{1,0:T(8,128)}, u32[]{:S(2)}, u32[]{:S(2)}) collective-permute-start(f32[512,256]{1,0:T(8,128)} %get-tuple-element.92), channel_id=1, source_target_pairs={{0,1},{1,0},{2,3},{3,2},{4,5},{5,4},{6,7},{7,6},{8,9},{9,8},{10,11... | collective-permute-start | bytes 1572872 | tf_op jit(solution)/shard_map/ppermute | solution.py:536
  135.7 24.7 %collective-permute-start.19 = (f32[512,256]{1,0:T(8,128)}, f32[512,256]{1,0:T(8,128)}, u32[]{:S(2)}, u32[]{:S(2)}) collective-permute-start(f32[512,256]{1,0:T(8,128)} %get-tuple-element.100), channel_id=1, source_target_pairs={{0,1},{1,0},{2,3},{3,2},{4,5},{5,4},{6,7},{7,6},{8,9},{9,8},{10,11... | collective-permute-start | bytes 1572872 | tf_op jit(solution)/shard_map/ppermute | solution.py:536
  137.2 23.2 %collective-permute-start.18 = (f32[512,256]{1,0:T(8,128)}, f32[512,256]{1,0:T(8,128)}, u32[]{:S(2)}, u32[]{:S(2)}) collective-permute-start(f32[512,256]{1,0:T(8,128)} %get-tuple-element.98), channel_id=1, source_target_pairs={{0,2},{1,3},{2,0},{3,1},{4,6},{5,7},{6,4},{7,5},{8,10},{9,11},{10,... | collective-permute-start | bytes 1572872 | tf_op jit(solution)/shard_map/ppermute | solution.py:536
  154.2 19.1 %collective-permute-start.13 = (f32[136,512]{1,0:T(8,128)S(1)}, f32[136,512]{1,0:T(8,128)S(1)}, u32[]{:S(2)}, u32[]{:S(2)}) collective-permute-start(f32[136,512]{1,0:T(8,128)S(1)} %get-tuple-element.95), channel_id=1, source_target_pairs={{0,16},{4,20},{8,24},{12,28},{16,0},{20,4},{24,8},{28,12},{1,17},{... | collective-permute-start | bytes 835592 | tf_op jit(solution)/shard_map/ppermute | solution.py:536
  154.8 23.5 %collective-permute-start.14 = (f32[136,512]{1,0:T(8,128)S(1)}, f32[136,512]{1,0:T(8,128)S(1)}, u32[]{:S(2)}, u32[]{:S(2)}) collective-permute-start(f32[136,512]{1,0:T(8,128)S(1)} %get-tuple-element.96), channel_id=1, source_target_pairs={{0,24},{4,28},{8,16},{12,20},{16,8},{20,12},{24,0},{28,4},{1,25},{... | collective-permute-start | bytes 835592 | tf_op jit(solution)/shard_map/ppermute | solution.py:536
  178.4 26.9 %collective-permute-start.15 = (f32[136,512]{1,0:T(8,128)S(1)}, f32[136,512]{1,0:T(8,128)S(1)}, u32[]{:S(2)}, u32[]{:S(2)}) collective-permute-start(f32[136,512]{1,0:T(8,128)S(1)} %block_sum.2.refs_1_), channel_id=1, source_target_pairs={{0,1},{1,0},{2,3},{3,2},{4,5},{5,4},{6,7},{7,6},{8,9},{9,8},{10,11... | collective-permute-start | bytes 835592 | tf_op jit(solution)/shard_map/ppermute | solution.py:536
  179.0 18.4 %collective-permute-start.21 = (f32[128,512]{1,0:T(8,128)S(1)}, f32[128,512]{1,0:T(8,128)S(1)}, u32[]{:S(2)}, u32[]{:S(2)}) collective-permute-start(f32[128,512]{1,0:T(8,128)S(1)} %get-tuple-element.103), channel_id=1, source_target_pairs={{0,16},{4,20},{8,24},{12,28},{16,0},{20,4},{24,8},{28,12},{1,17},{... | collective-permute-start | bytes 786440 | tf_op jit(solution)/shard_map/ppermute | solution.py:536
  181.0 21.6 %collective-permute-start.22 = (f32[128,512]{1,0:T(8,128)S(1)}, f32[128,512]{1,0:T(8,128)S(1)}, u32[]{:S(2)}, u32[]{:S(2)}) collective-permute-start(f32[128,512]{1,0:T(8,128)S(1)} %get-tuple-element.104), channel_id=1, source_target_pairs={{0,24},{4,28},{8,16},{12,20},{16,8},{20,12},{24,0},{28,4},{1,25},{... | collective-permute-start | bytes 786440 | tf_op jit(solution)/shard_map/ppermute | solution.py:536
  182.4 33.6 %collective-permute-start.16 = (f32[136,512]{1,0:T(8,128)S(1)}, f32[136,512]{1,0:T(8,128)S(1)}, u32[]{:S(2)}, u32[]{:S(2)}) collective-permute-start(f32[136,512]{1,0:T(8,128)S(1)} %block_sum.2.refs_1_), channel_id=1, source_target_pairs={{0,2},{1,3},{2,0},{3,1},{4,6},{5,7},{6,4},{7,5},{8,10},{9,11},{10,... | collective-permute-start | bytes 835592 | tf_op jit(solution)/shard_map/ppermute | solution.py:536
  188.2 27.9 %collective-permute-start.17 = (f32[136,512]{1,0:T(8,128)S(1)}, f32[136,512]{1,0:T(8,128)}, u32[]{:S(2)}, u32[]{:S(2)}) collective-permute-start(f32[136,512]{1,0:T(8,128)S(1)} %block_sum.2.refs_1_), channel_id=1, source_target_pairs={{0,3},{1,2},{2,1},{3,0},{4,7},{5,6},{6,5},{7,4},{8,11},{9,10},{10,... | collective-permute-start | bytes 835592 | tf_op jit(solution)/shard_map/ppermute | solution.py:536
  204.2 11.8 %collective-permute-start.24 = (f32[128,512]{1,0:T(8,128)S(1)}, f32[128,512]{1,0:T(8,128)}, u32[]{:S(2)}, u32[]{:S(2)}) collective-permute-start(f32[128,512]{1,0:T(8,128)S(1)} %block_sum.3.refs_5_), channel_id=1, source_target_pairs={{0,2},{1,3},{2,0},{3,1},{4,6},{5,7},{6,4},{7,5},{8,10},{9,11},{10,... | collective-permute-start | bytes 786440 | tf_op jit(solution)/shard_map/ppermute | solution.py:536
  205.3 10.8 %collective-permute-start.25 = (f32[128,512]{1,0:T(8,128)S(1)}, f32[128,512]{1,0:T(8,128)}, u32[]{:S(2)}, u32[]{:S(2)}) collective-permute-start(f32[128,512]{1,0:T(8,128)S(1)} %block_sum.3.refs_5_), channel_id=1, source_target_pairs={{0,3},{1,2},{2,1},{3,0},{4,7},{5,6},{6,5},{7,4},{8,11},{9,10},{10,... | collective-permute-start | bytes 786440 | tf_op jit(solution)/shard_map/ppermute | solution.py:536
  (29 other events, 227.7 us)
